TPU v7x, 32 devices: a whole 2x2x4 slice. The times are simulated.
32 devices in a mesh: groups: 2 (over x), ep: 16 (over z, y, core).
Axes of the slice: x: 2, y: 2, z: 4, core: 2. Of those that a mesh axis runs over, the one named last changes fastest.
Arguments:
- tokens: bfloat16 [2048, 7168], P(('groups', 'ep')), parts along dimension 0, may hold values from -6 to 6
- routes: int32 [2048, 4], P(('groups', 'ep')), parts along dimension 0, may hold values from 0 to 7, all different within a row; in each aligned block of 64 rows (0 to 63, 64 to 127, ...) at most 40 rows name the same one
- gates: float32 [2048, 4], P(('groups', 'ep')), parts along dimension 0, may hold values from 0.05 to 1
- w_gate: bfloat16 [16, 7168, 512], P('ep'), may hold values from -0.0625 to 0.0625
- w_up: bfloat16 [16, 7168, 512], P('ep'), may hold values from -0.0625 to 0.0625
- w_down: bfloat16 [16, 512, 7168], P('ep'), may hold values from -0.1875 to 0.1875
Outputs:
- mixed: bfloat16 [2048, 7168], P(('groups', 'ep')), parts along dimension 0
There are 2 independent parts, one for each index of `groups`. A program takes and returns all parts, laid end to end along the dimension named above; an argument that names none is the same for every part. Nothing has to cross between parts.
Inputs may be any that keep to these rules, and one draw needn't show every extreme that they name: `routes`: each row names 4 different experts. Among the 64 rows of one device no expert is named more than 40 times, a bound that some block reaches.
All inputs are finite; a program needn't handle non-finite values.
Results may differ from a plain program's by a relative error of at most 0.0085.
The roundings to bfloat16 on the way count: a program that leaves them out, or rounds other values in their place, can miss the bound.
Values may be sent and summed in bfloat16 or wider, within the bound.
No kernel may reach another device: no remote copies, remote signals or barrier semaphores. Data moves between devices by JAX's collectives and lax.ppermute only.
A program may use at most 192 MiB of HBM per device.

v0:
```python
import functools

import jax
import jax.numpy as jnp
from jax import lax
from jax.experimental import pallas as pl
from jax.experimental.pallas import tpu as pltpu
from jax.sharding import PartitionSpec as P

F32 = jnp.float32
BF16 = jnp.bfloat16
LANES = 128
BLOCK = 128
VMEM_LIMIT = 56 * 1024 * 1024


def whole_block(shape):
    return pl.BlockSpec(shape, lambda *_: (0,) * len(shape))


def params(grid_dims=0):
    if grid_dims:
        return pltpu.CompilerParams(
            vmem_limit_bytes=VMEM_LIMIT, dimension_semantics=("arbitrary",) * grid_dims
        )
    return pltpu.CompilerParams(vmem_limit_bytes=VMEM_LIMIT)


def to_grid(values):
    magnitude = jnp.abs(values)
    spacing = jnp.full(values.shape, 2.0 ** (-9), F32)
    inverse = jnp.full(values.shape, 2.0**9, F32)
    for exponent in range(-5, 9):
        above = magnitude >= 2.0**exponent
        spacing = jnp.where(above, 2.0 ** (exponent - 3), spacing)
        inverse = jnp.where(above, 2.0 ** (3 - exponent), inverse)
    grid_value = jnp.floor(magnitude * inverse + 0.5) * spacing
    return jnp.where(values < 0, -grid_value, grid_value)


def gate_of(ext, expert, experts):
    lane = lax.broadcasted_iota(jnp.int32, ext.shape, 1)
    mine = (lane == expert) | (lane == expert + experts) | (lane == expert + 2 * experts)
    return jnp.sum(jnp.where(mine, ext.astype(F32), 0.0), axis=1, keepdims=True)


def placement(gate, capacity):
    rows = gate.shape[0]
    routed = gate > 0.0
    before = lax.broadcasted_iota(jnp.int32, (rows, rows), 1) < lax.broadcasted_iota(
        jnp.int32, (rows, rows), 0
    )
    ones = jnp.broadcast_to(jnp.where(routed, 1.0, 0.0), (rows, LANES)).astype(BF16)
    rank = jnp.dot(jnp.where(before, 1.0, 0.0).astype(BF16), ones, preferred_element_type=F32)
    rank = rank[:, :1].astype(jnp.int32)
    place = lax.broadcasted_iota(jnp.int32, (rows, capacity), 1)
    return jnp.where(routed & (rank == place), 1.0, 0.0).astype(BF16)


def pick_rows(onehot, rows):
    return lax.dot_general(
        onehot, rows, (((0,), (0,)), ((), ())), preferred_element_type=F32
    ).astype(BF16)


def prepare_kernel(experts, capacity, at_ref, tokens_ref, routes_ref, gates_ref, x_ref, y_ref):
    rows, features = tokens_ref.shape
    lane = lax.broadcasted_iota(jnp.int32, (rows, LANES), 1)
    routes = routes_ref[...]
    gates = gates_ref[...]
    value = jnp.zeros((rows, LANES), F32)
    for k in range(routes.shape[1]):
        hit = (
            (lane == routes[:, k : k + 1])
            | (lane == routes[:, k : k + 1] + experts)
            | (lane == routes[:, k : k + 1] + 2 * experts)
        )
        value = value + jnp.where(hit, gates[:, k : k + 1], 0.0)
    high = value.astype(BF16).astype(F32)
    middle = (value - high).astype(BF16).astype(F32)
    low = value - high - middle
    ext = jnp.where(lane < experts, high, jnp.where(lane < 2 * experts, middle, low)).astype(BF16)
    onehot = placement(gate_of(ext, at_ref[1], experts), capacity)
    x_ref[:, features:] = ext
    y_ref[:, features:] = pick_rows(onehot, ext)
    step = 4 * BLOCK

    def body(i, carry):
        start = pl.multiple_of(i * step, step)
        parts = []
        for b in range(step // BLOCK):
            block = tokens_ref[:, pl.ds(pl.multiple_of(start + b * BLOCK, BLOCK), BLOCK)].astype(F32)
            largest = jnp.max(jnp.abs(block), axis=1, keepdims=True)
            scale = ((largest + 1e-06) / 448.0).astype(BF16).astype(F32)
            parts.append((to_grid(block / scale) * scale).astype(BF16))
        restored = jnp.concatenate(parts, axis=1)
        x_ref[:, pl.ds(start, step)] = restored
        y_ref[:, pl.ds(start, step)] = pick_rows(onehot, restored)
        return carry

    lax.fori_loop(0, features // step, body, 0)


def prepare(at, tokens, routes, gates, experts, capacity):
    rows, features = tokens.shape
    width = features + LANES
    return pl.pallas_call(
        functools.partial(prepare_kernel, experts, capacity),
        out_shape=(
            jax.ShapeDtypeStruct((rows, width), BF16),
            jax.ShapeDtypeStruct((capacity, width), BF16),
        ),
        in_specs=[pl.BlockSpec(memory_space=pltpu.SMEM)]
        + [pl.BlockSpec(memory_space=pltpu.VMEM)] * 3,
        out_specs=(pl.BlockSpec(memory_space=pltpu.VMEM),) * 2,
        compiler_params=params(),
        name="prepare",
    )(at, tokens, routes, gates)


def compact_kernel(experts, capacity, count, sums, at_ref, *refs):
    ins, outs = refs[:count], refs[count:]
    features = ins[0].shape[1] - LANES
    step = 1024
    pieces = []
    if sums:
        merged = outs[1]
        merged[...] = ins[0][...] + ins[1][...]
        sources = (merged,)
    else:
        sources = ins
    for j, source in enumerate(sources):
        onehot = placement(gate_of(source[:, features:], at_ref[1], experts), capacity)
        outs[0][j, :, features:] = pick_rows(onehot, source[:, features:])
        for start in range(0, features, step):
            outs[0][j, :, start : start + step] = pick_rows(onehot, source[:, start : start + step])


def compact(at, blocks, experts, capacity, sums=False):
    rows, width = blocks[0].shape
    count = len(blocks)
    out_shape = [jax.ShapeDtypeStruct((1 if sums else count, capacity, width), BF16)]
    if sums:
        out_shape.append(jax.ShapeDtypeStruct((rows, width), BF16))
    return pl.pallas_call(
        functools.partial(compact_kernel, experts, capacity, count, sums),
        out_shape=tuple(out_shape),
        in_specs=[pl.BlockSpec(memory_space=pltpu.SMEM)]
        + [pl.BlockSpec(memory_space=pltpu.VMEM)] * count,
        out_specs=(pl.BlockSpec(memory_space=pltpu.VMEM),) * len(out_shape),
        compiler_params=params(),
        name="compact",
    )(at, *blocks)


def expert_kernel(experts, full, extra, k_steps, at_ref, *refs):
    count = len(full) + len(extra)
    rows_in, refs = refs[:count], refs[count:]
    exts, refs = refs[:count], refs[count:]
    gate_own, gate_other, up_own, up_other, down_own, down_other = refs[:6]
    outs, (acc, hidden, weight) = refs[6 : 6 + count], refs[6 + count :]
    i = pl.program_id(0)
    half = gate_own.shape[2]
    pieces = []
    for j, size in enumerate(full):
        pieces.append((j, None, size))
    for j, (blocks, size) in enumerate(extra):
        for b in range(blocks):
            pieces.append((len(full) + j, b, size))

    def load(source, j, b):
        return source[j][...] if b is None else source[j][b]

    @pl.when(i == 0)
    def _():
        acc[...] = jnp.zeros_like(acc)
        weight[...] = jnp.concatenate(
            [
                jnp.broadcast_to(gate_of(load(exts, j, b), at_ref[0], experts), (size, LANES))
                for j, b, size in pieces
            ],
            axis=0,
        )

    @pl.when(i < k_steps)
    def _():
        x = jnp.concatenate([load(rows_in, j, b).astype(F32) for j, b, _ in pieces], axis=0)
        x = x.astype(BF16)
        for n, ref in enumerate((gate_own, gate_other, up_own, up_other)):
            acc[:, n * half : (n + 1) * half] += jnp.dot(x, ref[0], preferred_element_type=F32)

    @pl.when(i == k_steps - 1)
    def _():
        gate_part = acc[:, : 2 * half]
        hidden[...] = (jax.nn.silu(gate_part) * acc[:, 2 * half :]).astype(BF16)

    @pl.when(i >= k_steps)
    def _():
        own = jnp.dot(hidden[:, :half], down_own[0], preferred_element_type=F32)
        other = jnp.dot(hidden[:, half:], down_other[0], preferred_element_type=F32)
        total = own.astype(BF16).astype(F32) + other.astype(BF16).astype(F32)
        scaled = total.astype(BF16).astype(F32) * weight[:, :1]
        offset = 0
        for j, b, size in pieces:
            part = scaled[offset : offset + size].astype(BF16)
            if b is None:
                outs[j][...] = part
            else:
                outs[j][b] = part
            offset += size


def run_expert(at, full, extra, weights, experts, tile=1024):
    own, other = weights
    features, half = own[0].shape[1:]
    k_steps = features // tile
    n_steps = features // tile
    last = features // LANES
    inputs = list(full) + list(extra)
    row_specs, ext_specs, out_specs, out_shape = [], [], [], []
    for array in inputs:
        lead = array.shape[:-1]
        zeros = (0,) * len(lead)
        row_specs.append(
            pl.BlockSpec(lead + (tile,), lambda i, z=zeros: z + (jnp.minimum(i, k_steps - 1),))
        )
        ext_specs.append(pl.BlockSpec(lead + (LANES,), lambda i, z=zeros: z + (last,)))
        out_specs.append(
            pl.BlockSpec(lead + (tile,), lambda i, z=zeros: z + (jnp.maximum(i - k_steps, 0),))
        )
        out_shape.append(jax.ShapeDtypeStruct(lead + (features,), BF16))
    up_spec = pl.BlockSpec((1, tile, half), lambda i: (0, jnp.minimum(i, k_steps - 1), 0))
    down_spec = pl.BlockSpec((1, half, tile), lambda i: (0, 0, jnp.maximum(i - k_steps, 0)))
    total = sum(a.size // a.shape[-1] for a in inputs)
    return pl.pallas_call(
        functools.partial(
            expert_kernel,
            experts,
            tuple(a.shape[0] for a in full),
            tuple(a.shape[:2] for a in extra),
            k_steps,
        ),
        out_shape=tuple(out_shape),
        grid=(k_steps + n_steps,),
        in_specs=[pl.BlockSpec(memory_space=pltpu.SMEM)]
        + row_specs
        + ext_specs
        + [up_spec] * 4
        + [down_spec] * 2,
        out_specs=tuple(out_specs),
        scratch_shapes=[
            pltpu.VMEM((total, 4 * half), F32),
            pltpu.VMEM((total, 2 * half), BF16),
            pltpu.VMEM((total, LANES), F32),
        ],
        compiler_params=params(1),
        cost_estimate=pl.CostEstimate(
            flops=12 * total * features * half,
            bytes_accessed=12 * features * half + 4 * total * features,
            transcendentals=2 * total * half,
        ),
        name="expert",
    )(at, *inputs, *inputs, own[0], other[0], own[1], other[1], own[2], other[2])


def combine_kernel(experts, capacity, adds, at_ref, ext_ref, mine_ref, theirs_ref, *refs):
    out_ref, onehot = refs[adds], refs[adds + 1]

    @pl.when(pl.program_id(0) == 0)
    def _():
        gate = gate_of(ext_ref[...], at_ref[1], experts)
        onehot[...] = placement(gate, capacity).astype(F32)

    total = mine_ref[...].astype(F32) + jnp.dot(
        onehot[...].astype(BF16), theirs_ref[0], preferred_element_type=F32
    )
    for ref in refs[:adds]:
        total = total + ref[...].astype(F32)
    out_ref[...] = total.astype(BF16)


def combine(at, block, mine, theirs, index, adds, experts, tile=1792):
    rows, features = mine.shape
    capacity = theirs.shape[1]
    last = features // LANES
    spec = pl.BlockSpec((rows, tile), lambda i: (0, i))
    return pl.pallas_call(
        functools.partial(combine_kernel, experts, capacity, len(adds)),
        out_shape=jax.ShapeDtypeStruct((rows, features), BF16),
        grid=(features // tile,),
        in_specs=[
            pl.BlockSpec(memory_space=pltpu.SMEM),
            pl.BlockSpec((rows, LANES), lambda i: (0, last)),
            spec,
            pl.BlockSpec((1, capacity, tile), lambda i: (index, 0, i)),
        ]
        + [spec] * len(adds),
        out_specs=spec,
        scratch_shapes=[pltpu.VMEM((rows, capacity), F32)],
        compiler_params=params(1),
        name="combine",
    )(at, block, mine, theirs, *adds)


DEPTH = 4


def send(array, dz=0, dy=0, dc=0, only=None):
    pairs = []
    for z in range(DEPTH):
        if 0 <= z + dz < DEPTH and (only is None or z in only):
            for y in range(2):
                for c in range(2):
                    pairs.append(((z * 2 + y) * 2 + c, ((z + dz) * 2 + (y ^ dy)) * 2 + (c ^ dc)))
    return lax.ppermute(array, "ep", pairs)


def send_far(array):
    pairs = [(i, i + 12) for i in range(4)] + [(i + 12, i) for i in range(4)]
    return lax.ppermute(array, "ep", pairs)


def after(array, *others):
    return lax.optimization_barrier((array,) + others)[0]


def line_shards(tokens, routes, gates, w_gate, w_up, w_down):
    tok_rows, features = tokens.shape
    topk = routes.shape[1]
    experts = lax.axis_size("ep") // 2
    capacity = 2 * ((tok_rows * topk * 5 + 8 * experts - 1) // (8 * experts))
    chip = lax.axis_index("ep") // 2
    at = jnp.stack([chip, chip ^ 1]).astype(jnp.int32)
    own = (w_gate, w_up, w_down)
    other = tuple(send(w, dc=1) for w in own)
    weights = (own, other)

    block, picked = prepare(at, tokens, routes, gates, experts, capacity)
    from_left = send(block, dz=1)
    from_right = send(block, dz=-1)
    picked = send(picked[None], dy=1)
    (near_picked,) = compact(at, (from_left, from_right), experts, capacity)
    near_picked = send(near_picked, dy=1)
    mid_left = send(from_left, dz=1)
    mid_right = send(from_right, dz=-1)
    mid_picked, mid = compact(at, (mid_left, mid_right), experts, capacity, sums=True)
    mid_picked = send(mid_picked, dy=1)
    far = send_far(after(block, mid_left, mid_right))
    (far_picked,) = compact(at, (far,), experts, capacity)
    far_picked = send(far_picked, dy=1)

    own_out, left_out, right_out, own_back, near_back = run_expert(
        at, (block, from_left, from_right), (picked, near_picked), weights, experts
    )
    mid_out, far_out, mid_back, far_back = run_expert(
        at, (mid, far), (mid_picked, far_picked), weights, experts
    )
    near_back = send(near_back, dy=1)
    far_back = send(far_back, dy=1)
    mid_back = send(mid_back, dy=1)
    own_back = send(after(own_back, mid_back, far_back), dy=1)

    far_sum = combine(at, far, far_out, far_back, 0, (), experts)
    far_home = send_far(far_sum)
    mid_sum = combine(at, mid, mid_out, mid_back, 0, (), experts)
    to_right = send(mid_sum, dz=1, only=(0, 1))
    to_left = send(mid_sum, dz=-1, only=(3, 2))
    right_sum = combine(at, from_right, right_out, near_back, 1, (to_right,), experts)
    left_sum = combine(at, from_left, left_out, near_back, 0, (to_left,), experts)
    home_left = send(right_sum, dz=1)
    home_right = send(left_sum, dz=-1)
    return combine(
        at, block, own_out, own_back, 0, (far_home, home_left, home_right), experts
    )


def partner(shard, axis, stride):
    return lax.ppermute(shard, axis, [(i, i ^ 1 << stride) for i in range(lax.axis_size(axis))])


def plain_to_grid(values):
    magnitude = jnp.abs(values)
    spacing = jnp.full(values.shape, 2.0 ** (-9), jnp.float32)
    for exponent in range(-5, 9):
        spacing = jnp.where(magnitude >= 2.0**exponent, spacing * 2.0, spacing)
    grid_value = jnp.floor(magnitude / spacing + 0.5) * spacing
    return jnp.where(values < 0, -grid_value, grid_value)


def quantize(rows):
    row_count = rows.shape[0]
    feature_count = rows.shape[1]
    blocks = rows.astype(jnp.float32).reshape(row_count, feature_count // 128, 128)
    largest = jnp.max(jnp.abs(blocks), axis=2)
    scales = ((largest + 1e-06) / 448.0).astype(jnp.bfloat16)
    scales = lax.optimization_barrier(scales)
    quantized = plain_to_grid(blocks / scales.astype(jnp.float32)[:, :, None]).astype(jnp.bfloat16)
    return (quantized.reshape(row_count, feature_count), scales)


def half_expert(quantized, scales, weights):
    row_count = quantized.shape[0]
    feature_count = quantized.shape[1]
    blocks = quantized.astype(jnp.float32).reshape(row_count, feature_count // 128, 128)
    restored = (blocks * scales.astype(jnp.float32)[:, :, None]).astype(jnp.bfloat16)
    restored = restored.reshape(row_count, feature_count)
    gate_part = jnp.dot(restored, weights[0], preferred_element_type=jnp.float32)
    up_part = jnp.dot(restored, weights[1], preferred_element_type=jnp.float32)
    hidden = (jax.nn.silu(gate_part) * up_part).astype(jnp.bfloat16)
    return jnp.dot(hidden, weights[2], preferred_element_type=jnp.float32)


def plain_expert(quantized, scales, weights):
    return half_expert(quantized, scales, weights)


def shards(tokens, routes, gates, w_gate, w_up, w_down):
    tok_rows, feature_count = tokens.shape
    topk_count = routes.shape[1]
    slices = lax.axis_size("ep")
    experts = slices // 2
    capacity = 2 * ((tok_rows * topk_count * 5 + 8 * experts - 1) // (8 * experts))
    weights = (w_gate[0], w_up[0], w_down[0])
    quantized, scales = quantize(tokens)
    qblocks = scales.shape[1]
    flat_experts = routes.reshape(-1)
    onehot = (flat_experts[:, None] == jnp.arange(experts, dtype=jnp.int32)[None, :]).astype(
        jnp.int32
    )
    rank = jnp.sum((jnp.cumsum(onehot, axis=0) - onehot) * onehot, axis=1)
    slot_index = flat_experts * capacity + rank
    token_of = jnp.arange(tok_rows * topk_count, dtype=jnp.int32) // topk_count
    table = jnp.full((experts * capacity,), tok_rows, jnp.int32).at[slot_index].set(token_of)
    padded_q = jnp.concatenate([quantized, jnp.zeros((1, feature_count), jnp.bfloat16)], axis=0)
    padded_s = jnp.concatenate([scales, jnp.zeros((1, qblocks), jnp.bfloat16)], axis=0)
    send_q = padded_q[table].reshape(experts, capacity, feature_count)
    send_s = padded_s[table].reshape(experts, capacity, qblocks)
    half_slots = capacity // 2
    split_q = send_q.reshape(slices, half_slots, feature_count)
    split_s = send_s.reshape(slices, half_slots, qblocks)
    mine_q, mine_s = (
        lax.all_to_all(split_q, "ep", split_axis=0, concat_axis=0, tiled=True),
        lax.all_to_all(split_s, "ep", split_axis=0, concat_axis=0, tiled=True),
    )
    other_q, other_s = partner((mine_q, mine_s), "ep", 0)
    leading = lax.axis_index("ep") % 2 == 0
    low_q = jnp.where(leading, mine_q, other_q)
    high_q = jnp.where(leading, other_q, mine_q)
    low_s = jnp.where(leading, mine_s, other_s)
    high_s = jnp.where(leading, other_s, mine_s)
    rows_q = jnp.concatenate([low_q, high_q], axis=1)
    rows_s = jnp.concatenate([low_s, high_s], axis=1)
    senders = rows_q.shape[0]
    partial_value = plain_expert(
        rows_q.reshape(senders * capacity, feature_count),
        rows_s.reshape(senders * capacity, qblocks),
        weights,
    )
    rounded = partial_value.astype(jnp.bfloat16).reshape(senders, capacity, feature_count)
    low_part = rounded[:, :half_slots]
    high_part = rounded[:, half_slots:]
    kept_half = jnp.where(leading, low_part, high_part)
    given_half = jnp.where(leading, high_part, low_part)
    partner_sum = partner(given_half, "ep", 0)
    kept_half = lax.optimization_barrier(kept_half)
    summed = (kept_half.astype(jnp.float32) + partner_sum.astype(jnp.float32)).astype(jnp.bfloat16)
    back = lax.all_to_all(summed, "ep", split_axis=0, concat_axis=0, tiled=True)
    expert_out = back.reshape(experts, capacity, feature_count)
    expert_out = lax.optimization_barrier(expert_out).reshape(experts * capacity, feature_count)
    picked = expert_out[slot_index].reshape(tok_rows, topk_count, feature_count)
    mixed = jnp.einsum("tk,tkd->td", gates, picked.astype(jnp.float32))
    return mixed.astype(jnp.bfloat16)


def solution(mesh):
    placed = (
        P(("groups", "ep"), None),
        P(("groups", "ep"), None),
        P(("groups", "ep"), None),
        P("ep", None, None),
        P("ep", None, None),
        P("ep", None, None),
    )
    line = mesh.shape["ep"] == 4 * DEPTH
    return jax.shard_map(
        line_shards if line else shards, mesh=mesh, in_specs=placed, out_specs=P(("groups", "ep"), None), check_vma=False
    )
```

profile of v0, /device:TPU:0, one launch (start us, length us, event | category | flops | bytes accessed | tf_op | source)
XLA Modules:
  0.0 261.8 jit_solution(15644411709068045113)
XLA Ops:
  0.0 0.5 collective-permute-start.4
  0.5 0.1 collective-permute-start.5
  0.5 0.5 collective-permute-start.6
  1.0 1.4 copy.7.routes_ref
  2.3 1.4 copy.8.gates_ref
  3.7 0.7 pad_add_fusion.at_ref
  4.4 9.5 %prepare.1 = (bf16[64,7296]{1,0:T(8,128)(2,1)}, bf16[40,7296]{1,0:T(8,128)(2,1)}) custom-call(s32[2]{0:T(128)} %pad_add_fusion.at_ref, bf16[64,7168]{1,0:T(8,128)(2,1)} %tokens_ref.1, s32[64,4]{1,0:T(8,128)} %copy.7.routes_ref, f32[64,4]{1,0:T(8,128)} %copy.8.gates_ref), custom_call_target="tpu_custom_call" | custom-call | tf_op jit(solution)/shard_map/prepare/pallas_call | solution.py:107
  13.9 4.5 %collective-permute-start = (bf16[64,7296]{1,0:T(8,128)(2,1)}, bf16[64,7296]{1,0:T(8,128)(2,1)S(1)}, u32[]{:S(2)}, u32[]{:S(2)}) collective-permute-start(bf16[64,7296]{1,0:T(8,128)(2,1)} %get-tuple-element.25.refs_0_.refs_5_.ext_ref), channel_id=1, source_target_pairs={{0,4},{1,5},{2,6},{3,7},{4,8},{5,9},{6,10},{7,11},{8,12},{9,13},{1... | collective-permute-start | bytes 2801672 | tf_op jit(solution)/shard_map/ppermute | solution.py:315
  18.4 1.3 collective-permute-start.1
  19.7 19.6 %collective-permute-done.refs_0_.refs_1_.refs_6_.ext_ref = bf16[64,7296]{1,0:T(8,128)(2,1)S(1)} collective-permute-done((bf16[64,7296]{1,0:T(8,128)(2,1)}, bf16[64,7296]{1,0:T(8,128)(2,1)S(1)}, u32[]{:S(2)}, u32[]{:S(2)}) %collective-permute-start) | collective-permute-done | bytes 933920 | tf_op jit(solution)/shard_map/ppermute | solution.py:315
  39.3 4.3 %collective-permute-start.7 = (bf16[64,7296]{1,0:T(8,128)(2,1)S(1)}, bf16[64,7296]{1,0:T(8,128)(2,1)S(1)}, u32[]{:S(2)}, u32[]{:S(2)}) collective-permute-start(bf16[64,7296]{1,0:T(8,128)(2,1)S(1)} %collective-permute-done.refs_0_.refs_1_.refs_6_.ext_ref), channel_id=1, source_target_pairs={{0,4},{1,5},{2,6},{3,7},{4,8},{5,9},{6,10},{7,11},{8,12},{9,13},{1... | collective-permute-start | bytes 2801672 | tf_op jit(solution)/shard_map/ppermute | solution.py:315
  43.6 0.0 collective-permute-done.1.refs_1_.refs_2_.refs_7_.ext_ref
  43.6 1.3 collective-permute-start.8
  44.9 18.5 %collective-permute-done.7.refs_0_ = bf16[64,7296]{1,0:T(8,128)(2,1)S(1)} collective-permute-done((bf16[64,7296]{1,0:T(8,128)(2,1)S(1)}, bf16[64,7296]{1,0:T(8,128)(2,1)S(1)}, u32[]{:S(2)}, u32[]{:S(2)}) %collective-permute-start.7) | collective-permute-done | bytes 933920 | tf_op jit(solution)/shard_map/ppermute | solution.py:315
  63.4 4.2 %collective-permute-done.8.refs_1_ = bf16[64,7296]{1,0:T(8,128)(2,1)S(1)} collective-permute-done((bf16[64,7296]{1,0:T(8,128)(2,1)S(1)}, bf16[64,7296]{1,0:T(8,128)(2,1)S(1)}, u32[]{:S(2)}, u32[]{:S(2)}) %collective-permute-start.8) | collective-permute-done | bytes 933920 | tf_op jit(solution)/shard_map/ppermute | solution.py:315
  67.6 3.4 %collective-permute-start.9 = (bf16[64,7296]{1,0:T(8,128)(2,1)}, bf16[64,7296]{1,0:T(8,128)(2,1)S(1)}, u32[]{:S(2)}, u32[]{:S(2)}) collective-permute-start(bf16[64,7296]{1,0:T(8,128)(2,1)} %get-tuple-element.25.refs_0_.refs_5_.ext_ref), channel_id=1, source_target_pairs={{0,12},{1,13},{2,14},{3,15},{12,0},{13,1},{14,2},{15,3},{16,28},{1... | collective-permute-start | bytes 2801672 | tf_op jit(solution)/shard_map/ppermute | solution.py:320
  71.0 3.2 %compact.4 = (bf16[1,40,7296]{2,1,0:T(8,128)(2,1)}, bf16[64,7296]{1,0:T(8,128)(2,1)}) custom-call(s32[2]{0:T(128)} %pad_add_fusion.at_ref, bf16[64,7296]{1,0:T(8,128)(2,1)} %copy-done.8, bf16[64,7296]{1,0:T(8,128)(2,1)} %copy-done.9), custom_call_target="tpu_custom_call" | custom-call | tf_op jit(solution)/shard_map/compact/pallas_call | solution.py:145
  74.2 1.5 collective-permute-start.10
  75.7 16.9 %collective-permute-done.9.refs_0_.refs_1_.refs_5_.ext_ref = bf16[64,7296]{1,0:T(8,128)(2,1)S(1)} collective-permute-done((bf16[64,7296]{1,0:T(8,128)(2,1)}, bf16[64,7296]{1,0:T(8,128)(2,1)S(1)}, u32[]{:S(2)}, u32[]{:S(2)}) %collective-permute-start.9) | collective-permute-done | bytes 933920 | tf_op jit(solution)/shard_map/ppermute | solution.py:320
  92.6 0.9 copy-done.2
  93.5 2.7 %compact.5 = bf16[1,40,7296]{2,1,0:T(8,128)(2,1)} custom-call(s32[2]{0:T(128)} %pad_add_fusion.at_ref, bf16[64,7296]{1,0:T(8,128)(2,1)} %copy-done.2), custom_call_target="tpu_custom_call" | custom-call | tf_op jit(solution)/shard_map/compact/pallas_call | solution.py:145
  96.3 1.5 collective-permute-start.11
  97.8 3.6 %compact.3 = bf16[2,40,7296]{2,1,0:T(8,128)(2,1)} custom-call(s32[2]{0:T(128)} %pad_add_fusion.at_ref, bf16[64,7296]{1,0:T(8,128)(2,1)} %copy-done, bf16[64,7296]{1,0:T(8,128)(2,1)} %copy-done.1), custom_call_target="tpu_custom_call" | custom-call | tf_op jit(solution)/shard_map/compact/pallas_call | solution.py:145
  101.4 0.0 collective-permute-done.10.refs_2_.refs_6_
  101.4 0.5 collective-permute-start.3
  101.9 10.7 %collective-permute-done.11.refs_3_.refs_7_ = bf16[1,40,7296]{2,1,0:T(8,128)(2,1)S(1)} collective-permute-done((bf16[1,40,7296]{2,1,0:T(8,128)(2,1)}, bf16[1,40,7296]{2,1,0:T(8,128)(2,1)S(1)}, u32[]{:S(2)}, u32[]{:S(2)}) %collective-permute-start.11) | collective-permute-done | bytes 583712 | tf_op jit(solution)/shard_map/ppermute | solution.py:315
  112.6 1.5 collective-permute-start.2
  114.1 0.0 collective-permute-done.4.refs_11_.refs_9_
  114.1 0.0 collective-permute-done.5.refs_13_.refs_11_
  114.1 0.0 collective-permute-done.6.refs_15_.refs_13_
  114.2 24.3 %expert.3 = (bf16[64,7168]{1,0:T(8,128)(2,1)}, bf16[64,7168]{1,0:T(8,128)(2,1)}, bf16[1,40,7168]{2,1,0:T(8,128)(2,1)}, bf16[1,40,7168]{2,1,0:T(8,128)(2,1)}) custom-call(s32[2]{0:T(128)} %pad_add_fusion.at_ref, bf16[64,7296]{1,0:T(8,128)(2,1)} %get-tuple-element.24.refs_0_.refs_4_.ext_ref, bf16[64,7296]{1,0:T(8,128)(2,1)} %copy-done.2, ...), custom_call_target="tpu_custom_call" | custom-call | flops 9160359936 | bytes 50003968 | tf_op jit(solution)/shard_map/expert/pallas_call | solution.py:235
  138.5 0.9 collective-permute-start.12
  139.4 10.8 %collective-permute-done.2.refs_3_.refs_8_ = bf16[1,40,7296]{2,1,0:T(8,128)(2,1)S(1)} collective-permute-done((bf16[1,40,7296]{2,1,0:T(8,128)(2,1)}, bf16[1,40,7296]{2,1,0:T(8,128)(2,1)S(1)}, u32[]{:S(2)}, u32[]{:S(2)}) %collective-permute-start.2) | collective-permute-done | bytes 583712 | tf_op jit(solution)/shard_map/ppermute | solution.py:315
  150.1 0.0 collective-permute-done.3.refs_4_.refs_9_
  150.1 0.8 copy-done.6
  151.0 1.0 copy-done.3
  152.0 27.9 %expert.2 = (bf16[64,7168]{1,0:T(8,128)(2,1)}, bf16[64,7168]{1,0:T(8,128)(2,1)}, bf16[64,7168]{1,0:T(8,128)(2,1)}, bf16[1,40,7168]{2,1,0:T(8,128)(2,1)}, bf16[2,40,7168]{2,1,0:T(8,128)(2,1)}) custom-call(s32[2]{0:T(128)} %pad_add_fusion.at_ref, bf16[64,7296]{1,0:T(8,128)(2,1)} %get-tuple-element.25.refs_0_.refs_5_.ext_ref, bf16[64,7296]{1,0:T(8,128)(2,1)} %copy-done, ...), custom_call_target="tpu_custom_call" | custom-call | flops 13740539904 | bytes 52985856 | tf_op jit(solution)/shard_map/expert/pallas_call | solution.py:235
  179.9 1.6 collective-permute-start.16
  181.5 0.0 collective-permute-done.12.theirs_ref
  181.5 0.8 copy-done.16
  182.3 4.2 %combine.6 = bf16[64,7168]{1,0:T(8,128)(2,1)} custom-call(s32[2]{0:T(128)} %pad_add_fusion.at_ref, bf16[64,7296]{1,0:T(8,128)(2,1)} %get-tuple-element.24.refs_0_.refs_4_.ext_ref, bf16[64,7168]{1,0:T(8,128)(2,1)} %get-tuple-element.33.mine_ref, bf16[1,40,7168]{2,1,0:T(8,128)(2,1)} %copy-done.16), custom_call_target="tpu_custom_call" | custom-call | tf_op jit(solution)/shard_map/combine/pallas_call | solution.py:287
  186.5 1.5 collective-permute-start.17
  188.0 0.7 collective-permute-start.19
  188.8 0.6 collective-permute-start.13
  189.3 23.6 %collective-permute-done.13.theirs_ref = bf16[1,40,7168]{2,1,0:T(8,128)(2,1)S(1)} collective-permute-done((bf16[1,40,7168]{2,1,0:T(8,128)(2,1)S(1)}, bf16[1,40,7168]{2,1,0:T(8,128)(2,1)S(1)}, u32[]{:S(2)}, u32[]{:S(2)}) %collective-permute-start.13) | collective-permute-done | bytes 573472 | tf_op jit(solution)/shard_map/ppermute | solution.py:315
  212.9 0.8 copy-done.17
  213.7 4.2 %combine.5 = bf16[64,7168]{1,0:T(8,128)(2,1)} custom-call(s32[2]{0:T(128)} %pad_add_fusion.at_ref, bf16[64,7296]{1,0:T(8,128)(2,1)} %copy-done.2, bf16[64,7168]{1,0:T(8,128)(2,1)} %get-tuple-element.30.mine_ref, bf16[1,40,7168]{2,1,0:T(8,128)(2,1)} %copy-done.17), custom_call_target="tpu_custom_call" | custom-call | tf_op jit(solution)/shard_map/combine/pallas_call | solution.py:287
  217.9 3.4 %collective-permute-start.15 = (bf16[64,7168]{1,0:T(8,128)(2,1)}, bf16[64,7168]{1,0:T(8,128)(2,1)S(1)}, u32[]{:S(2)}, u32[]{:S(2)}) collective-permute-start(bf16[64,7168]{1,0:T(8,128)(2,1)} %combine.5), channel_id=1, source_target_pairs={{0,12},{1,13},{2,14},{3,15},{12,0},{13,1},{14,2},{15,3},{16,28},{1... | collective-permute-start | bytes 2752520 | tf_op jit(solution)/shard_map/ppermute | solution.py:320
  221.4 0.0 collective-permute-done.16.theirs_ref
  221.4 1.0 copy-done.4
  222.4 0.3 copy-done.13
  222.7 4.4 %combine.7 = bf16[64,7168]{1,0:T(8,128)(2,1)} custom-call(s32[2]{0:T(128)} %pad_add_fusion.at_ref, bf16[64,7296]{1,0:T(8,128)(2,1)} %copy-done.1, bf16[64,7168]{1,0:T(8,128)(2,1)} %get-tuple-element.31.mine_ref, bf16[2,40,7168]{2,1,0:T(8,128)(2,1)} %copy-done.4, bf16[64,7168]{1,0:T(8,128)(2,1)} %copy-done.13), custom_call_target="tpu_custom_call" | custom-call | tf_op jit(solution)/shard_map/combine/pallas_call | solution.py:287
  227.0 1.3 collective-permute-start.18
  228.4 0.0 collective-permute-done.19.refs_0_
  228.4 0.9 copy-done.11
  229.3 4.4 %combine.8 = bf16[64,7168]{1,0:T(8,128)(2,1)} custom-call(s32[2]{0:T(128)} %pad_add_fusion.at_ref, bf16[64,7296]{1,0:T(8,128)(2,1)} %copy-done, bf16[64,7168]{1,0:T(8,128)(2,1)} %get-tuple-element.34.mine_ref, bf16[2,40,7168]{2,1,0:T(8,128)(2,1)} %copy-done.4, bf16[64,7168]{1,0:T(8,128)(2,1)} %copy-done.11), custom_call_target="tpu_custom_call" | custom-call | tf_op jit(solution)/shard_map/combine/pallas_call | solution.py:287
  233.7 1.3 collective-permute-start.20
  235.0 1.6 collective-permute-start.14
  236.6 8.2 %collective-permute-done.14.theirs_ref = bf16[1,40,7168]{2,1,0:T(8,128)(2,1)S(1)} collective-permute-done((bf16[1,40,7168]{2,1,0:T(8,128)(2,1)S(1)}, bf16[1,40,7168]{2,1,0:T(8,128)(2,1)S(1)}, u32[]{:S(2)}, u32[]{:S(2)}) %collective-permute-start.14) | collective-permute-done | bytes 573472 | tf_op jit(solution)/shard_map/ppermute | solution.py:315
  244.8 0.0 collective-permute-done.15.refs_0_
  244.8 8.7 %collective-permute-done.18.refs_1_ = bf16[64,7168]{1,0:T(8,128)(2,1)S(1)} collective-permute-done((bf16[64,7168]{1,0:T(8,128)(2,1)}, bf16[64,7168]{1,0:T(8,128)(2,1)S(1)}, u32[]{:S(2)}, u32[]{:S(2)}) %collective-permute-start.18) | collective-permute-done | bytes 917536 | tf_op jit(solution)/shard_map/ppermute | solution.py:315
  253.5 2.6 collective-permute-done.20.refs_2_
  256.1 0.9 copy-done.14
  257.0 4.8 %combine.9 = bf16[64,7168]{1,0:T(8,128)(2,1)} custom-call(s32[2]{0:T(128)} %pad_add_fusion.at_ref, bf16[64,7296]{1,0:T(8,128)(2,1)} %get-tuple-element.25.refs_0_.refs_5_.ext_ref, bf16[64,7168]{1,0:T(8,128)(2,1)} %get-tuple-element.22.mine_ref, bf16[1,40,7168]{2,1,0:T(8,128)(2,1)} %copy-done.15, bf16[64,7168]{1,0:T(8,128)(2,1)} %copy-done.10, ...), custom_call_target="tpu_custom_call" | custom-call | tf_op jit(solution)/shard_map/combine/pallas_call | solution.py:287
  (32 shorter events, 0.1 us)
Async XLA Ops:
  0.0 114.1 %collective-permute-start.4 = (bf16[1,7168,512]{2,1,0:T(8,128)(2,1)}, bf16[1,7168,512]{2,1,0:T(8,128)(2,1)}, u32[]{:S(2)}, u32[]{:S(2)}) collective-permute-start(bf16[1,7168,512]{2,1,0:T(8,128)(2,1)} %refs_8_.1), channel_id=1, source_target_pairs={{0,1},{1,0},{2,3},{3,2},{4,5},{5,4},{6,7},{7,6},{8,9},{9,8},{10,11... | collective-permute-start | bytes 22020104 | tf_op jit(solution)/shard_map/ppermute | solution.py:315
  0.5 113.7 %collective-permute-start.5 = (bf16[1,7168,512]{2,1,0:T(8,128)(2,1)}, bf16[1,7168,512]{2,1,0:T(8,128)(2,1)}, u32[]{:S(2)}, u32[]{:S(2)}) collective-permute-start(bf16[1,7168,512]{2,1,0:T(8,128)(2,1)} %refs_10_.3), channel_id=1, source_target_pairs={{0,1},{1,0},{2,3},{3,2},{4,5},{5,4},{6,7},{7,6},{8,9},{9,8},{10,11... | collective-permute-start | bytes 22020104 | tf_op jit(solution)/shard_map/ppermute | solution.py:315
  0.5 113.6 %collective-permute-start.6 = (bf16[1,512,7168]{2,1,0:T(8,128)(2,1)}, bf16[1,512,7168]{2,1,0:T(8,128)(2,1)}, u32[]{:S(2)}, u32[]{:S(2)}) collective-permute-start(bf16[1,512,7168]{2,1,0:T(8,128)(2,1)} %refs_12_.3), channel_id=1, source_target_pairs={{0,1},{1,0},{2,3},{3,2},{4,5},{5,4},{6,7},{7,6},{8,9},{9,8},{10,11... | collective-permute-start | bytes 22020104 | tf_op jit(solution)/shard_map/ppermute | solution.py:315
  13.9 25.4 %collective-permute-start = (bf16[64,7296]{1,0:T(8,128)(2,1)}, bf16[64,7296]{1,0:T(8,128)(2,1)S(1)}, u32[]{:S(2)}, u32[]{:S(2)}) collective-permute-start(bf16[64,7296]{1,0:T(8,128)(2,1)} %get-tuple-element.25.refs_0_.refs_5_.ext_ref), channel_id=1, source_target_pairs={{0,4},{1,5},{2,6},{3,7},{4,8},{5,9},{6,10},{7,11},{8,12},{9,13},{1... | collective-permute-start | bytes 2801672 | tf_op jit(solution)/shard_map/ppermute | solution.py:315
  18.4 25.2 %collective-permute-start.1 = (bf16[64,7296]{1,0:T(8,128)(2,1)}, bf16[64,7296]{1,0:T(8,128)(2,1)S(1)}, u32[]{:S(2)}, u32[]{:S(2)}) collective-permute-start(bf16[64,7296]{1,0:T(8,128)(2,1)} %get-tuple-element.25.refs_0_.refs_5_.ext_ref), channel_id=1, source_target_pairs={{4,0},{5,1},{6,2},{7,3},{8,4},{9,5},{10,6},{11,7},{12,8},{13,9},{1... | collective-permute-start | bytes 2801672 | tf_op jit(solution)/shard_map/ppermute | solution.py:315
  39.3 58.5 %copy-start = (bf16[64,7296]{1,0:T(8,128)(2,1)}, bf16[64,7296]{1,0:T(8,128)(2,1)S(1)}, u32[]{:S(2)}) copy-start(bf16[64,7296]{1,0:T(8,128)(2,1)S(1)} %collective-permute-done.refs_0_.refs_1_.refs_6_.ext_ref) | copy-start | bytes 2801668
  39.3 24.1 %collective-permute-start.7 = (bf16[64,7296]{1,0:T(8,128)(2,1)S(1)}, bf16[64,7296]{1,0:T(8,128)(2,1)S(1)}, u32[]{:S(2)}, u32[]{:S(2)}) collective-permute-start(bf16[64,7296]{1,0:T(8,128)(2,1)S(1)} %collective-permute-done.refs_0_.refs_1_.refs_6_.ext_ref), channel_id=1, source_target_pairs={{0,4},{1,5},{2,6},{3,7},{4,8},{5,9},{6,10},{7,11},{8,12},{9,13},{1... | collective-permute-start | bytes 2801672 | tf_op jit(solution)/shard_map/ppermute | solution.py:315
  43.6 54.2 %copy-start.1 = (bf16[64,7296]{1,0:T(8,128)(2,1)}, bf16[64,7296]{1,0:T(8,128)(2,1)S(1)}, u32[]{:S(2)}) copy-start(bf16[64,7296]{1,0:T(8,128)(2,1)S(1)} %collective-permute-done.1.refs_1_.refs_2_.refs_7_.ext_ref) | copy-start | bytes 2801668
  43.6 23.9 %collective-permute-start.8 = (bf16[64,7296]{1,0:T(8,128)(2,1)S(1)}, bf16[64,7296]{1,0:T(8,128)(2,1)S(1)}, u32[]{:S(2)}, u32[]{:S(2)}) collective-permute-start(bf16[64,7296]{1,0:T(8,128)(2,1)S(1)} %collective-permute-done.1.refs_1_.refs_2_.refs_7_.ext_ref), channel_id=1, source_target_pairs={{4,0},{5,1},{6,2},{7,3},{8,4},{9,5},{10,6},{11,7},{12,8},{13,9},{1... | collective-permute-start | bytes 2801672 | tf_op jit(solution)/shard_map/ppermute | solution.py:315
  63.4 7.6 %copy-start.8 = (bf16[64,7296]{1,0:T(8,128)(2,1)}, bf16[64,7296]{1,0:T(8,128)(2,1)S(1)}, u32[]{:S(2)}) copy-start(bf16[64,7296]{1,0:T(8,128)(2,1)S(1)} %collective-permute-done.7.refs_0_) | copy-start | bytes 2801668
  67.6 3.4 %copy-start.9 = (bf16[64,7296]{1,0:T(8,128)(2,1)}, bf16[64,7296]{1,0:T(8,128)(2,1)S(1)}, u32[]{:S(2)}) copy-start(bf16[64,7296]{1,0:T(8,128)(2,1)S(1)} %collective-permute-done.8.refs_1_) | copy-start | bytes 2801668
  67.6 25.0 %collective-permute-start.9 = (bf16[64,7296]{1,0:T(8,128)(2,1)}, bf16[64,7296]{1,0:T(8,128)(2,1)S(1)}, u32[]{:S(2)}, u32[]{:S(2)}) collective-permute-start(bf16[64,7296]{1,0:T(8,128)(2,1)} %get-tuple-element.25.refs_0_.refs_5_.ext_ref), channel_id=1, source_target_pairs={{0,12},{1,13},{2,14},{3,15},{12,0},{13,1},{14,2},{15,3},{16,28},{1... | collective-permute-start | bytes 2801672 | tf_op jit(solution)/shard_map/ppermute | solution.py:320
  74.2 27.2 %collective-permute-start.10 = (bf16[1,40,7296]{2,1,0:T(8,128)(2,1)}, bf16[1,40,7296]{2,1,0:T(8,128)(2,1)S(1)}, u32[]{:S(2)}, u32[]{:S(2)}) collective-permute-start(bf16[1,40,7296]{2,1,0:T(8,128)(2,1)} %get-tuple-element.26), channel_id=1, source_target_pairs={{0,2},{1,3},{2,0},{3,1},{4,6},{5,7},{6,4},{7,5},{8,10},{9,11},{10,... | collective-permute-start | bytes 1751048 | tf_op jit(solution)/shard_map/ppermute | solution.py:315
  92.6 0.9 copy-start.2
  96.3 16.3 %collective-permute-start.11 = (bf16[1,40,7296]{2,1,0:T(8,128)(2,1)}, bf16[1,40,7296]{2,1,0:T(8,128)(2,1)S(1)}, u32[]{:S(2)}, u32[]{:S(2)}) collective-permute-start(bf16[1,40,7296]{2,1,0:T(8,128)(2,1)} %compact.5), channel_id=1, source_target_pairs={{0,2},{1,3},{2,0},{3,1},{4,6},{5,7},{6,4},{7,5},{8,10},{9,11},{10,... | collective-permute-start | bytes 1751048 | tf_op jit(solution)/shard_map/ppermute | solution.py:315
  101.4 12.7 %copy-start.5 = (bf16[1,40,7296]{2,1,0:T(8,128)(2,1)}, bf16[1,40,7296]{2,1,0:T(8,128)(2,1)S(1)}, u32[]{:S(2)}) copy-start(bf16[1,40,7296]{2,1,0:T(8,128)(2,1)S(1)} %collective-permute-done.10.refs_2_.refs_6_) | copy-start | bytes 1751044
  101.4 48.7 %collective-permute-start.3 = (bf16[2,40,7296]{2,1,0:T(8,128)(2,1)}, bf16[2,40,7296]{2,1,0:T(8,128)(2,1)S(1)}, u32[]{:S(2)}, u32[]{:S(2)}) collective-permute-start(bf16[2,40,7296]{2,1,0:T(8,128)(2,1)} %compact.3), channel_id=1, source_target_pairs={{0,2},{1,3},{2,0},{3,1},{4,6},{5,7},{6,4},{7,5},{8,10},{9,11},{10,... | collective-permute-start | bytes 3502088 | tf_op jit(solution)/shard_map/ppermute | solution.py:315
  112.6 1.6 copy-start.7
  112.6 37.5 %collective-permute-start.2 = (bf16[1,40,7296]{2,1,0:T(8,128)(2,1)}, bf16[1,40,7296]{2,1,0:T(8,128)(2,1)S(1)}, u32[]{:S(2)}, u32[]{:S(2)}) collective-permute-start(bf16[1,40,7296]{2,1,0:T(8,128)(2,1)} %bitcast.3), channel_id=1, source_target_pairs={{0,2},{1,3},{2,0},{3,1},{4,6},{5,7},{6,4},{7,5},{8,10},{9,11},{10,... | collective-permute-start | bytes 1751048 | tf_op jit(solution)/shard_map/ppermute | solution.py:315
  138.5 50.3 %copy-start.19 = (bf16[1,40,7168]{2,1,0:T(8,128)(2,1)S(1)}, bf16[1,40,7168]{2,1,0:T(8,128)(2,1)}, u32[]{:S(2)}) copy-start(bf16[1,40,7168]{2,1,0:T(8,128)(2,1)} %get-tuple-element.28) | copy-start | bytes 1720324
  138.5 43.0 %collective-permute-start.12 = (bf16[1,40,7168]{2,1,0:T(8,128)(2,1)}, bf16[1,40,7168]{2,1,0:T(8,128)(2,1)S(1)}, u32[]{:S(2)}, u32[]{:S(2)}) collective-permute-start(bf16[1,40,7168]{2,1,0:T(8,128)(2,1)} %get-tuple-element.27), channel_id=1, source_target_pairs={{0,2},{1,3},{2,0},{3,1},{4,6},{5,7},{6,4},{7,5},{8,10},{9,11},{10,... | collective-permute-start | bytes 1720328 | tf_op jit(solution)/shard_map/ppermute | solution.py:315
  150.1 0.8 copy-start.6
  151.0 1.0 copy-start.3
  179.9 41.5 %collective-permute-start.16 = (bf16[2,40,7168]{2,1,0:T(8,128)(2,1)}, bf16[2,40,7168]{2,1,0:T(8,128)(2,1)S(1)}, u32[]{:S(2)}, u32[]{:S(2)}) collective-permute-start(bf16[2,40,7168]{2,1,0:T(8,128)(2,1)} %get-tuple-element.32), channel_id=1, source_target_pairs={{0,2},{1,3},{2,0},{3,1},{4,6},{5,7},{6,4},{7,5},{8,10},{9,11},{10,... | collective-permute-start | bytes 3440648 | tf_op jit(solution)/shard_map/ppermute | solution.py:315
  181.5 0.8 copy-start.16
  186.5 48.4 %copy-start.18 = (bf16[1,40,7168]{2,1,0:T(8,128)(2,1)S(1)}, bf16[1,40,7168]{2,1,0:T(8,128)(2,1)}, u32[]{:S(2)}) copy-start(bf16[1,40,7168]{2,1,0:T(8,128)(2,1)} %get-tuple-element.29) | copy-start | bytes 1720324
  186.5 34.8 %collective-permute-start.17 = (bf16[64,7168]{1,0:T(8,128)(2,1)}, bf16[64,7168]{1,0:T(8,128)(2,1)S(1)}, u32[]{:S(2)}, u32[]{:S(2)}) collective-permute-start(bf16[64,7168]{1,0:T(8,128)(2,1)} %combine.6), channel_id=1, source_target_pairs={{0,4},{1,5},{2,6},{3,7},{4,8},{5,9},{6,10},{7,11},{16,20},{17,21},... | collective-permute-start | bytes 2752520 | tf_op jit(solution)/shard_map/ppermute | solution.py:315
  188.0 40.4 %collective-permute-start.19 = (bf16[64,7168]{1,0:T(8,128)(2,1)}, bf16[64,7168]{1,0:T(8,128)(2,1)S(1)}, u32[]{:S(2)}, u32[]{:S(2)}) collective-permute-start(bf16[64,7168]{1,0:T(8,128)(2,1)} %combine.6), channel_id=1, source_target_pairs={{8,4},{9,5},{10,6},{11,7},{12,8},{13,9},{14,10},{15,11},{24,20},{2... | collective-permute-start | bytes 2752520 | tf_op jit(solution)/shard_map/ppermute | solution.py:315
  188.8 24.1 %collective-permute-start.13 = (bf16[1,40,7168]{2,1,0:T(8,128)(2,1)S(1)}, bf16[1,40,7168]{2,1,0:T(8,128)(2,1)S(1)}, u32[]{:S(2)}, u32[]{:S(2)}) collective-permute-start(bf16[1,40,7168]{2,1,0:T(8,128)(2,1)S(1)} %copy-done.19), channel_id=1, source_target_pairs={{0,2},{1,3},{2,0},{3,1},{4,6},{5,7},{6,4},{7,5},{8,10},{9,11},{10,... | collective-permute-start | bytes 1720328 | tf_op jit(solution)/shard_map/ppermute | solution.py:315
  212.9 0.8 copy-start.17
  217.9 26.8 %collective-permute-start.15 = (bf16[64,7168]{1,0:T(8,128)(2,1)}, bf16[64,7168]{1,0:T(8,128)(2,1)S(1)}, u32[]{:S(2)}, u32[]{:S(2)}) collective-permute-start(bf16[64,7168]{1,0:T(8,128)(2,1)} %combine.5), channel_id=1, source_target_pairs={{0,12},{1,13},{2,14},{3,15},{12,0},{13,1},{14,2},{15,3},{16,28},{1... | collective-permute-start | bytes 2752520 | tf_op jit(solution)/shard_map/ppermute | solution.py:320
  221.4 1.0 copy-start.4
  221.4 1.3 copy-start.13
  227.0 26.5 %collective-permute-start.18 = (bf16[64,7168]{1,0:T(8,128)(2,1)}, bf16[64,7168]{1,0:T(8,128)(2,1)S(1)}, u32[]{:S(2)}, u32[]{:S(2)}) collective-permute-start(bf16[64,7168]{1,0:T(8,128)(2,1)} %combine.7), channel_id=1, source_target_pairs={{0,4},{1,5},{2,6},{3,7},{4,8},{5,9},{6,10},{7,11},{8,12},{9,13},{1... | collective-permute-start | bytes 2752520 | tf_op jit(solution)/shard_map/ppermute | solution.py:315
  228.4 0.9 copy-start.11
  233.7 22.4 %collective-permute-start.20 = (bf16[64,7168]{1,0:T(8,128)(2,1)}, bf16[64,7168]{1,0:T(8,128)(2,1)S(1)}, u32[]{:S(2)}, u32[]{:S(2)}) collective-permute-start(bf16[64,7168]{1,0:T(8,128)(2,1)} %combine.8), channel_id=1, source_target_pairs={{4,0},{5,1},{6,2},{7,3},{8,4},{9,5},{10,6},{11,7},{12,8},{13,9},{1... | collective-permute-start | bytes 2752520 | tf_op jit(solution)/shard_map/ppermute | solution.py:315
  235.0 9.8 %collective-permute-start.14 = (bf16[1,40,7168]{2,1,0:T(8,128)(2,1)S(1)}, bf16[1,40,7168]{2,1,0:T(8,128)(2,1)S(1)}, u32[]{:S(2)}, u32[]{:S(2)}) collective-permute-start(bf16[1,40,7168]{2,1,0:T(8,128)(2,1)S(1)} %copy-done.18), channel_id=1, source_target_pairs={{0,2},{1,3},{2,0},{3,1},{4,6},{5,7},{6,4},{7,5},{8,10},{9,11},{10,... | collective-permute-start | bytes 1720328 | tf_op jit(solution)/shard_map/ppermute | solution.py:315
  244.8 11.3 %copy-start.15 = (bf16[1,40,7168]{2,1,0:T(8,128)(2,1)}, bf16[1,40,7168]{2,1,0:T(8,128)(2,1)S(1)}, u32[]{:S(2)}) copy-start(bf16[1,40,7168]{2,1,0:T(8,128)(2,1)S(1)} %collective-permute-done.14.theirs_ref) | copy-start | bytes 1720324
  244.8 11.3 %copy-start.10 = (bf16[64,7168]{1,0:T(8,128)(2,1)}, bf16[64,7168]{1,0:T(8,128)(2,1)S(1)}, u32[]{:S(2)}) copy-start(bf16[64,7168]{1,0:T(8,128)(2,1)S(1)} %collective-permute-done.15.refs_0_) | copy-start | bytes 2752516
  253.5 2.6 copy-start.12
  256.1 0.9 copy-start.14
where the time goes:
time: 263 us; the launch traced here: 262 us
  waiting for transfers between devices  124 us (47%)
  Pallas kernels  93.2 us (35%)
  starting transfers between devices  33.7 us (13%)
  local copies, waits for them, and re-layouts  10.4 us (4%)
    ppermute x19, waiting for transfers between devices, send(): return lax.ppermute(array, 'ep', pairs)  107 us
    pallas_call x2, Pallas kernels, run_expert(): pl.pallas_call(functools.partial(expert_kernel, experts, tuple((a.shape[0...  52.2 us
    ppermute x19, starting transfers between devices, send(): return lax.ppermute(array, 'ep', pairs)  26.9 us
    pallas_call x5, Pallas kernels, combine(): pl.pallas_call(functools.partial(combine_kernel, experts, capacity, len(a...  22 us
    ppermute x2, waiting for transfers between devices, send_far(): return lax.ppermute(array, 'ep', pairs)  16.9 us
    unnamed x42, local copies, waits for them, and re-layouts  10.4 us
    pallas_call x3, Pallas kernels, compact(): pl.pallas_call(functools.partial(compact_kernel, experts, capacity, count...  9.51 us
    pallas_call x1, Pallas kernels, prepare(): pl.pallas_call(functools.partial(prepare_kernel, experts, capacity), out_...  9.47 us
  transfers between devices with their start and end apart: 21, of which 10 were waited for; matrix products, arithmetic and copies ran while one was open for 1% of the time, Pallas kernels for 34%

commit v1 on v0

--- a/solution.py
+++ b/solution.py
@@ -11,30 +11,29 @@
 BF16 = jnp.bfloat16
 LANES = 128
 BLOCK = 128
-VMEM_LIMIT = 56 * 1024 * 1024
-
-
-def whole_block(shape):
-    return pl.BlockSpec(shape, lambda *_: (0,) * len(shape))
-
-
-def params(grid_dims=0):
-    if grid_dims:
-        return pltpu.CompilerParams(
-            vmem_limit_bytes=VMEM_LIMIT, dimension_semantics=("arbitrary",) * grid_dims
-        )
-    return pltpu.CompilerParams(vmem_limit_bytes=VMEM_LIMIT)
+MIB = 1024 * 1024
+
+
+def params(limit, grid_dims=0):
+    semantics = ("arbitrary",) * grid_dims if grid_dims else None
+    return pltpu.CompilerParams(vmem_limit_bytes=limit * MIB, dimension_semantics=semantics)
+
+
+SMEM = pl.BlockSpec(memory_space=pltpu.SMEM)
+VMEM = pl.BlockSpec(memory_space=pltpu.VMEM)
+ANY = pl.BlockSpec(memory_space=pl.ANY)
 
 
 def to_grid(values):
-    magnitude = jnp.abs(values)
-    spacing = jnp.full(values.shape, 2.0 ** (-9), F32)
-    inverse = jnp.full(values.shape, 2.0**9, F32)
-    for exponent in range(-5, 9):
-        above = magnitude >= 2.0**exponent
-        spacing = jnp.where(above, 2.0 ** (exponent - 3), spacing)
-        inverse = jnp.where(above, 2.0 ** (3 - exponent), inverse)
-    grid_value = jnp.floor(magnitude * inverse + 0.5) * spacing
+    scaled = jnp.abs(values) * 512.0
+    above = scaled >= 2.0**11
+    power = jnp.where(above, 2.0**-1, 2.0**-9)
+    scaled = jnp.where(above, scaled * 2.0**-8, scaled)
+    for exponent in (4, 2, 1):
+        above = scaled >= 2.0 ** (3 + exponent)
+        power = jnp.where(above, power * 2.0**exponent, power)
+        scaled = jnp.where(above, scaled * 2.0**-exponent, scaled)
+    grid_value = jnp.floor(scaled + 0.5) * power
     return jnp.where(values < 0, -grid_value, grid_value)
 
 
@@ -44,7 +43,7 @@
     return jnp.sum(jnp.where(mine, ext.astype(F32), 0.0), axis=1, keepdims=True)
 
 
-def placement(gate, capacity):
+def placement(gate):
     rows = gate.shape[0]
     routed = gate > 0.0
     before = lax.broadcasted_iota(jnp.int32, (rows, rows), 1) < lax.broadcasted_iota(
@@ -52,44 +51,43 @@
     )
     ones = jnp.broadcast_to(jnp.where(routed, 1.0, 0.0), (rows, LANES)).astype(BF16)
     rank = jnp.dot(jnp.where(before, 1.0, 0.0).astype(BF16), ones, preferred_element_type=F32)
-    rank = rank[:, :1].astype(jnp.int32)
-    place = lax.broadcasted_iota(jnp.int32, (rows, capacity), 1)
-    return jnp.where(routed & (rank == place), 1.0, 0.0).astype(BF16)
+    place = lax.broadcasted_iota(jnp.int32, (rows, LANES), 1)
+    return jnp.where(routed & (rank.astype(jnp.int32) == place), 1.0, 0.0)
+
+
+def picker(gate, capacity):
+    return placement(gate).T[:capacity].astype(BF16)
 
 
 def pick_rows(onehot, rows):
-    return lax.dot_general(
-        onehot, rows, (((0,), (0,)), ((), ())), preferred_element_type=F32
-    ).astype(BF16)
+    return jnp.dot(onehot, rows, preferred_element_type=F32).astype(BF16)
 
 
 def prepare_kernel(experts, capacity, at_ref, tokens_ref, routes_ref, gates_ref, x_ref, y_ref):
     rows, features = tokens_ref.shape
+    sub = lax.broadcasted_iota(jnp.int32, (LANES, rows), 0)
+    value = jnp.zeros((LANES, rows), F32)
+    for k in range(routes_ref.shape[0]):
+        route = routes_ref[k : k + 1, :]
+        hit = (sub == route) | (sub == route + experts) | (sub == route + 2 * experts)
+        value = value + jnp.where(hit, gates_ref[k : k + 1, :], 0.0)
+    value = value.T
     lane = lax.broadcasted_iota(jnp.int32, (rows, LANES), 1)
-    routes = routes_ref[...]
-    gates = gates_ref[...]
-    value = jnp.zeros((rows, LANES), F32)
-    for k in range(routes.shape[1]):
-        hit = (
-            (lane == routes[:, k : k + 1])
-            | (lane == routes[:, k : k + 1] + experts)
-            | (lane == routes[:, k : k + 1] + 2 * experts)
-        )
-        value = value + jnp.where(hit, gates[:, k : k + 1], 0.0)
     high = value.astype(BF16).astype(F32)
     middle = (value - high).astype(BF16).astype(F32)
     low = value - high - middle
     ext = jnp.where(lane < experts, high, jnp.where(lane < 2 * experts, middle, low)).astype(BF16)
-    onehot = placement(gate_of(ext, at_ref[1], experts), capacity)
+    onehot = picker(gate_of(ext, at_ref[1], experts), capacity)
     x_ref[:, features:] = ext
     y_ref[:, features:] = pick_rows(onehot, ext)
     step = 4 * BLOCK
 
     def body(i, carry):
         start = pl.multiple_of(i * step, step)
+        tokens = tokens_ref[:, pl.ds(start, step)].astype(F32)
         parts = []
         for b in range(step // BLOCK):
-            block = tokens_ref[:, pl.ds(pl.multiple_of(start + b * BLOCK, BLOCK), BLOCK)].astype(F32)
+            block = tokens[:, b * BLOCK : (b + 1) * BLOCK]
             largest = jnp.max(jnp.abs(block), axis=1, keepdims=True)
             scale = ((largest + 1e-06) / 448.0).astype(BF16).astype(F32)
             parts.append((to_grid(block / scale) * scale).astype(BF16))
@@ -98,7 +96,7 @@
         y_ref[:, pl.ds(start, step)] = pick_rows(onehot, restored)
         return carry
 
-    lax.fori_loop(0, features // step, body, 0)
+    lax.fori_loop(0, features // step, body, 0, unroll=2)
 
 
 def prepare(at, tokens, routes, gates, experts, capacity):
@@ -110,33 +108,36 @@
             jax.ShapeDtypeStruct((rows, width), BF16),
             jax.ShapeDtypeStruct((capacity, width), BF16),
         ),
-        in_specs=[pl.BlockSpec(memory_space=pltpu.SMEM)]
-        + [pl.BlockSpec(memory_space=pltpu.VMEM)] * 3,
-        out_specs=(pl.BlockSpec(memory_space=pltpu.VMEM),) * 2,
-        compiler_params=params(),
+        in_specs=[SMEM] + [VMEM] * 3,
+        out_specs=(VMEM,) * 2,
+        compiler_params=params(12),
         name="prepare",
-    )(at, tokens, routes, gates)
+    )(at, tokens, routes.T, gates.T)
 
 
 def compact_kernel(experts, capacity, count, sums, at_ref, *refs):
-    ins, outs = refs[:count], refs[count:]
+    ins, outs = refs[:count], refs[len(refs) - (2 if sums else 1) :]
     features = ins[0].shape[1] - LANES
     step = 1024
-    pieces = []
-    if sums:
-        merged = outs[1]
-        merged[...] = ins[0][...] + ins[1][...]
-        sources = (merged,)
-    else:
-        sources = ins
-    for j, source in enumerate(sources):
-        onehot = placement(gate_of(source[:, features:], at_ref[1], experts), capacity)
-        outs[0][j, :, features:] = pick_rows(onehot, source[:, features:])
+    for j in range(1 if sums else count):
+
+        def load(columns, j=j):
+            if not sums:
+                return ins[j][:, columns]
+            merged = ins[0][:, columns] + ins[1][:, columns]
+            outs[1][:, columns] = merged
+            return merged
+
+        tail = slice(features, features + LANES)
+        ext = load(tail)
+        onehot = picker(gate_of(ext, at_ref[1], experts), capacity)
+        outs[0][j, :, tail] = pick_rows(onehot, ext)
         for start in range(0, features, step):
-            outs[0][j, :, start : start + step] = pick_rows(onehot, source[:, start : start + step])
-
-
-def compact(at, blocks, experts, capacity, sums=False):
+            columns = slice(start, start + step)
+            outs[0][j, :, columns] = pick_rows(onehot, load(columns))
+
+
+def compact(at, blocks, experts, capacity, sums=False, behind=()):
     rows, width = blocks[0].shape
     count = len(blocks)
     out_shape = [jax.ShapeDtypeStruct((1 if sums else count, capacity, width), BF16)]
@@ -145,12 +146,11 @@
     return pl.pallas_call(
         functools.partial(compact_kernel, experts, capacity, count, sums),
         out_shape=tuple(out_shape),
-        in_specs=[pl.BlockSpec(memory_space=pltpu.SMEM)]
-        + [pl.BlockSpec(memory_space=pltpu.VMEM)] * count,
-        out_specs=(pl.BlockSpec(memory_space=pltpu.VMEM),) * len(out_shape),
-        compiler_params=params(),
+        in_specs=[SMEM] + [VMEM] * count + [ANY] * len(behind),
+        out_specs=(VMEM,) * len(out_shape),
+        compiler_params=params(12),
         name="compact",
-    )(at, *blocks)
+    )(at, *blocks, *behind)
 
 
 def expert_kernel(experts, full, extra, k_steps, at_ref, *refs):
@@ -158,7 +158,7 @@
     rows_in, refs = refs[:count], refs[count:]
     exts, refs = refs[:count], refs[count:]
     gate_own, gate_other, up_own, up_other, down_own, down_other = refs[:6]
-    outs, (acc, hidden, weight) = refs[6 : 6 + count], refs[6 + count :]
+    outs, (acc, hidden, weight) = refs[len(refs) - 3 - count : -3], refs[-3:]
     i = pl.program_id(0)
     half = gate_own.shape[2]
     pieces = []
@@ -210,7 +210,7 @@
             offset += size
 
 
-def run_expert(at, full, extra, weights, experts, tile=1024):
+def run_expert(at, full, extra, weights, experts, behind=(), tile=1792):
     own, other = weights
     features, half = own[0].shape[1:]
     k_steps = features // tile
@@ -242,64 +242,51 @@
         ),
         out_shape=tuple(out_shape),
         grid=(k_steps + n_steps,),
-        in_specs=[pl.BlockSpec(memory_space=pltpu.SMEM)]
-        + row_specs
-        + ext_specs
-        + [up_spec] * 4
-        + [down_spec] * 2,
+        in_specs=[SMEM] + row_specs + ext_specs + [up_spec] * 4 + [down_spec] * 2
+        + [ANY] * len(behind),
         out_specs=tuple(out_specs),
         scratch_shapes=[
             pltpu.VMEM((total, 4 * half), F32),
             pltpu.VMEM((total, 2 * half), BF16),
             pltpu.VMEM((total, LANES), F32),
         ],
-        compiler_params=params(1),
+        compiler_params=params(44, 1),
         cost_estimate=pl.CostEstimate(
             flops=12 * total * features * half,
             bytes_accessed=12 * features * half + 4 * total * features,
             transcendentals=2 * total * half,
         ),
         name="expert",
-    )(at, *inputs, *inputs, own[0], other[0], own[1], other[1], own[2], other[2])
-
-
-def combine_kernel(experts, capacity, adds, at_ref, ext_ref, mine_ref, theirs_ref, *refs):
-    out_ref, onehot = refs[adds], refs[adds + 1]
-
-    @pl.when(pl.program_id(0) == 0)
-    def _():
-        gate = gate_of(ext_ref[...], at_ref[1], experts)
-        onehot[...] = placement(gate, capacity).astype(F32)
-
-    total = mine_ref[...].astype(F32) + jnp.dot(
-        onehot[...].astype(BF16), theirs_ref[0], preferred_element_type=F32
-    )
-    for ref in refs[:adds]:
-        total = total + ref[...].astype(F32)
-    out_ref[...] = total.astype(BF16)
-
-
-def combine(at, block, mine, theirs, index, adds, experts, tile=1792):
+    )(at, *inputs, *inputs, own[0], other[0], own[1], other[1], own[2], other[2], *behind)
+
+
+def combine_kernel(experts, capacity, index, adds, at_ref, block_ref, mine_ref, theirs_ref, *refs):
+    out_ref = refs[-1]
+    features = mine_ref.shape[1]
+    onehot = placement(gate_of(block_ref[:, features:], at_ref[1], experts))
+    onehot = onehot[:, :capacity].astype(BF16)
+    step = 1024
+    for start in range(0, features, step):
+        columns = slice(start, start + step)
+        total = mine_ref[:, columns].astype(F32) + jnp.dot(
+            onehot, theirs_ref[index, :, columns], preferred_element_type=F32
+        )
+        for ref in refs[:adds]:
+            total = total + ref[:, columns].astype(F32)
+        out_ref[:, columns] = total.astype(BF16)
+
+
+def combine(at, block, mine, theirs, index, adds, experts, behind=()):
     rows, features = mine.shape
     capacity = theirs.shape[1]
-    last = features // LANES
-    spec = pl.BlockSpec((rows, tile), lambda i: (0, i))
     return pl.pallas_call(
-        functools.partial(combine_kernel, experts, capacity, len(adds)),
+        functools.partial(combine_kernel, experts, capacity, index, len(adds)),
         out_shape=jax.ShapeDtypeStruct((rows, features), BF16),
-        grid=(features // tile,),
-        in_specs=[
-            pl.BlockSpec(memory_space=pltpu.SMEM),
-            pl.BlockSpec((rows, LANES), lambda i: (0, last)),
-            spec,
-            pl.BlockSpec((1, capacity, tile), lambda i: (index, 0, i)),
-        ]
-        + [spec] * len(adds),
-        out_specs=spec,
-        scratch_shapes=[pltpu.VMEM((rows, capacity), F32)],
-        compiler_params=params(1),
+        in_specs=[SMEM] + [VMEM] * (3 + len(adds)) + [ANY] * len(behind),
+        out_specs=VMEM,
+        compiler_params=params(14),
         name="combine",
-    )(at, block, mine, theirs, *adds)
+    )(at, block, mine, theirs, *adds, *behind)
 
 
 DEPTH = 4
@@ -339,39 +326,36 @@
     from_left = send(block, dz=1)
     from_right = send(block, dz=-1)
     picked = send(picked[None], dy=1)
-    (near_picked,) = compact(at, (from_left, from_right), experts, capacity)
+    mid_left = send(after(from_left, from_right), dz=1)
+    mid_right = send(after(from_right, from_left), dz=-1)
+    (near_picked,) = compact(at, (from_left, from_right), experts, capacity, behind=(picked,))
+    far = send_far(after(block, mid_left, mid_right, near_picked))
     near_picked = send(near_picked, dy=1)
-    mid_left = send(from_left, dz=1)
-    mid_right = send(from_right, dz=-1)
     mid_picked, mid = compact(at, (mid_left, mid_right), experts, capacity, sums=True)
     mid_picked = send(mid_picked, dy=1)
-    far = send_far(after(block, mid_left, mid_right))
+    own_out, left_out, right_out, own_back, near_back = run_expert(
+        at, (block, from_left, from_right), (picked, near_picked), weights, experts
+    )
     (far_picked,) = compact(at, (far,), experts, capacity)
     far_picked = send(far_picked, dy=1)
-
-    own_out, left_out, right_out, own_back, near_back = run_expert(
-        at, (block, from_left, from_right), (picked, near_picked), weights, experts
-    )
     mid_out, far_out, mid_back, far_back = run_expert(
-        at, (mid, far), (mid_picked, far_picked), weights, experts
+        at, (mid, far), (mid_picked, far_picked), weights, experts, behind=(near_back,)
     )
     near_back = send(near_back, dy=1)
-    far_back = send(far_back, dy=1)
-    mid_back = send(mid_back, dy=1)
-    own_back = send(after(own_back, mid_back, far_back), dy=1)
-
-    far_sum = combine(at, far, far_out, far_back, 0, (), experts)
-    far_home = send_far(far_sum)
+    mid_back = send(after(mid_back, near_back), dy=1)
+    far_back = send(after(far_back, mid_back), dy=1)
+    own_back = send(after(own_back, far_back), dy=1)
+
     mid_sum = combine(at, mid, mid_out, mid_back, 0, (), experts)
     to_right = send(mid_sum, dz=1, only=(0, 1))
     to_left = send(mid_sum, dz=-1, only=(3, 2))
+    far_sum = combine(at, far, far_out, far_back, 0, (), experts, behind=(mid_sum,))
+    far_home = send_far(far_sum)
     right_sum = combine(at, from_right, right_out, near_back, 1, (to_right,), experts)
     left_sum = combine(at, from_left, left_out, near_back, 0, (to_left,), experts)
     home_left = send(right_sum, dz=1)
     home_right = send(left_sum, dz=-1)
-    return combine(
-        at, block, own_out, own_back, 0, (far_home, home_left, home_right), experts
-    )
+    return combine(at, block, own_out, own_back, 0, (far_home, home_left, home_right), experts)
 
 
 def partner(shard, axis, stride):

time: 263 us -> 221 us (0.84)
  Pallas kernels: 93.2 us -> 60.5 us
  local copies, waits for them, and re-layouts: 10.4 us -> 2.54 us
    pallas_call x5, Pallas kernels: 22 us -> 7.11 us  [combine(): pl.pallas_call(functools.partial(combine_kernel, experts, capacity, index...]
    ppermute x19, waiting for transfers between devices: 107 us -> 97.9 us  [send(): return lax.ppermute(array, 'ep', pairs)]
    unnamed x42 -> x6, local copies, waits for them, and re-layouts: 10.4 us -> 2.54 us
    pallas_call x2, Pallas kernels: 52.2 us -> 44.8 us  [run_expert(): pl.pallas_call(functools.partial(expert_kernel, experts, tuple((a.shape[0...]
    ppermute x2, waiting for transfers between devices: 16.9 us -> 24.3 us  [send_far(): return lax.ppermute(array, 'ep', pairs)]
    pallas_call x3, Pallas kernels: 9.51 us -> 3.81 us  [compact(): pl.pallas_call(functools.partial(compact_kernel, experts, capacity, count...]
    pallas_call x1, Pallas kernels: 9.47 us -> 4.79 us  [prepare(): pl.pallas_call(functools.partial(prepare_kernel, experts, capacity), out_...]
  transfers between devices with their start and end apart: 21 -> 21, of which waited for: 10 -> 13; matrix products, arithmetic and copies ran while one was open for 1% -> 0% of each run, Pallas kernels for 34% -> 26%
where the time goes in v1:
time: 221 us
  waiting for transfers between devices  122 us (55%)
  Pallas kernels  60.5 us (27%)
  starting transfers between devices  35.2 us (16%)
  local copies, waits for them, and re-layouts  2.54 us (1%)
    ppermute x19, waiting for transfers between devices, send(): return lax.ppermute(array, 'ep', pairs)  97.9 us
    pallas_call x2, Pallas kernels, run_expert(): pl.pallas_call(functools.partial(expert_kernel, experts, tuple((a.shape[0...  44.8 us
    ppermute x19, starting transfers between devices, send(): return lax.ppermute(array, 'ep', pairs)  29.3 us
    ppermute x2, waiting for transfers between devices, send_far(): return lax.ppermute(array, 'ep', pairs)  24.3 us
    pallas_call x5, Pallas kernels, combine(): pl.pallas_call(functools.partial(combine_kernel, experts, capacity, index...  7.11 us
    ppermute x2, starting transfers between devices, send_far(): return lax.ppermute(array, 'ep', pairs)  5.88 us
    pallas_call x1, Pallas kernels, prepare(): pl.pallas_call(functools.partial(prepare_kernel, experts, capacity), out_...  4.79 us
  transfers between devices with their start and end apart: 21, of which 13 were waited for; matrix products, arithmetic and copies ran while one was open for 0% of the time, Pallas kernels for 26%

profile of v1, /device:TPU:0, one launch (start us, length us, event | category | flops | bytes accessed | tf_op | source)
XLA Modules:
  0.0 220.7 jit_solution(5465579081156640094)
XLA Ops:
  0.0 0.5 collective-permute-start.4
  0.5 0.1 collective-permute-start.5
  0.5 0.5 collective-permute-start.6
  1.0 0.1 pad_add_fusion.at_ref
  1.0 0.0 copy-start
  1.0 1.2 copy-done
  2.2 0.0 copy-start.1
  2.2 0.7 copy-done.1
  2.9 0.0 copy-start.2
  2.9 0.7 copy-done.2
  3.6 4.8 %prepare.1 = (bf16[64,7296]{1,0:T(8,128)(2,1)S(1)}, bf16[40,7296]{1,0:T(8,128)(2,1)S(1)}) custom-call(s32[2]{0:T(128)S(1)} %pad_add_fusion.at_ref, bf16[64,7168]{1,0:T(8,128)(2,1)S(1)} %copy-done, s32[4,64]{1,0:T(4,128)S(1)} %bitcast.5, f32[4,64]{1,0:T(4,128)S(1)} %bitcast.6), custom_call_target="tpu_custom_call" | custom-call | tf_op jit(solution)/shard_map/prepare/pallas_call | solution.py:105
  8.4 1.3 collective-permute-start.1
  9.7 5.2 %collective-permute-start = (bf16[64,7296]{1,0:T(8,128)(2,1)S(1)}, bf16[64,7296]{1,0:T(8,128)(2,1)S(1)}, u32[]{:S(2)}, u32[]{:S(2)}) collective-permute-start(bf16[64,7296]{1,0:T(8,128)(2,1)S(1)} %get-tuple-element.31.refs_0_.refs_5_.block_ref), channel_id=1, source_target_pairs={{0,4},{1,5},{2,6},{3,7},{4,8},{5,9},{6,10},{7,11},{8,12},{9,13},{1... | collective-permute-start | bytes 2801672 | tf_op jit(solution)/shard_map/ppermute | solution.py:302
  14.9 19.4 %collective-permute-done.1.refs_1_.refs_2_.refs_7_.block_ref = bf16[64,7296]{1,0:T(8,128)(2,1)S(1)} collective-permute-done((bf16[64,7296]{1,0:T(8,128)(2,1)S(1)}, bf16[64,7296]{1,0:T(8,128)(2,1)S(1)}, u32[]{:S(2)}, u32[]{:S(2)}) %collective-permute-start.1) | collective-permute-done | bytes 933920 | tf_op jit(solution)/shard_map/ppermute | solution.py:302
  34.2 1.7 collective-permute-start.2
  35.9 0.0 collective-permute-done.refs_0_.refs_1_.refs_6_.block_ref
  35.9 3.9 %collective-permute-start.7 = (bf16[64,7296]{1,0:T(8,128)(2,1)S(1)}, bf16[64,7296]{1,0:T(8,128)(2,1)S(1)}, u32[]{:S(2)}, u32[]{:S(2)}) collective-permute-start(bf16[64,7296]{1,0:T(8,128)(2,1)S(1)} %collective-permute-done.refs_0_.refs_1_.refs_6_.block_ref), channel_id=1, source_target_pairs={{0,4},{1,5},{2,6},{3,7},{4,8},{5,9},{6,10},{7,11},{8,12},{9,13},{1... | collective-permute-start | bytes 2801672 | tf_op jit(solution)/shard_map/ppermute | solution.py:302
  39.9 9.4 %collective-permute-done.2.refs_2_.refs_3_.refs_8_ = bf16[1,40,7296]{2,1,0:T(8,128)(2,1)S(1)} collective-permute-done((bf16[1,40,7296]{2,1,0:T(8,128)(2,1)S(1)}, bf16[1,40,7296]{2,1,0:T(8,128)(2,1)S(1)}, u32[]{:S(2)}, u32[]{:S(2)}) %collective-permute-start.2) | collective-permute-done | bytes 583712 | tf_op jit(solution)/shard_map/ppermute | solution.py:302
  49.3 1.3 collective-permute-start.8
  50.5 1.5 compact.3
  52.1 7.5 %collective-permute-done.7.refs_0_ = bf16[64,7296]{1,0:T(8,128)(2,1)S(1)} collective-permute-done((bf16[64,7296]{1,0:T(8,128)(2,1)S(1)}, bf16[64,7296]{1,0:T(8,128)(2,1)S(1)}, u32[]{:S(2)}, u32[]{:S(2)}) %collective-permute-start.7) | collective-permute-done | bytes 933920 | tf_op jit(solution)/shard_map/ppermute | solution.py:302
  59.6 1.4 collective-permute-start.3
  61.0 11.8 %collective-permute-done.8.refs_1_ = bf16[64,7296]{1,0:T(8,128)(2,1)S(1)} collective-permute-done((bf16[64,7296]{1,0:T(8,128)(2,1)S(1)}, bf16[64,7296]{1,0:T(8,128)(2,1)S(1)}, u32[]{:S(2)}, u32[]{:S(2)}) %collective-permute-start.8) | collective-permute-done | bytes 933920 | tf_op jit(solution)/shard_map/ppermute | solution.py:302
  72.8 3.2 %collective-permute-start.9 = (bf16[64,7296]{1,0:T(8,128)(2,1)S(1)}, bf16[64,7296]{1,0:T(8,128)(2,1)S(1)}, u32[]{:S(2)}, u32[]{:S(2)}) collective-permute-start(bf16[64,7296]{1,0:T(8,128)(2,1)S(1)} %get-tuple-element.31.refs_0_.refs_5_.block_ref), channel_id=1, source_target_pairs={{0,12},{1,13},{2,14},{3,15},{12,0},{13,1},{14,2},{15,3},{16,28},{1... | collective-permute-start | bytes 2801672 | tf_op jit(solution)/shard_map/ppermute | solution.py:307
  76.0 1.1 compact.4
  77.2 20.1 %collective-permute-done.9.refs_0_.refs_1_.refs_5_.block_ref = bf16[64,7296]{1,0:T(8,128)(2,1)S(1)} collective-permute-done((bf16[64,7296]{1,0:T(8,128)(2,1)S(1)}, bf16[64,7296]{1,0:T(8,128)(2,1)S(1)}, u32[]{:S(2)}, u32[]{:S(2)}) %collective-permute-start.9) | collective-permute-done | bytes 933920 | tf_op jit(solution)/shard_map/ppermute | solution.py:307
  97.2 1.0 collective-permute-start.10
  98.3 1.1 compact.5
  99.4 0.0 collective-permute-done.3.refs_4_.refs_9_
  99.4 1.1 collective-permute-start.11
  100.5 0.0 collective-permute-done.4.refs_11_.refs_9_
  100.5 0.0 collective-permute-done.5.refs_13_.refs_11_
  100.5 0.0 collective-permute-done.6.refs_15_.refs_13_
  100.5 24.1 %expert.2 = (bf16[64,7168]{1,0:T(8,128)(2,1)S(1)}, bf16[64,7168]{1,0:T(8,128)(2,1)S(1)}, bf16[64,7168]{1,0:T(8,128)(2,1)S(1)}, bf16[1,40,7168]{2,1,0:T(8,128)(2,1)S(1)}, bf16[2,40,7168]{2,1,0:T(8,128)(2,1)S(1)}) custom-call(s32[2]{0:T(128)S(1)} %pad_add_fusion.at_ref, bf16[64,7296]{1,0:T(8,128)(2,1)S(1)} %get-tuple-element.31.refs_0_.refs_5_.block_ref, ...), custom_call_target="tpu_custom_call" | custom-call | flops 13740539904 | bytes 52985856 | tf_op jit(solution)/shard_map/expert/pallas_call | solution.py:235
  124.7 1.1 collective-permute-start.12
  125.7 0.0 collective-permute-done.10.refs_2_.refs_6_
  125.7 0.0 collective-permute-done.11.refs_3_.refs_7_
  125.7 20.6 %expert.3 = (bf16[64,7168]{1,0:T(8,128)(2,1)S(1)}, bf16[64,7168]{1,0:T(8,128)(2,1)S(1)}, bf16[1,40,7168]{2,1,0:T(8,128)(2,1)S(1)}, bf16[1,40,7168]{2,1,0:T(8,128)(2,1)S(1)}) custom-call(s32[2]{0:T(128)S(1)} %pad_add_fusion.at_ref, bf16[64,7296]{1,0:T(8,128)(2,1)S(1)} %get-tuple-element.30.refs_0_.refs_4_.block_ref, ...), custom_call_target="tpu_custom_call" | custom-call | flops 9160359936 | bytes 50003968 | tf_op jit(solution)/shard_map/expert/pallas_call | solution.py:235
  146.4 3.8 %collective-permute-done.12.theirs_ref = bf16[2,40,7168]{2,1,0:T(8,128)(2,1)S(1)} collective-permute-done((bf16[2,40,7168]{2,1,0:T(8,128)(2,1)S(1)}, bf16[2,40,7168]{2,1,0:T(8,128)(2,1)S(1)}, u32[]{:S(2)}, u32[]{:S(2)}) %collective-permute-start.12) | collective-permute-done | bytes 1146912 | tf_op jit(solution)/shard_map/ppermute | solution.py:302
  150.2 1.0 collective-permute-start.13
  151.2 9.7 %collective-permute-done.13.theirs_ref = bf16[1,40,7168]{2,1,0:T(8,128)(2,1)S(1)} collective-permute-done((bf16[1,40,7168]{2,1,0:T(8,128)(2,1)S(1)}, bf16[1,40,7168]{2,1,0:T(8,128)(2,1)S(1)}, u32[]{:S(2)}, u32[]{:S(2)}) %collective-permute-start.13) | collective-permute-done | bytes 573472 | tf_op jit(solution)/shard_map/ppermute | solution.py:302
  160.9 1.1 combine.5.refs_0_
  162.0 0.7 collective-permute-start.19
  162.7 1.3 collective-permute-start.17
  164.1 0.8 collective-permute-start.14
  164.9 9.0 %collective-permute-done.14.theirs_ref = bf16[1,40,7168]{2,1,0:T(8,128)(2,1)S(1)} collective-permute-done((bf16[1,40,7168]{2,1,0:T(8,128)(2,1)S(1)}, bf16[1,40,7168]{2,1,0:T(8,128)(2,1)S(1)}, u32[]{:S(2)}, u32[]{:S(2)}) %collective-permute-start.14) | collective-permute-done | bytes 573472 | tf_op jit(solution)/shard_map/ppermute | solution.py:302
  173.9 1.1 combine.6
  175.0 2.7 %collective-permute-start.16 = (bf16[64,7168]{1,0:T(8,128)(2,1)S(1)}, bf16[64,7168]{1,0:T(8,128)(2,1)S(1)}, u32[]{:S(2)}, u32[]{:S(2)}) collective-permute-start(bf16[64,7168]{1,0:T(8,128)(2,1)S(1)} %combine.6), channel_id=1, source_target_pairs={{0,12},{1,13},{2,14},{3,15},{12,0},{13,1},{14,2},{15,3},{16,28},{1... | collective-permute-start | bytes 2752520 | tf_op jit(solution)/shard_map/ppermute | solution.py:307
  177.7 0.0 collective-permute-done.19.refs_0_
  177.7 1.2 combine.8
  179.0 1.3 collective-permute-start.20
  180.3 4.5 %collective-permute-done.17.refs_0_ = bf16[64,7168]{1,0:T(8,128)(2,1)S(1)} collective-permute-done((bf16[64,7168]{1,0:T(8,128)(2,1)S(1)}, bf16[64,7168]{1,0:T(8,128)(2,1)S(1)}, u32[]{:S(2)}, u32[]{:S(2)}) %collective-permute-start.17) | collective-permute-done | bytes 917536 | tf_op jit(solution)/shard_map/ppermute | solution.py:302
  184.8 1.2 combine.7
  186.0 4.5 %collective-permute-start.18 = (bf16[64,7168]{1,0:T(8,128)(2,1)S(1)}, bf16[64,7168]{1,0:T(8,128)(2,1)S(1)}, u32[]{:S(2)}, u32[]{:S(2)}) collective-permute-start(bf16[64,7168]{1,0:T(8,128)(2,1)S(1)} %combine.7), channel_id=1, source_target_pairs={{0,4},{1,5},{2,6},{3,7},{4,8},{5,9},{6,10},{7,11},{8,12},{9,13},{1... | collective-permute-start | bytes 2752520 | tf_op jit(solution)/shard_map/ppermute | solution.py:302
  190.5 0.8 collective-permute-start.15
  191.3 8.9 %collective-permute-done.15.theirs_ref = bf16[1,40,7168]{2,1,0:T(8,128)(2,1)S(1)} collective-permute-done((bf16[1,40,7168]{2,1,0:T(8,128)(2,1)S(1)}, bf16[1,40,7168]{2,1,0:T(8,128)(2,1)S(1)}, u32[]{:S(2)}, u32[]{:S(2)}) %collective-permute-start.15) | collective-permute-done | bytes 573472 | tf_op jit(solution)/shard_map/ppermute | solution.py:302
  200.3 4.2 %collective-permute-done.16.refs_0_ = bf16[64,7168]{1,0:T(8,128)(2,1)S(1)} collective-permute-done((bf16[64,7168]{1,0:T(8,128)(2,1)S(1)}, bf16[64,7168]{1,0:T(8,128)(2,1)S(1)}, u32[]{:S(2)}, u32[]{:S(2)}) %collective-permute-start.16) | collective-permute-done | bytes 917536 | tf_op jit(solution)/shard_map/ppermute | solution.py:307
  204.5 10.7 %collective-permute-done.20.refs_2_ = bf16[64,7168]{1,0:T(8,128)(2,1)S(1)} collective-permute-done((bf16[64,7168]{1,0:T(8,128)(2,1)S(1)}, bf16[64,7168]{1,0:T(8,128)(2,1)S(1)}, u32[]{:S(2)}, u32[]{:S(2)}) %collective-permute-start.20) | collective-permute-done | bytes 917536 | tf_op jit(solution)/shard_map/ppermute | solution.py:302
  215.2 3.1 %collective-permute-done.18.refs_1_ = bf16[64,7168]{1,0:T(8,128)(2,1)S(1)} collective-permute-done((bf16[64,7168]{1,0:T(8,128)(2,1)S(1)}, bf16[64,7168]{1,0:T(8,128)(2,1)S(1)}, u32[]{:S(2)}, u32[]{:S(2)}) %collective-permute-start.18) | collective-permute-done | bytes 917536 | tf_op jit(solution)/shard_map/ppermute | solution.py:302
  218.3 2.4 %combine.9 = bf16[64,7168]{1,0:T(8,128)(2,1)} custom-call(s32[2]{0:T(128)S(1)} %pad_add_fusion.at_ref, bf16[64,7296]{1,0:T(8,128)(2,1)S(1)} %get-tuple-element.31.refs_0_.refs_5_.block_ref, bf16[64,7168]{1,0:T(8,128)(2,1)S(1)} %get-tuple-element.26.mine_ref, bf16[1,40,7168]{2,1,0:T(8,128)(2,1)S(1)} %collective-permute-done.15.theirs_ref, ...), custom_call_target="tpu_custom_call" | custom-call | tf_op jit(solution)/shard_map/combine/pallas_call | solution.py:282
Async XLA Ops:
  0.0 100.5 %collective-permute-start.4 = (bf16[1,7168,512]{2,1,0:T(8,128)(2,1)}, bf16[1,7168,512]{2,1,0:T(8,128)(2,1)}, u32[]{:S(2)}, u32[]{:S(2)}) collective-permute-start(bf16[1,7168,512]{2,1,0:T(8,128)(2,1)} %refs_8_.1), channel_id=1, source_target_pairs={{0,1},{1,0},{2,3},{3,2},{4,5},{5,4},{6,7},{7,6},{8,9},{9,8},{10,11... | collective-permute-start | bytes 22020104 | tf_op jit(solution)/shard_map/ppermute | solution.py:302
  0.5 100.0 %collective-permute-start.5 = (bf16[1,7168,512]{2,1,0:T(8,128)(2,1)}, bf16[1,7168,512]{2,1,0:T(8,128)(2,1)}, u32[]{:S(2)}, u32[]{:S(2)}) collective-permute-start(bf16[1,7168,512]{2,1,0:T(8,128)(2,1)} %refs_10_.3), channel_id=1, source_target_pairs={{0,1},{1,0},{2,3},{3,2},{4,5},{5,4},{6,7},{7,6},{8,9},{9,8},{10,11... | collective-permute-start | bytes 22020104 | tf_op jit(solution)/shard_map/ppermute | solution.py:302
  0.5 100.0 %collective-permute-start.6 = (bf16[1,512,7168]{2,1,0:T(8,128)(2,1)}, bf16[1,512,7168]{2,1,0:T(8,128)(2,1)}, u32[]{:S(2)}, u32[]{:S(2)}) collective-permute-start(bf16[1,512,7168]{2,1,0:T(8,128)(2,1)} %refs_12_.3), channel_id=1, source_target_pairs={{0,1},{1,0},{2,3},{3,2},{4,5},{5,4},{6,7},{7,6},{8,9},{9,8},{10,11... | collective-permute-start | bytes 22020104 | tf_op jit(solution)/shard_map/ppermute | solution.py:302
  1.0 1.2 copy-start
  2.2 0.7 copy-start.1
  2.9 0.7 copy-start.2
  8.4 25.8 %collective-permute-start.1 = (bf16[64,7296]{1,0:T(8,128)(2,1)S(1)}, bf16[64,7296]{1,0:T(8,128)(2,1)S(1)}, u32[]{:S(2)}, u32[]{:S(2)}) collective-permute-start(bf16[64,7296]{1,0:T(8,128)(2,1)S(1)} %get-tuple-element.31.refs_0_.refs_5_.block_ref), channel_id=1, source_target_pairs={{4,0},{5,1},{6,2},{7,3},{8,4},{9,5},{10,6},{11,7},{12,8},{13,9},{1... | collective-permute-start | bytes 2801672 | tf_op jit(solution)/shard_map/ppermute | solution.py:302
  9.7 26.2 %collective-permute-start = (bf16[64,7296]{1,0:T(8,128)(2,1)S(1)}, bf16[64,7296]{1,0:T(8,128)(2,1)S(1)}, u32[]{:S(2)}, u32[]{:S(2)}) collective-permute-start(bf16[64,7296]{1,0:T(8,128)(2,1)S(1)} %get-tuple-element.31.refs_0_.refs_5_.block_ref), channel_id=1, source_target_pairs={{0,4},{1,5},{2,6},{3,7},{4,8},{5,9},{6,10},{7,11},{8,12},{9,13},{1... | collective-permute-start | bytes 2801672 | tf_op jit(solution)/shard_map/ppermute | solution.py:302
  34.2 15.0 %collective-permute-start.2 = (bf16[1,40,7296]{2,1,0:T(8,128)(2,1)S(1)}, bf16[1,40,7296]{2,1,0:T(8,128)(2,1)S(1)}, u32[]{:S(2)}, u32[]{:S(2)}) collective-permute-start(bf16[1,40,7296]{2,1,0:T(8,128)(2,1)S(1)} %bitcast.7), channel_id=1, source_target_pairs={{0,2},{1,3},{2,0},{3,1},{4,6},{5,7},{6,4},{7,5},{8,10},{9,11},{10,... | collective-permute-start | bytes 1751048 | tf_op jit(solution)/shard_map/ppermute | solution.py:302
  35.9 23.7 %collective-permute-start.7 = (bf16[64,7296]{1,0:T(8,128)(2,1)S(1)}, bf16[64,7296]{1,0:T(8,128)(2,1)S(1)}, u32[]{:S(2)}, u32[]{:S(2)}) collective-permute-start(bf16[64,7296]{1,0:T(8,128)(2,1)S(1)} %collective-permute-done.refs_0_.refs_1_.refs_6_.block_ref), channel_id=1, source_target_pairs={{0,4},{1,5},{2,6},{3,7},{4,8},{5,9},{6,10},{7,11},{8,12},{9,13},{1... | collective-permute-start | bytes 2801672 | tf_op jit(solution)/shard_map/ppermute | solution.py:302
  49.3 23.6 %collective-permute-start.8 = (bf16[64,7296]{1,0:T(8,128)(2,1)S(1)}, bf16[64,7296]{1,0:T(8,128)(2,1)S(1)}, u32[]{:S(2)}, u32[]{:S(2)}) collective-permute-start(bf16[64,7296]{1,0:T(8,128)(2,1)S(1)} %collective-permute-done.1.refs_1_.refs_2_.refs_7_.block_ref), channel_id=1, source_target_pairs={{4,0},{5,1},{6,2},{7,3},{8,4},{9,5},{10,6},{11,7},{12,8},{13,9},{1... | collective-permute-start | bytes 2801672 | tf_op jit(solution)/shard_map/ppermute | solution.py:302
  59.6 39.8 %collective-permute-start.3 = (bf16[2,40,7296]{2,1,0:T(8,128)(2,1)S(1)}, bf16[2,40,7296]{2,1,0:T(8,128)(2,1)S(1)}, u32[]{:S(2)}, u32[]{:S(2)}) collective-permute-start(bf16[2,40,7296]{2,1,0:T(8,128)(2,1)S(1)} %compact.3), channel_id=1, source_target_pairs={{0,2},{1,3},{2,0},{3,1},{4,6},{5,7},{6,4},{7,5},{8,10},{9,11},{10,... | collective-permute-start | bytes 3502088 | tf_op jit(solution)/shard_map/ppermute | solution.py:302
  72.8 24.4 %collective-permute-start.9 = (bf16[64,7296]{1,0:T(8,128)(2,1)S(1)}, bf16[64,7296]{1,0:T(8,128)(2,1)S(1)}, u32[]{:S(2)}, u32[]{:S(2)}) collective-permute-start(bf16[64,7296]{1,0:T(8,128)(2,1)S(1)} %get-tuple-element.31.refs_0_.refs_5_.block_ref), channel_id=1, source_target_pairs={{0,12},{1,13},{2,14},{3,15},{12,0},{13,1},{14,2},{15,3},{16,28},{1... | collective-permute-start | bytes 2801672 | tf_op jit(solution)/shard_map/ppermute | solution.py:307
  97.2 28.5 %collective-permute-start.10 = (bf16[1,40,7296]{2,1,0:T(8,128)(2,1)S(1)}, bf16[1,40,7296]{2,1,0:T(8,128)(2,1)S(1)}, u32[]{:S(2)}, u32[]{:S(2)}) collective-permute-start(bf16[1,40,7296]{2,1,0:T(8,128)(2,1)S(1)} %get-tuple-element.32), channel_id=1, source_target_pairs={{0,2},{1,3},{2,0},{3,1},{4,6},{5,7},{6,4},{7,5},{8,10},{9,11},{10,... | collective-permute-start | bytes 1751048 | tf_op jit(solution)/shard_map/ppermute | solution.py:302
  99.4 26.3 %collective-permute-start.11 = (bf16[1,40,7296]{2,1,0:T(8,128)(2,1)S(1)}, bf16[1,40,7296]{2,1,0:T(8,128)(2,1)S(1)}, u32[]{:S(2)}, u32[]{:S(2)}) collective-permute-start(bf16[1,40,7296]{2,1,0:T(8,128)(2,1)S(1)} %compact.5), channel_id=1, source_target_pairs={{0,2},{1,3},{2,0},{3,1},{4,6},{5,7},{6,4},{7,5},{8,10},{9,11},{10,... | collective-permute-start | bytes 1751048 | tf_op jit(solution)/shard_map/ppermute | solution.py:302
  124.7 25.5 %collective-permute-start.12 = (bf16[2,40,7168]{2,1,0:T(8,128)(2,1)S(1)}, bf16[2,40,7168]{2,1,0:T(8,128)(2,1)S(1)}, u32[]{:S(2)}, u32[]{:S(2)}) collective-permute-start(bf16[2,40,7168]{2,1,0:T(8,128)(2,1)S(1)} %get-tuple-element.33.refs_14_), channel_id=1, source_target_pairs={{0,2},{1,3},{2,0},{3,1},{4,6},{5,7},{6,4},{7,5},{8,10},{9,11},{10,... | collective-permute-start | bytes 3440648 | tf_op jit(solution)/shard_map/ppermute | solution.py:302
  150.2 10.7 %collective-permute-start.13 = (bf16[1,40,7168]{2,1,0:T(8,128)(2,1)S(1)}, bf16[1,40,7168]{2,1,0:T(8,128)(2,1)S(1)}, u32[]{:S(2)}, u32[]{:S(2)}) collective-permute-start(bf16[1,40,7168]{2,1,0:T(8,128)(2,1)S(1)} %get-tuple-element.36), channel_id=1, source_target_pairs={{0,2},{1,3},{2,0},{3,1},{4,6},{5,7},{6,4},{7,5},{8,10},{9,11},{10,... | collective-permute-start | bytes 1720328 | tf_op jit(solution)/shard_map/ppermute | solution.py:302
  162.0 15.7 %collective-permute-start.19 = (bf16[64,7168]{1,0:T(8,128)(2,1)S(1)}, bf16[64,7168]{1,0:T(8,128)(2,1)S(1)}, u32[]{:S(2)}, u32[]{:S(2)}) collective-permute-start(bf16[64,7168]{1,0:T(8,128)(2,1)S(1)} %combine.5.refs_0_), channel_id=1, source_target_pairs={{8,4},{9,5},{10,6},{11,7},{12,8},{13,9},{14,10},{15,11},{24,20},{2... | collective-permute-start | bytes 2752520 | tf_op jit(solution)/shard_map/ppermute | solution.py:302
  162.7 22.1 %collective-permute-start.17 = (bf16[64,7168]{1,0:T(8,128)(2,1)S(1)}, bf16[64,7168]{1,0:T(8,128)(2,1)S(1)}, u32[]{:S(2)}, u32[]{:S(2)}) collective-permute-start(bf16[64,7168]{1,0:T(8,128)(2,1)S(1)} %combine.5.refs_0_), channel_id=1, source_target_pairs={{0,4},{1,5},{2,6},{3,7},{4,8},{5,9},{6,10},{7,11},{16,20},{17,21},... | collective-permute-start | bytes 2752520 | tf_op jit(solution)/shard_map/ppermute | solution.py:302
  164.1 9.8 %collective-permute-start.14 = (bf16[1,40,7168]{2,1,0:T(8,128)(2,1)S(1)}, bf16[1,40,7168]{2,1,0:T(8,128)(2,1)S(1)}, u32[]{:S(2)}, u32[]{:S(2)}) collective-permute-start(bf16[1,40,7168]{2,1,0:T(8,128)(2,1)S(1)} %get-tuple-element.37), channel_id=1, source_target_pairs={{0,2},{1,3},{2,0},{3,1},{4,6},{5,7},{6,4},{7,5},{8,10},{9,11},{10,... | collective-permute-start | bytes 1720328 | tf_op jit(solution)/shard_map/ppermute | solution.py:302
  175.0 29.5 %collective-permute-start.16 = (bf16[64,7168]{1,0:T(8,128)(2,1)S(1)}, bf16[64,7168]{1,0:T(8,128)(2,1)S(1)}, u32[]{:S(2)}, u32[]{:S(2)}) collective-permute-start(bf16[64,7168]{1,0:T(8,128)(2,1)S(1)} %combine.6), channel_id=1, source_target_pairs={{0,12},{1,13},{2,14},{3,15},{12,0},{13,1},{14,2},{15,3},{16,28},{1... | collective-permute-start | bytes 2752520 | tf_op jit(solution)/shard_map/ppermute | solution.py:307
  179.0 36.2 %collective-permute-start.20 = (bf16[64,7168]{1,0:T(8,128)(2,1)S(1)}, bf16[64,7168]{1,0:T(8,128)(2,1)S(1)}, u32[]{:S(2)}, u32[]{:S(2)}) collective-permute-start(bf16[64,7168]{1,0:T(8,128)(2,1)S(1)} %combine.8), channel_id=1, source_target_pairs={{4,0},{5,1},{6,2},{7,3},{8,4},{9,5},{10,6},{11,7},{12,8},{13,9},{1... | collective-permute-start | bytes 2752520 | tf_op jit(solution)/shard_map/ppermute | solution.py:302
  186.0 32.3 %collective-permute-start.18 = (bf16[64,7168]{1,0:T(8,128)(2,1)S(1)}, bf16[64,7168]{1,0:T(8,128)(2,1)S(1)}, u32[]{:S(2)}, u32[]{:S(2)}) collective-permute-start(bf16[64,7168]{1,0:T(8,128)(2,1)S(1)} %combine.7), channel_id=1, source_target_pairs={{0,4},{1,5},{2,6},{3,7},{4,8},{5,9},{6,10},{7,11},{8,12},{9,13},{1... | collective-permute-start | bytes 2752520 | tf_op jit(solution)/shard_map/ppermute | solution.py:302
  190.5 9.8 %collective-permute-start.15 = (bf16[1,40,7168]{2,1,0:T(8,128)(2,1)S(1)}, bf16[1,40,7168]{2,1,0:T(8,128)(2,1)S(1)}, u32[]{:S(2)}, u32[]{:S(2)}) collective-permute-start(bf16[1,40,7168]{2,1,0:T(8,128)(2,1)S(1)} %get-tuple-element.38), channel_id=1, source_target_pairs={{0,2},{1,3},{2,0},{3,1},{4,6},{5,7},{6,4},{7,5},{8,10},{9,11},{10,... | collective-permute-start | bytes 1720328 | tf_op jit(solution)/shard_map/ppermute | solution.py:302

commit v2 on v1

--- a/solution.py
+++ b/solution.py
@@ -12,6 +12,7 @@
 LANES = 128
 BLOCK = 128
 MIB = 1024 * 1024
+COST = 1024
 
 
 def params(limit, grid_dims=0):
@@ -251,11 +252,7 @@
             pltpu.VMEM((total, LANES), F32),
         ],
         compiler_params=params(44, 1),
-        cost_estimate=pl.CostEstimate(
-            flops=12 * total * features * half,
-            bytes_accessed=12 * features * half + 4 * total * features,
-            transcendentals=2 * total * half,
-        ),
+        cost_estimate=pl.CostEstimate(flops=COST, bytes_accessed=COST, transcendentals=0),
         name="expert",
     )(at, *inputs, *inputs, own[0], other[0], own[1], other[1], own[2], other[2], *behind)
 
@@ -318,33 +315,37 @@
     capacity = 2 * ((tok_rows * topk * 5 + 8 * experts - 1) // (8 * experts))
     chip = lax.axis_index("ep") // 2
     at = jnp.stack([chip, chip ^ 1]).astype(jnp.int32)
-    own = (w_gate, w_up, w_down)
-    other = tuple(send(w, dc=1) for w in own)
-    weights = (own, other)
-
     block, picked = prepare(at, tokens, routes, gates, experts, capacity)
+    other_gate, other_up = send(w_gate, dc=1), send(w_up, dc=1)
     from_left = send(block, dz=1)
     from_right = send(block, dz=-1)
     picked = send(picked[None], dy=1)
-    mid_left = send(after(from_left, from_right), dz=1)
-    mid_right = send(after(from_right, from_left), dz=-1)
-    (near_picked,) = compact(at, (from_left, from_right), experts, capacity, behind=(picked,))
-    far = send_far(after(block, mid_left, mid_right, near_picked))
+
+    first = (from_left, from_right, picked, other_gate, other_up)
+    from_left, from_right, picked, other_gate, other_up = lax.optimization_barrier(first)
+    other_down = send(after(w_down, *first), dc=1)
+    mid_left = send(from_left, dz=1)
+    mid_right = send(from_right, dz=-1)
+    (near_picked,) = compact(at, (from_left, from_right), experts, capacity)
     near_picked = send(near_picked, dy=1)
+
+    far = send_far(after(block, mid_left, mid_right, near_picked, other_down))
     mid_picked, mid = compact(at, (mid_left, mid_right), experts, capacity, sums=True)
     mid_picked = send(mid_picked, dy=1)
-    own_out, left_out, right_out, own_back, near_back = run_expert(
+    weights = ((w_gate, w_up, w_down), (other_gate, other_up, other_down))
+    block_out, left_out, right_out, back, near_back = run_expert(
         at, (block, from_left, from_right), (picked, near_picked), weights, experts
     )
-    (far_picked,) = compact(at, (far,), experts, capacity)
+
+    (far_picked,) = compact(at, (far,), experts, capacity, behind=(near_back, mid_picked))
     far_picked = send(far_picked, dy=1)
     mid_out, far_out, mid_back, far_back = run_expert(
-        at, (mid, far), (mid_picked, far_picked), weights, experts, behind=(near_back,)
-    )
-    near_back = send(near_back, dy=1)
+        at, (mid, far), (mid_picked, far_picked), weights, experts
+    )
+    near_back = send(after(near_back, far_picked), dy=1)
     mid_back = send(after(mid_back, near_back), dy=1)
     far_back = send(after(far_back, mid_back), dy=1)
-    own_back = send(after(own_back, far_back), dy=1)
+    back = send(after(back, far_back), dy=1)
 
     mid_sum = combine(at, mid, mid_out, mid_back, 0, (), experts)
     to_right = send(mid_sum, dz=1, only=(0, 1))
@@ -355,7 +356,7 @@
     left_sum = combine(at, from_left, left_out, near_back, 0, (to_left,), experts)
     home_left = send(right_sum, dz=1)
     home_right = send(left_sum, dz=-1)
-    return combine(at, block, own_out, own_back, 0, (far_home, home_left, home_right), experts)
+    return combine(at, block, block_out, back, 0, (far_home, home_left, home_right), experts)
 
 
 def partner(shard, axis, stride):

time: 221 us -> 213 us (0.964)
  waiting for transfers between devices: 122 us -> 114 us
    ppermute x2, waiting for transfers between devices: 24.3 us -> 4.24 us  [send_far(): return lax.ppermute(array, 'ep', pairs)]
    ppermute x19, waiting for transfers between devices: 97.9 us -> 110 us  [send(): return lax.ppermute(array, 'ep', pairs)]
  transfers between devices with their start and end apart: 21 -> 21, of which waited for: 13 -> 14; matrix products, arithmetic and copies ran while one was open for 0% -> 0% of each run, Pallas kernels for 26% -> 26%
where the time goes in v2:
time: 213 us
  waiting for transfers between devices  114 us (54%)
  Pallas kernels  60.4 us (28%)
  starting transfers between devices  35.4 us (17%)
  local copies, waits for them, and re-layouts  2.54 us (1%)
    ppermute x19, waiting for transfers between devices, send(): return lax.ppermute(array, 'ep', pairs)  110 us
    pallas_call x2, Pallas kernels, run_expert(): pl.pallas_call(functools.partial(expert_kernel, experts, tuple((a.shape[0...  44.6 us
    ppermute x19, starting transfers between devices, send(): return lax.ppermute(array, 'ep', pairs)  29.2 us
    pallas_call x5, Pallas kernels, combine(): pl.pallas_call(functools.partial(combine_kernel, experts, capacity, index...  7.12 us
    ppermute x2, starting transfers between devices, send_far(): return lax.ppermute(array, 'ep', pairs)  6.22 us
    pallas_call x1, Pallas kernels, prepare(): pl.pallas_call(functools.partial(prepare_kernel, experts, capacity), out_...  4.79 us
  transfers between devices with their start and end apart: 21, of which 14 were waited for; matrix products, arithmetic and copies ran while one was open for 0% of the time, Pallas kernels for 26%

profile of v2, /device:TPU:0, one launch (start us, length us, event | category | flops | bytes accessed | tf_op | source)
XLA Modules:
  0.0 212.6 jit_solution(1330458954541321224)
XLA Ops:
  0.0 0.5 collective-permute-start.3
  0.5 0.1 collective-permute-start.4
  0.5 0.1 pad_add_fusion.at_ref
  0.6 0.0 copy-start
  0.6 1.2 copy-done
  1.8 0.0 copy-start.1
  1.8 0.7 copy-done.1
  2.4 0.0 copy-start.2
  2.5 0.7 copy-done.2
  3.1 4.8 %prepare.1 = (bf16[64,7296]{1,0:T(8,128)(2,1)S(1)}, bf16[40,7296]{1,0:T(8,128)(2,1)S(1)}) custom-call(s32[2]{0:T(128)S(1)} %pad_add_fusion.at_ref, bf16[64,7168]{1,0:T(8,128)(2,1)S(1)} %copy-done, s32[4,64]{1,0:T(4,128)S(1)} %bitcast.5, f32[4,64]{1,0:T(4,128)S(1)} %bitcast.6), custom_call_target="tpu_custom_call" | custom-call | tf_op jit(solution)/shard_map/prepare/pallas_call | solution.py:106
  7.9 1.3 collective-permute-start.1
  9.2 5.6 %collective-permute-start = (bf16[64,7296]{1,0:T(8,128)(2,1)S(1)}, bf16[64,7296]{1,0:T(8,128)(2,1)S(1)}, u32[]{:S(2)}, u32[]{:S(2)}) collective-permute-start(bf16[64,7296]{1,0:T(8,128)(2,1)S(1)} %get-tuple-element.40.refs_0_.refs_5_.block_ref), channel_id=1, source_target_pairs={{0,4},{1,5},{2,6},{3,7},{4,8},{5,9},{6,10},{7,11},{8,12},{9,13},{1... | collective-permute-start | bytes 2801672 | tf_op jit(solution)/shard_map/ppermute | solution.py:299
  14.8 2.0 collective-permute-start.2
  16.9 12.9 %collective-permute-done.2.refs_3_.refs_8_ = bf16[1,40,7296]{2,1,0:T(8,128)(2,1)S(1)} collective-permute-done((bf16[1,40,7296]{2,1,0:T(8,128)(2,1)S(1)}, bf16[1,40,7296]{2,1,0:T(8,128)(2,1)S(1)}, u32[]{:S(2)}, u32[]{:S(2)}) %collective-permute-start.2) | collective-permute-done | bytes 583712 | tf_op jit(solution)/shard_map/ppermute | solution.py:299
  29.7 4.0 %collective-permute-done.1.refs_1_.refs_2_.refs_7_.block_ref = bf16[64,7296]{1,0:T(8,128)(2,1)S(1)} collective-permute-done((bf16[64,7296]{1,0:T(8,128)(2,1)S(1)}, bf16[64,7296]{1,0:T(8,128)(2,1)S(1)}, u32[]{:S(2)}, u32[]{:S(2)}) %collective-permute-start.1) | collective-permute-done | bytes 933920 | tf_op jit(solution)/shard_map/ppermute | solution.py:299
  33.7 1.2 collective-permute-done.refs_0_.refs_1_.refs_6_.block_ref
  34.9 0.0 collective-permute-done.3.refs_11_.refs_9_
  34.9 0.0 collective-permute-done.4.refs_13_.refs_11_
  34.9 0.0 collective-permute-start.6
  34.9 1.5 compact.3
  36.5 1.7 collective-permute-start.5
  38.2 4.4 %collective-permute-start.7 = (bf16[64,7296]{1,0:T(8,128)(2,1)S(1)}, bf16[64,7296]{1,0:T(8,128)(2,1)S(1)}, u32[]{:S(2)}, u32[]{:S(2)}) collective-permute-start(bf16[64,7296]{1,0:T(8,128)(2,1)S(1)} %collective-permute-done.refs_0_.refs_1_.refs_6_.block_ref), channel_id=1, source_target_pairs={{0,4},{1,5},{2,6},{3,7},{4,8},{5,9},{6,10},{7,11},{8,12},{9,13},{1... | collective-permute-start | bytes 2801672 | tf_op jit(solution)/shard_map/ppermute | solution.py:299
  42.6 1.3 collective-permute-start.8
  43.9 19.0 %collective-permute-done.7.refs_0_ = bf16[64,7296]{1,0:T(8,128)(2,1)S(1)} collective-permute-done((bf16[64,7296]{1,0:T(8,128)(2,1)S(1)}, bf16[64,7296]{1,0:T(8,128)(2,1)S(1)}, u32[]{:S(2)}, u32[]{:S(2)}) %collective-permute-start.7) | collective-permute-done | bytes 933920 | tf_op jit(solution)/shard_map/ppermute | solution.py:299
  62.9 4.2 %collective-permute-done.8.refs_1_ = bf16[64,7296]{1,0:T(8,128)(2,1)S(1)} collective-permute-done((bf16[64,7296]{1,0:T(8,128)(2,1)S(1)}, bf16[64,7296]{1,0:T(8,128)(2,1)S(1)}, u32[]{:S(2)}, u32[]{:S(2)}) %collective-permute-start.8) | collective-permute-done | bytes 933920 | tf_op jit(solution)/shard_map/ppermute | solution.py:299
  67.1 0.0 collective-permute-done.5.refs_4_.refs_9_
  67.1 0.0 collective-permute-done.6.refs_15_.refs_13_
  67.1 0.0 copy-start.3
  67.1 4.2 %collective-permute-start.9 = (bf16[64,7296]{1,0:T(8,128)(2,1)S(1)}, bf16[64,7296]{1,0:T(8,128)(2,1)S(1)}, u32[]{:S(2)}, u32[]{:S(2)}) collective-permute-start(bf16[64,7296]{1,0:T(8,128)(2,1)S(1)} %get-tuple-element.40.refs_0_.refs_5_.block_ref), channel_id=1, source_target_pairs={{0,12},{1,13},{2,14},{3,15},{12,0},{13,1},{14,2},{15,3},{16,28},{1... | collective-permute-start | bytes 2801672 | tf_op jit(solution)/shard_map/ppermute | solution.py:304
  71.3 1.2 compact.4
  72.4 1.6 collective-permute-start.10
  74.0 0.0 copy-done.3
  74.0 24.1 %expert.2 = (bf16[64,7168]{1,0:T(8,128)(2,1)S(1)}, bf16[64,7168]{1,0:T(8,128)(2,1)S(1)}, bf16[64,7168]{1,0:T(8,128)(2,1)S(1)}, bf16[1,40,7168]{2,1,0:T(8,128)(2,1)S(1)}, bf16[2,40,7168]{2,1,0:T(8,128)(2,1)S(1)}) custom-call(s32[2]{0:T(128)S(1)} %pad_add_fusion.at_ref, bf16[64,7296]{1,0:T(8,128)(2,1)S(1)} %get-tuple-element.40.refs_0_.refs_5_.block_ref, ...), custom_call_target="tpu_custom_call" | custom-call | flops 1024 | bytes 1024 | tf_op jit(solution)/shard_map/expert/pallas_call | solution.py:236
  98.1 0.0 collective-permute-done.10.refs_2_.refs_6_
  98.1 0.0 collective-permute-done.9.refs_0_.refs_1_.refs_5_.block_ref
  98.1 1.1 compact.5
  99.3 0.6 collective-permute-start.11
  99.8 13.7 %collective-permute-done.11.refs_3_.refs_7_ = bf16[1,40,7296]{2,1,0:T(8,128)(2,1)S(1)} collective-permute-done((bf16[1,40,7296]{2,1,0:T(8,128)(2,1)S(1)}, bf16[1,40,7296]{2,1,0:T(8,128)(2,1)S(1)}, u32[]{:S(2)}, u32[]{:S(2)}) %collective-permute-start.11) | collective-permute-done | bytes 583712 | tf_op jit(solution)/shard_map/ppermute | solution.py:299
  113.6 0.5 collective-permute-start.12
  114.1 20.5 %expert.3 = (bf16[64,7168]{1,0:T(8,128)(2,1)S(1)}, bf16[64,7168]{1,0:T(8,128)(2,1)S(1)}, bf16[1,40,7168]{2,1,0:T(8,128)(2,1)S(1)}, bf16[1,40,7168]{2,1,0:T(8,128)(2,1)S(1)}) custom-call(s32[2]{0:T(128)S(1)} %pad_add_fusion.at_ref, bf16[64,7296]{1,0:T(8,128)(2,1)S(1)} %get-tuple-element.39.refs_0_.refs_4_.block_ref, ...), custom_call_target="tpu_custom_call" | custom-call | flops 1024 | bytes 1024 | tf_op jit(solution)/shard_map/expert/pallas_call | solution.py:236
  134.7 4.3 %collective-permute-done.12.theirs_ref = bf16[2,40,7168]{2,1,0:T(8,128)(2,1)S(1)} collective-permute-done((bf16[2,40,7168]{2,1,0:T(8,128)(2,1)S(1)}, bf16[2,40,7168]{2,1,0:T(8,128)(2,1)S(1)}, u32[]{:S(2)}, u32[]{:S(2)}) %collective-permute-start.12) | collective-permute-done | bytes 1146912 | tf_op jit(solution)/shard_map/ppermute | solution.py:299
  139.0 0.5 collective-permute-start.13
  139.6 11.7 %collective-permute-done.13.theirs_ref = bf16[1,40,7168]{2,1,0:T(8,128)(2,1)S(1)} collective-permute-done((bf16[1,40,7168]{2,1,0:T(8,128)(2,1)S(1)}, bf16[1,40,7168]{2,1,0:T(8,128)(2,1)S(1)}, u32[]{:S(2)}, u32[]{:S(2)}) %collective-permute-start.13) | collective-permute-done | bytes 573472 | tf_op jit(solution)/shard_map/ppermute | solution.py:299
  151.2 1.1 combine.5.refs_0_
  152.4 0.7 collective-permute-start.19
  153.1 1.3 collective-permute-start.17
  154.5 0.6 collective-permute-start.14
  155.1 10.7 %collective-permute-done.14.theirs_ref = bf16[1,40,7168]{2,1,0:T(8,128)(2,1)S(1)} collective-permute-done((bf16[1,40,7168]{2,1,0:T(8,128)(2,1)S(1)}, bf16[1,40,7168]{2,1,0:T(8,128)(2,1)S(1)}, u32[]{:S(2)}, u32[]{:S(2)}) %collective-permute-start.14) | collective-permute-done | bytes 573472 | tf_op jit(solution)/shard_map/ppermute | solution.py:299
  165.8 1.1 combine.6
  167.0 2.1 collective-permute-start.16
  169.0 0.0 collective-permute-done.19.refs_0_
  169.0 1.2 combine.8
  170.3 1.3 collective-permute-start.20
  171.6 3.6 %collective-permute-done.17.refs_0_ = bf16[64,7168]{1,0:T(8,128)(2,1)S(1)} collective-permute-done((bf16[64,7168]{1,0:T(8,128)(2,1)S(1)}, bf16[64,7168]{1,0:T(8,128)(2,1)S(1)}, u32[]{:S(2)}, u32[]{:S(2)}) %collective-permute-start.17) | collective-permute-done | bytes 917536 | tf_op jit(solution)/shard_map/ppermute | solution.py:299
  175.2 1.2 combine.7
  176.4 4.4 %collective-permute-start.18 = (bf16[64,7168]{1,0:T(8,128)(2,1)S(1)}, bf16[64,7168]{1,0:T(8,128)(2,1)S(1)}, u32[]{:S(2)}, u32[]{:S(2)}) collective-permute-start(bf16[64,7168]{1,0:T(8,128)(2,1)S(1)} %combine.7), channel_id=1, source_target_pairs={{0,4},{1,5},{2,6},{3,7},{4,8},{5,9},{6,10},{7,11},{8,12},{9,13},{1... | collective-permute-start | bytes 2752520 | tf_op jit(solution)/shard_map/ppermute | solution.py:299
  180.9 0.6 collective-permute-start.15
  181.5 9.1 %collective-permute-done.15.theirs_ref = bf16[1,40,7168]{2,1,0:T(8,128)(2,1)S(1)} collective-permute-done((bf16[1,40,7168]{2,1,0:T(8,128)(2,1)S(1)}, bf16[1,40,7168]{2,1,0:T(8,128)(2,1)S(1)}, u32[]{:S(2)}, u32[]{:S(2)}) %collective-permute-start.15) | collective-permute-done | bytes 573472 | tf_op jit(solution)/shard_map/ppermute | solution.py:299
  190.7 4.2 %collective-permute-done.16.refs_0_ = bf16[64,7168]{1,0:T(8,128)(2,1)S(1)} collective-permute-done((bf16[64,7168]{1,0:T(8,128)(2,1)S(1)}, bf16[64,7168]{1,0:T(8,128)(2,1)S(1)}, u32[]{:S(2)}, u32[]{:S(2)}) %collective-permute-start.16) | collective-permute-done | bytes 917536 | tf_op jit(solution)/shard_map/ppermute | solution.py:304
  194.9 13.9 %collective-permute-done.20.refs_2_ = bf16[64,7168]{1,0:T(8,128)(2,1)S(1)} collective-permute-done((bf16[64,7168]{1,0:T(8,128)(2,1)S(1)}, bf16[64,7168]{1,0:T(8,128)(2,1)S(1)}, u32[]{:S(2)}, u32[]{:S(2)}) %collective-permute-start.20) | collective-permute-done | bytes 917536 | tf_op jit(solution)/shard_map/ppermute | solution.py:299
  208.8 1.4 collective-permute-done.18.refs_1_
  210.2 2.4 %combine.9 = bf16[64,7168]{1,0:T(8,128)(2,1)} custom-call(s32[2]{0:T(128)S(1)} %pad_add_fusion.at_ref, bf16[64,7296]{1,0:T(8,128)(2,1)S(1)} %get-tuple-element.40.refs_0_.refs_5_.block_ref, bf16[64,7168]{1,0:T(8,128)(2,1)S(1)} %get-tuple-element.37.mine_ref, bf16[1,40,7168]{2,1,0:T(8,128)(2,1)S(1)} %collective-permute-done.15.theirs_ref, ...), custom_call_target="tpu_custom_call" | custom-call | tf_op jit(solution)/shard_map/combine/pallas_call | solution.py:279
Async XLA Ops:
  0.0 34.9 %collective-permute-start.3 = (bf16[1,7168,512]{2,1,0:T(8,128)(2,1)}, bf16[1,7168,512]{2,1,0:T(8,128)(2,1)}, u32[]{:S(2)}, u32[]{:S(2)}) collective-permute-start(bf16[1,7168,512]{2,1,0:T(8,128)(2,1)} %refs_8_.1), channel_id=1, source_target_pairs={{0,1},{1,0},{2,3},{3,2},{4,5},{5,4},{6,7},{7,6},{8,9},{9,8},{10,11... | collective-permute-start | bytes 22020104 | tf_op jit(solution)/shard_map/ppermute | solution.py:299
  0.5 34.5 %collective-permute-start.4 = (bf16[1,7168,512]{2,1,0:T(8,128)(2,1)}, bf16[1,7168,512]{2,1,0:T(8,128)(2,1)}, u32[]{:S(2)}, u32[]{:S(2)}) collective-permute-start(bf16[1,7168,512]{2,1,0:T(8,128)(2,1)} %refs_10_.3), channel_id=1, source_target_pairs={{0,1},{1,0},{2,3},{3,2},{4,5},{5,4},{6,7},{7,6},{8,9},{9,8},{10,11... | collective-permute-start | bytes 22020104 | tf_op jit(solution)/shard_map/ppermute | solution.py:299
  0.6 1.2 copy-start
  1.8 0.7 copy-start.1
  2.4 0.7 copy-start.2
  7.9 25.8 %collective-permute-start.1 = (bf16[64,7296]{1,0:T(8,128)(2,1)S(1)}, bf16[64,7296]{1,0:T(8,128)(2,1)S(1)}, u32[]{:S(2)}, u32[]{:S(2)}) collective-permute-start(bf16[64,7296]{1,0:T(8,128)(2,1)S(1)} %get-tuple-element.40.refs_0_.refs_5_.block_ref), channel_id=1, source_target_pairs={{4,0},{5,1},{6,2},{7,3},{8,4},{9,5},{10,6},{11,7},{12,8},{13,9},{1... | collective-permute-start | bytes 2801672 | tf_op jit(solution)/shard_map/ppermute | solution.py:299
  9.2 25.7 %collective-permute-start = (bf16[64,7296]{1,0:T(8,128)(2,1)S(1)}, bf16[64,7296]{1,0:T(8,128)(2,1)S(1)}, u32[]{:S(2)}, u32[]{:S(2)}) collective-permute-start(bf16[64,7296]{1,0:T(8,128)(2,1)S(1)} %get-tuple-element.40.refs_0_.refs_5_.block_ref), channel_id=1, source_target_pairs={{0,4},{1,5},{2,6},{3,7},{4,8},{5,9},{6,10},{7,11},{8,12},{9,13},{1... | collective-permute-start | bytes 2801672 | tf_op jit(solution)/shard_map/ppermute | solution.py:299
  14.8 14.9 %collective-permute-start.2 = (bf16[1,40,7296]{2,1,0:T(8,128)(2,1)S(1)}, bf16[1,40,7296]{2,1,0:T(8,128)(2,1)S(1)}, u32[]{:S(2)}, u32[]{:S(2)}) collective-permute-start(bf16[1,40,7296]{2,1,0:T(8,128)(2,1)S(1)} %bitcast.7), channel_id=1, source_target_pairs={{0,2},{1,3},{2,0},{3,1},{4,6},{5,7},{6,4},{7,5},{8,10},{9,11},{10,... | collective-permute-start | bytes 1751048 | tf_op jit(solution)/shard_map/ppermute | solution.py:299
  34.9 32.2 %collective-permute-start.6 = (bf16[1,512,7168]{2,1,0:T(8,128)(2,1)}, bf16[1,512,7168]{2,1,0:T(8,128)(2,1)S(1)}, u32[]{:S(2)}, u32[]{:S(2)}) collective-permute-start(bf16[1,512,7168]{2,1,0:T(8,128)(2,1)} %refs_12_.3), channel_id=1, source_target_pairs={{0,1},{1,0},{2,3},{3,2},{4,5},{5,4},{6,7},{7,6},{8,9},{9,8},{10,11... | collective-permute-start | bytes 22020104 | tf_op jit(solution)/shard_map/ppermute | solution.py:299
  36.5 30.6 %collective-permute-start.5 = (bf16[2,40,7296]{2,1,0:T(8,128)(2,1)S(1)}, bf16[2,40,7296]{2,1,0:T(8,128)(2,1)S(1)}, u32[]{:S(2)}, u32[]{:S(2)}) collective-permute-start(bf16[2,40,7296]{2,1,0:T(8,128)(2,1)S(1)} %compact.3), channel_id=1, source_target_pairs={{0,2},{1,3},{2,0},{3,1},{4,6},{5,7},{6,4},{7,5},{8,10},{9,11},{10,... | collective-permute-start | bytes 3502088 | tf_op jit(solution)/shard_map/ppermute | solution.py:299
  38.2 24.7 %collective-permute-start.7 = (bf16[64,7296]{1,0:T(8,128)(2,1)S(1)}, bf16[64,7296]{1,0:T(8,128)(2,1)S(1)}, u32[]{:S(2)}, u32[]{:S(2)}) collective-permute-start(bf16[64,7296]{1,0:T(8,128)(2,1)S(1)} %collective-permute-done.refs_0_.refs_1_.refs_6_.block_ref), channel_id=1, source_target_pairs={{0,4},{1,5},{2,6},{3,7},{4,8},{5,9},{6,10},{7,11},{8,12},{9,13},{1... | collective-permute-start | bytes 2801672 | tf_op jit(solution)/shard_map/ppermute | solution.py:299
  42.6 24.5 %collective-permute-start.8 = (bf16[64,7296]{1,0:T(8,128)(2,1)S(1)}, bf16[64,7296]{1,0:T(8,128)(2,1)S(1)}, u32[]{:S(2)}, u32[]{:S(2)}) collective-permute-start(bf16[64,7296]{1,0:T(8,128)(2,1)S(1)} %collective-permute-done.1.refs_1_.refs_2_.refs_7_.block_ref), channel_id=1, source_target_pairs={{4,0},{5,1},{6,2},{7,3},{8,4},{9,5},{10,6},{11,7},{12,8},{13,9},{1... | collective-permute-start | bytes 2801672 | tf_op jit(solution)/shard_map/ppermute | solution.py:299
  67.1 6.9 %copy-start.3 = (bf16[1,512,7168]{2,1,0:T(8,128)(2,1)}, bf16[1,512,7168]{2,1,0:T(8,128)(2,1)S(1)}, u32[]{:S(2)}) copy-start(bf16[1,512,7168]{2,1,0:T(8,128)(2,1)S(1)} %collective-permute-done.6.refs_15_.refs_13_) | copy-start | bytes 22020100
  67.1 31.0 %collective-permute-start.9 = (bf16[64,7296]{1,0:T(8,128)(2,1)S(1)}, bf16[64,7296]{1,0:T(8,128)(2,1)S(1)}, u32[]{:S(2)}, u32[]{:S(2)}) collective-permute-start(bf16[64,7296]{1,0:T(8,128)(2,1)S(1)} %get-tuple-element.40.refs_0_.refs_5_.block_ref), channel_id=1, source_target_pairs={{0,12},{1,13},{2,14},{3,15},{12,0},{13,1},{14,2},{15,3},{16,28},{1... | collective-permute-start | bytes 2801672 | tf_op jit(solution)/shard_map/ppermute | solution.py:304
  72.4 25.7 %collective-permute-start.10 = (bf16[1,40,7296]{2,1,0:T(8,128)(2,1)S(1)}, bf16[1,40,7296]{2,1,0:T(8,128)(2,1)S(1)}, u32[]{:S(2)}, u32[]{:S(2)}) collective-permute-start(bf16[1,40,7296]{2,1,0:T(8,128)(2,1)S(1)} %get-tuple-element.41), channel_id=1, source_target_pairs={{0,2},{1,3},{2,0},{3,1},{4,6},{5,7},{6,4},{7,5},{8,10},{9,11},{10,... | collective-permute-start | bytes 1751048 | tf_op jit(solution)/shard_map/ppermute | solution.py:299
  99.3 14.3 %collective-permute-start.11 = (bf16[1,40,7296]{2,1,0:T(8,128)(2,1)S(1)}, bf16[1,40,7296]{2,1,0:T(8,128)(2,1)S(1)}, u32[]{:S(2)}, u32[]{:S(2)}) collective-permute-start(bf16[1,40,7296]{2,1,0:T(8,128)(2,1)S(1)} %compact.5), channel_id=1, source_target_pairs={{0,2},{1,3},{2,0},{3,1},{4,6},{5,7},{6,4},{7,5},{8,10},{9,11},{10,... | collective-permute-start | bytes 1751048 | tf_op jit(solution)/shard_map/ppermute | solution.py:299
  113.6 25.4 %collective-permute-start.12 = (bf16[2,40,7168]{2,1,0:T(8,128)(2,1)S(1)}, bf16[2,40,7168]{2,1,0:T(8,128)(2,1)S(1)}, u32[]{:S(2)}, u32[]{:S(2)}) collective-permute-start(bf16[2,40,7168]{2,1,0:T(8,128)(2,1)S(1)} %get-tuple-element.45.refs_1_), channel_id=1, source_target_pairs={{0,2},{1,3},{2,0},{3,1},{4,6},{5,7},{6,4},{7,5},{8,10},{9,11},{10,... | collective-permute-start | bytes 3440648 | tf_op jit(solution)/shard_map/ppermute | solution.py:299
  139.0 12.2 %collective-permute-start.13 = (bf16[1,40,7168]{2,1,0:T(8,128)(2,1)S(1)}, bf16[1,40,7168]{2,1,0:T(8,128)(2,1)S(1)}, u32[]{:S(2)}, u32[]{:S(2)}) collective-permute-start(bf16[1,40,7168]{2,1,0:T(8,128)(2,1)S(1)} %get-tuple-element.46), channel_id=1, source_target_pairs={{0,2},{1,3},{2,0},{3,1},{4,6},{5,7},{6,4},{7,5},{8,10},{9,11},{10,... | collective-permute-start | bytes 1720328 | tf_op jit(solution)/shard_map/ppermute | solution.py:299
  152.4 16.7 %collective-permute-start.19 = (bf16[64,7168]{1,0:T(8,128)(2,1)S(1)}, bf16[64,7168]{1,0:T(8,128)(2,1)S(1)}, u32[]{:S(2)}, u32[]{:S(2)}) collective-permute-start(bf16[64,7168]{1,0:T(8,128)(2,1)S(1)} %combine.5.refs_0_), channel_id=1, source_target_pairs={{8,4},{9,5},{10,6},{11,7},{12,8},{13,9},{14,10},{15,11},{24,20},{2... | collective-permute-start | bytes 2752520 | tf_op jit(solution)/shard_map/ppermute | solution.py:299
  153.1 22.1 %collective-permute-start.17 = (bf16[64,7168]{1,0:T(8,128)(2,1)S(1)}, bf16[64,7168]{1,0:T(8,128)(2,1)S(1)}, u32[]{:S(2)}, u32[]{:S(2)}) collective-permute-start(bf16[64,7168]{1,0:T(8,128)(2,1)S(1)} %combine.5.refs_0_), channel_id=1, source_target_pairs={{0,4},{1,5},{2,6},{3,7},{4,8},{5,9},{6,10},{7,11},{16,20},{17,21},... | collective-permute-start | bytes 2752520 | tf_op jit(solution)/shard_map/ppermute | solution.py:299
  154.5 11.4 %collective-permute-start.14 = (bf16[1,40,7168]{2,1,0:T(8,128)(2,1)S(1)}, bf16[1,40,7168]{2,1,0:T(8,128)(2,1)S(1)}, u32[]{:S(2)}, u32[]{:S(2)}) collective-permute-start(bf16[1,40,7168]{2,1,0:T(8,128)(2,1)S(1)} %get-tuple-element.47), channel_id=1, source_target_pairs={{0,2},{1,3},{2,0},{3,1},{4,6},{5,7},{6,4},{7,5},{8,10},{9,11},{10,... | collective-permute-start | bytes 1720328 | tf_op jit(solution)/shard_map/ppermute | solution.py:299
  167.0 27.9 %collective-permute-start.16 = (bf16[64,7168]{1,0:T(8,128)(2,1)S(1)}, bf16[64,7168]{1,0:T(8,128)(2,1)S(1)}, u32[]{:S(2)}, u32[]{:S(2)}) collective-permute-start(bf16[64,7168]{1,0:T(8,128)(2,1)S(1)} %combine.6), channel_id=1, source_target_pairs={{0,12},{1,13},{2,14},{3,15},{12,0},{13,1},{14,2},{15,3},{16,28},{1... | collective-permute-start | bytes 2752520 | tf_op jit(solution)/shard_map/ppermute | solution.py:304
  170.3 38.5 %collective-permute-start.20 = (bf16[64,7168]{1,0:T(8,128)(2,1)S(1)}, bf16[64,7168]{1,0:T(8,128)(2,1)S(1)}, u32[]{:S(2)}, u32[]{:S(2)}) collective-permute-start(bf16[64,7168]{1,0:T(8,128)(2,1)S(1)} %combine.8), channel_id=1, source_target_pairs={{4,0},{5,1},{6,2},{7,3},{8,4},{9,5},{10,6},{11,7},{12,8},{13,9},{1... | collective-permute-start | bytes 2752520 | tf_op jit(solution)/shard_map/ppermute | solution.py:299
  176.4 33.8 %collective-permute-start.18 = (bf16[64,7168]{1,0:T(8,128)(2,1)S(1)}, bf16[64,7168]{1,0:T(8,128)(2,1)S(1)}, u32[]{:S(2)}, u32[]{:S(2)}) collective-permute-start(bf16[64,7168]{1,0:T(8,128)(2,1)S(1)} %combine.7), channel_id=1, source_target_pairs={{0,4},{1,5},{2,6},{3,7},{4,8},{5,9},{6,10},{7,11},{8,12},{9,13},{1... | collective-permute-start | bytes 2752520 | tf_op jit(solution)/shard_map/ppermute | solution.py:299
  180.9 9.8 %collective-permute-start.15 = (bf16[1,40,7168]{2,1,0:T(8,128)(2,1)S(1)}, bf16[1,40,7168]{2,1,0:T(8,128)(2,1)S(1)}, u32[]{:S(2)}, u32[]{:S(2)}) collective-permute-start(bf16[1,40,7168]{2,1,0:T(8,128)(2,1)S(1)} %get-tuple-element.48), channel_id=1, source_target_pairs={{0,2},{1,3},{2,0},{3,1},{4,6},{5,7},{6,4},{7,5},{8,10},{9,11},{10,... | collective-permute-start | bytes 1720328 | tf_op jit(solution)/shard_map/ppermute | solution.py:299

commit v3 on v2

--- a/solution.py
+++ b/solution.py
@@ -116,42 +116,41 @@
     )(at, tokens, routes.T, gates.T)
 
 
-def compact_kernel(experts, capacity, count, sums, at_ref, *refs):
-    ins, outs = refs[:count], refs[len(refs) - (2 if sums else 1) :]
-    features = ins[0].shape[1] - LANES
+def compact_kernel(experts, capacity, choice, at_ref, first_ref, second_ref, *refs):
+    picked_ref, block_ref = refs[-2:]
+    features = first_ref.shape[1] - LANES
+    use_first = at_ref[choice] == 1
+
+    @pl.when(use_first)
+    def _():
+        block_ref[...] = first_ref[...]
+
+    @pl.when(jnp.logical_not(use_first))
+    def _():
+        block_ref[...] = second_ref[...]
+
+    ext = block_ref[:, features:]
+    onehot = picker(gate_of(ext, at_ref[1], experts), capacity)
+    picked_ref[0, :, features:] = pick_rows(onehot, ext)
     step = 1024
-    for j in range(1 if sums else count):
-
-        def load(columns, j=j):
-            if not sums:
-                return ins[j][:, columns]
-            merged = ins[0][:, columns] + ins[1][:, columns]
-            outs[1][:, columns] = merged
-            return merged
-
-        tail = slice(features, features + LANES)
-        ext = load(tail)
-        onehot = picker(gate_of(ext, at_ref[1], experts), capacity)
-        outs[0][j, :, tail] = pick_rows(onehot, ext)
-        for start in range(0, features, step):
-            columns = slice(start, start + step)
-            outs[0][j, :, columns] = pick_rows(onehot, load(columns))
-
-
-def compact(at, blocks, experts, capacity, sums=False, behind=()):
-    rows, width = blocks[0].shape
-    count = len(blocks)
-    out_shape = [jax.ShapeDtypeStruct((1 if sums else count, capacity, width), BF16)]
-    if sums:
-        out_shape.append(jax.ShapeDtypeStruct((rows, width), BF16))
+    for start in range(0, features, step):
+        columns = slice(start, start + step)
+        picked_ref[0, :, columns] = pick_rows(onehot, block_ref[:, columns])
+
+
+def compact(at, choice, first, second, experts, capacity, behind=()):
+    rows, width = first.shape
     return pl.pallas_call(
-        functools.partial(compact_kernel, experts, capacity, count, sums),
-        out_shape=tuple(out_shape),
-        in_specs=[SMEM] + [VMEM] * count + [ANY] * len(behind),
-        out_specs=(VMEM,) * len(out_shape),
+        functools.partial(compact_kernel, experts, capacity, choice),
+        out_shape=(
+            jax.ShapeDtypeStruct((1, capacity, width), BF16),
+            jax.ShapeDtypeStruct((rows, width), BF16),
+        ),
+        in_specs=[SMEM, VMEM, VMEM] + [ANY] * len(behind),
+        out_specs=(VMEM,) * 2,
         compiler_params=params(12),
         name="compact",
-    )(at, *blocks, *behind)
+    )(at, first, second, *behind)
 
 
 def expert_kernel(experts, full, extra, k_steps, at_ref, *refs):
@@ -286,7 +285,31 @@
     )(at, block, mine, theirs, *adds, *behind)
 
 
+def merge_kernel(choice, at_ref, first_ref, second_ref, more_ref, out_ref):
+    use_first = at_ref[choice] == 1
+
+    @pl.when(use_first)
+    def _():
+        out_ref[...] = (first_ref[...].astype(F32) + more_ref[...].astype(F32)).astype(BF16)
+
+    @pl.when(jnp.logical_not(use_first))
+    def _():
+        out_ref[...] = (second_ref[...].astype(F32) + more_ref[...].astype(F32)).astype(BF16)
+
+
+def merge(at, choice, first, second, more):
+    return pl.pallas_call(
+        functools.partial(merge_kernel, choice),
+        out_shape=jax.ShapeDtypeStruct(more.shape, BF16),
+        in_specs=[SMEM] + [VMEM] * 3,
+        out_specs=VMEM,
+        compiler_params=params(14),
+        name="merge",
+    )(at, first, second, more)
+
+
 DEPTH = 4
+FIRST, LOWER, END = 2, 3, 4
 
 
 def send(array, dz=0, dy=0, dc=0, only=None):
@@ -314,7 +337,9 @@
     experts = lax.axis_size("ep") // 2
     capacity = 2 * ((tok_rows * topk * 5 + 8 * experts - 1) // (8 * experts))
     chip = lax.axis_index("ep") // 2
-    at = jnp.stack([chip, chip ^ 1]).astype(jnp.int32)
+    place = chip // 2
+    end = (place == 0) | (place == DEPTH - 1)
+    at = jnp.stack([chip, chip ^ 1, place == 0, place < DEPTH // 2, end]).astype(jnp.int32)
     block, picked = prepare(at, tokens, routes, gates, experts, capacity)
     other_gate, other_up = send(w_gate, dc=1), send(w_up, dc=1)
     from_left = send(block, dz=1)
@@ -326,36 +351,37 @@
     other_down = send(after(w_down, *first), dc=1)
     mid_left = send(from_left, dz=1)
     mid_right = send(from_right, dz=-1)
-    (near_picked,) = compact(at, (from_left, from_right), experts, capacity)
+    near_picked, near = compact(at, FIRST, from_right, from_left, experts, capacity)
     near_picked = send(near_picked, dy=1)
 
     far = send_far(after(block, mid_left, mid_right, near_picked, other_down))
-    mid_picked, mid = compact(at, (mid_left, mid_right), experts, capacity, sums=True)
+    mid_picked, mid = compact(at, LOWER, mid_right, mid_left, experts, capacity)
     mid_picked = send(mid_picked, dy=1)
     weights = ((w_gate, w_up, w_down), (other_gate, other_up, other_down))
-    block_out, left_out, right_out, back, near_back = run_expert(
-        at, (block, from_left, from_right), (picked, near_picked), weights, experts
-    )
-
-    (far_picked,) = compact(at, (far,), experts, capacity, behind=(near_back, mid_picked))
-    far_picked = send(far_picked, dy=1)
-    mid_out, far_out, mid_back, far_back = run_expert(
-        at, (mid, far), (mid_picked, far_picked), weights, experts
-    )
-    near_back = send(after(near_back, far_picked), dy=1)
+    block_out, near_out, back, near_back = run_expert(
+        at, (block, near), (picked, near_picked), weights, experts
+    )
+
+    last_picked, last = compact(
+        at, END, far, from_right, experts, capacity, behind=(near_back, mid_picked)
+    )
+    last_picked = send(last_picked, dy=1)
+    mid_out, last_out, mid_back, last_back = run_expert(
+        at, (mid, last), (mid_picked, last_picked), weights, experts
+    )
+    near_back = send(after(near_back, last_picked), dy=1)
     mid_back = send(after(mid_back, near_back), dy=1)
-    far_back = send(after(far_back, mid_back), dy=1)
-    back = send(after(back, far_back), dy=1)
-
+    last_back = send(after(last_back, mid_back), dy=1)
+    back = send(after(back, last_back), dy=1)
+
+    near_sum = combine(at, near, near_out, near_back, 0, (), experts)
     mid_sum = combine(at, mid, mid_out, mid_back, 0, (), experts)
     to_right = send(mid_sum, dz=1, only=(0, 1))
     to_left = send(mid_sum, dz=-1, only=(3, 2))
-    far_sum = combine(at, far, far_out, far_back, 0, (), experts, behind=(mid_sum,))
-    far_home = send_far(far_sum)
-    right_sum = combine(at, from_right, right_out, near_back, 1, (to_right,), experts)
-    left_sum = combine(at, from_left, left_out, near_back, 0, (to_left,), experts)
-    home_left = send(right_sum, dz=1)
-    home_right = send(left_sum, dz=-1)
+    last_sum = combine(at, last, last_out, last_back, 0, (), experts, behind=(mid_sum,))
+    far_home = send_far(last_sum)
+    home_left = send(merge(at, FIRST, near_sum, last_sum, to_right), dz=1)
+    home_right = send(merge(at, FIRST, near_sum, near_sum, to_left), dz=-1)
     return combine(at, block, block_out, back, 0, (far_home, home_left, home_right), experts)
 
 

time: 213 us -> 204 us (0.958)
  waiting for transfers between devices: 114 us -> 90.4 us
  starting transfers between devices: 35.4 us -> 53.6 us
  Pallas kernels: 60.4 us -> 56.8 us
    ppermute x19, waiting for transfers between devices: 110 us -> 90.4 us  [send(): return lax.ppermute(array, 'ep', pairs)]
    ppermute x19, starting transfers between devices: 29.2 us -> 43.5 us  [send(): return lax.ppermute(array, 'ep', pairs)]
    ppermute x2, waiting for transfers between devices: 4.24 us -> 0.01 us  [send_far(): return lax.ppermute(array, 'ep', pairs)]
    ppermute x2, starting transfers between devices: 6.22 us -> 10.1 us  [send_far(): return lax.ppermute(array, 'ep', pairs)]
    pallas_call x2, Pallas kernels: 44.6 us -> 41.1 us  [run_expert(): pl.pallas_call(functools.partial(expert_kernel, experts, tuple((a.shape[0...]
    pallas_call x5 -> x4, Pallas kernels: 7.12 us -> 5.76 us  [combine(): pl.pallas_call(functools.partial(combine_kernel, experts, capacity, index...]
    pallas_call x3 -> x5, Pallas kernels: 3.83 us -> 5.15 us  [the longest x3 3.64 us: compact(): pl.pallas_call(functools.partial(compact_kernel, experts, capacity, choic...]
  transfers between devices with their start and end apart: 21 -> 21, of which waited for: 14 -> 13; matrix products, arithmetic and copies ran while one was open for 0% -> 0% of each run, Pallas kernels for 26% -> 26%
where the time goes in v3:
time: 204 us
  waiting for transfers between devices  90.4 us (44%)
  Pallas kernels  56.8 us (28%)
  starting transfers between devices  53.6 us (26%)
  local copies, waits for them, and re-layouts  2.63 us (1%)
    ppermute x19, waiting for transfers between devices, send(): return lax.ppermute(array, 'ep', pairs)  90.4 us
    ppermute x19, starting transfers between devices, send(): return lax.ppermute(array, 'ep', pairs)  43.5 us
    pallas_call x2, Pallas kernels, run_expert(): pl.pallas_call(functools.partial(expert_kernel, experts, tuple((a.shape[0...  41.1 us
    ppermute x2, starting transfers between devices, send_far(): return lax.ppermute(array, 'ep', pairs)  10.1 us
    pallas_call x4, Pallas kernels, combine(): pl.pallas_call(functools.partial(combine_kernel, experts, capacity, index...  5.76 us
    pallas_call x1, Pallas kernels, prepare(): pl.pallas_call(functools.partial(prepare_kernel, experts, capacity), out_...  4.79 us
  transfers between devices with their start and end apart: 21, of which 13 were waited for; matrix products, arithmetic and copies ran while one was open for 0% of the time, Pallas kernels for 26%

profile of v3, /device:TPU:0, one launch (start us, length us, event | category | flops | bytes accessed | tf_op | source)
XLA Modules:
  0.0 203.6 jit_solution(14503315829666117154)
XLA Ops:
  0.0 0.5 collective-permute-start.3
  0.5 0.1 collective-permute-start.4
  0.5 0.1 stack.35.at_ref
  0.6 0.0 copy-start
  0.6 1.2 copy-done
  1.8 0.0 copy-start.1
  1.8 0.7 copy-done.1
  2.5 0.0 copy-start.2
  2.5 0.7 copy-done.2
  3.1 4.8 %prepare.1 = (bf16[64,7296]{1,0:T(8,128)(2,1)S(1)}, bf16[40,7296]{1,0:T(8,128)(2,1)S(1)}) custom-call(s32[5]{0:T(128)S(1)} %stack.35.at_ref, bf16[64,7168]{1,0:T(8,128)(2,1)S(1)} %copy-done, s32[4,64]{1,0:T(4,128)S(1)} %bitcast.8, f32[4,64]{1,0:T(4,128)S(1)} %bitcast.9), custom_call_target="tpu_custom_call" | custom-call | tf_op jit(solution)/shard_map/prepare/pallas_call | solution.py:106
  7.9 5.0 %collective-permute-start = (bf16[64,7296]{1,0:T(8,128)(2,1)S(1)}, bf16[64,7296]{1,0:T(8,128)(2,1)S(1)}, u32[]{:S(2)}, u32[]{:S(2)}) collective-permute-start(bf16[64,7296]{1,0:T(8,128)(2,1)S(1)} %get-tuple-element.45.refs_0_.refs_4_.block_ref), channel_id=1, source_target_pairs={{0,4},{1,5},{2,6},{3,7},{4,8},{5,9},{6,10},{7,11},{8,12},{9,13},{1... | collective-permute-start | bytes 2801672 | tf_op jit(solution)/shard_map/ppermute | solution.py:322
  12.9 1.3 collective-permute-start.1
  14.2 1.6 collective-permute-start.2
  15.8 13.3 %collective-permute-done.2.refs_2_.refs_6_ = bf16[1,40,7296]{2,1,0:T(8,128)(2,1)S(1)} collective-permute-done((bf16[1,40,7296]{2,1,0:T(8,128)(2,1)S(1)}, bf16[1,40,7296]{2,1,0:T(8,128)(2,1)S(1)}, u32[]{:S(2)}, u32[]{:S(2)}) %collective-permute-start.2) | collective-permute-done | bytes 583712 | tf_op jit(solution)/shard_map/ppermute | solution.py:322
  29.1 3.9 %collective-permute-done.second_ref = bf16[64,7296]{1,0:T(8,128)(2,1)S(1)} collective-permute-done((bf16[64,7296]{1,0:T(8,128)(2,1)S(1)}, bf16[64,7296]{1,0:T(8,128)(2,1)S(1)}, u32[]{:S(2)}, u32[]{:S(2)}) %collective-permute-start) | collective-permute-done | bytes 933920 | tf_op jit(solution)/shard_map/ppermute | solution.py:322
  33.0 4.2 %collective-permute-done.1.first_ref.second_ref = bf16[64,7296]{1,0:T(8,128)(2,1)S(1)} collective-permute-done((bf16[64,7296]{1,0:T(8,128)(2,1)S(1)}, bf16[64,7296]{1,0:T(8,128)(2,1)S(1)}, u32[]{:S(2)}, u32[]{:S(2)}) %collective-permute-start.1) | collective-permute-done | bytes 933920 | tf_op jit(solution)/shard_map/ppermute | solution.py:322
  37.2 0.0 collective-permute-done.3.refs_9_
  37.2 0.0 collective-permute-done.4.refs_11_
  37.2 0.0 collective-permute-start.6
  37.2 1.3 collective-permute-start.7
  38.5 4.6 %collective-permute-start.8 = (bf16[64,7296]{1,0:T(8,128)(2,1)S(1)}, bf16[64,7296]{1,0:T(8,128)(2,1)S(1)}, u32[]{:S(2)}, u32[]{:S(2)}) collective-permute-start(bf16[64,7296]{1,0:T(8,128)(2,1)S(1)} %collective-permute-done.second_ref), channel_id=1, source_target_pairs={{0,4},{1,5},{2,6},{3,7},{4,8},{5,9},{6,10},{7,11},{8,12},{9,13},{1... | collective-permute-start | bytes 2801672 | tf_op jit(solution)/shard_map/ppermute | solution.py:322
  43.1 1.2 compact.3
  44.3 1.6 collective-permute-start.5
  45.9 13.5 %collective-permute-done.5.refs_3_.refs_7_ = bf16[1,40,7296]{2,1,0:T(8,128)(2,1)S(1)} collective-permute-done((bf16[1,40,7296]{2,1,0:T(8,128)(2,1)S(1)}, bf16[1,40,7296]{2,1,0:T(8,128)(2,1)S(1)}, u32[]{:S(2)}, u32[]{:S(2)}) %collective-permute-start.5) | collective-permute-done | bytes 583712 | tf_op jit(solution)/shard_map/ppermute | solution.py:322
  59.4 2.8 %collective-permute-done.7.first_ref = bf16[64,7296]{1,0:T(8,128)(2,1)S(1)} collective-permute-done((bf16[64,7296]{1,0:T(8,128)(2,1)S(1)}, bf16[64,7296]{1,0:T(8,128)(2,1)S(1)}, u32[]{:S(2)}, u32[]{:S(2)}) %collective-permute-start.7) | collective-permute-done | bytes 933920 | tf_op jit(solution)/shard_map/ppermute | solution.py:322
  62.2 1.2 collective-permute-done.8.second_ref
  63.3 0.0 collective-permute-done.6.refs_13_
  63.3 0.0 copy-start.3
  63.3 6.4 %collective-permute-start.9 = (bf16[64,7296]{1,0:T(8,128)(2,1)S(1)}, bf16[64,7296]{1,0:T(8,128)(2,1)S(1)}, u32[]{:S(2)}, u32[]{:S(2)}) collective-permute-start(bf16[64,7296]{1,0:T(8,128)(2,1)S(1)} %get-tuple-element.45.refs_0_.refs_4_.block_ref), channel_id=1, source_target_pairs={{0,12},{1,13},{2,14},{3,15},{12,0},{13,1},{14,2},{15,3},{16,28},{1... | collective-permute-start | bytes 2801672 | tf_op jit(solution)/shard_map/ppermute | solution.py:327
  69.8 1.2 compact.4
  71.0 1.6 collective-permute-start.10
  72.6 0.0 copy-done.3
  72.6 20.6 %expert.2 = (bf16[64,7168]{1,0:T(8,128)(2,1)S(1)}, bf16[64,7168]{1,0:T(8,128)(2,1)S(1)}, bf16[1,40,7168]{2,1,0:T(8,128)(2,1)S(1)}, bf16[1,40,7168]{2,1,0:T(8,128)(2,1)S(1)}) custom-call(s32[5]{0:T(128)S(1)} %stack.35.at_ref, bf16[64,7296]{1,0:T(8,128)(2,1)S(1)} %get-tuple-element.45.refs_0_.refs_4_.block_ref, ...), custom_call_target="tpu_custom_call" | custom-call | flops 1024 | bytes 1024 | tf_op jit(solution)/shard_map/expert/pallas_call | solution.py:235
  93.1 0.0 collective-permute-done.10.refs_1_.refs_2_.refs_6_
  93.1 0.0 collective-permute-done.9.first_ref
  93.2 1.2 compact.5
  94.4 0.6 collective-permute-start.11
  94.9 13.4 %collective-permute-done.11.refs_3_.refs_7_ = bf16[1,40,7296]{2,1,0:T(8,128)(2,1)S(1)} collective-permute-done((bf16[1,40,7296]{2,1,0:T(8,128)(2,1)S(1)}, bf16[1,40,7296]{2,1,0:T(8,128)(2,1)S(1)}, u32[]{:S(2)}, u32[]{:S(2)}) %collective-permute-start.11) | collective-permute-done | bytes 583712 | tf_op jit(solution)/shard_map/ppermute | solution.py:322
  108.4 0.5 collective-permute-start.12
  108.9 20.6 %expert.3 = (bf16[64,7168]{1,0:T(8,128)(2,1)S(1)}, bf16[64,7168]{1,0:T(8,128)(2,1)S(1)}, bf16[1,40,7168]{2,1,0:T(8,128)(2,1)S(1)}, bf16[1,40,7168]{2,1,0:T(8,128)(2,1)S(1)}) custom-call(s32[5]{0:T(128)S(1)} %stack.35.at_ref, bf16[64,7296]{1,0:T(8,128)(2,1)S(1)} %get-tuple-element.44.refs_0_.refs_4_.block_ref, ...), custom_call_target="tpu_custom_call" | custom-call | flops 1024 | bytes 1024 | tf_op jit(solution)/shard_map/expert/pallas_call | solution.py:235
  129.4 0.0 collective-permute-done.12.theirs_ref
  129.4 1.6 collective-permute-start.13
  131.0 11.0 %collective-permute-done.13.theirs_ref = bf16[1,40,7168]{2,1,0:T(8,128)(2,1)S(1)} collective-permute-done((bf16[1,40,7168]{2,1,0:T(8,128)(2,1)S(1)}, bf16[1,40,7168]{2,1,0:T(8,128)(2,1)S(1)}, u32[]{:S(2)}, u32[]{:S(2)}) %collective-permute-start.13) | collective-permute-done | bytes 573472 | tf_op jit(solution)/shard_map/ppermute | solution.py:322
  142.0 1.1 combine.4.refs_0_
  143.1 0.7 collective-permute-start.19
  143.9 1.3 collective-permute-start.17
  145.2 1.6 collective-permute-start.14
  146.8 1.1 combine.6.first_ref.second_ref
  147.9 8.9 %collective-permute-done.14.theirs_ref = bf16[1,40,7168]{2,1,0:T(8,128)(2,1)S(1)} collective-permute-done((bf16[1,40,7168]{2,1,0:T(8,128)(2,1)S(1)}, bf16[1,40,7168]{2,1,0:T(8,128)(2,1)S(1)}, u32[]{:S(2)}, u32[]{:S(2)}) %collective-permute-start.14) | collective-permute-done | bytes 573472 | tf_op jit(solution)/shard_map/ppermute | solution.py:322
  156.9 1.1 combine.5.second_ref
  158.0 3.7 %collective-permute-start.16 = (bf16[64,7168]{1,0:T(8,128)(2,1)S(1)}, bf16[64,7168]{1,0:T(8,128)(2,1)S(1)}, u32[]{:S(2)}, u32[]{:S(2)}) collective-permute-start(bf16[64,7168]{1,0:T(8,128)(2,1)S(1)} %combine.5.second_ref), channel_id=1, source_target_pairs={{0,12},{1,13},{2,14},{3,15},{12,0},{13,1},{14,2},{15,3},{16,28},{1... | collective-permute-start | bytes 2752520 | tf_op jit(solution)/shard_map/ppermute | solution.py:327
  161.7 0.0 collective-permute-done.19.more_ref
  161.7 0.8 merge.3
  162.5 1.3 collective-permute-start.20
  163.8 2.0 collective-permute-done.17.more_ref
  165.8 0.8 merge.2
  166.6 18.3 %collective-permute-start.18 = (bf16[64,7168]{1,0:T(8,128)(2,1)S(1)}, bf16[64,7168]{1,0:T(8,128)(2,1)S(1)}, u32[]{:S(2)}, u32[]{:S(2)}) collective-permute-start(bf16[64,7168]{1,0:T(8,128)(2,1)S(1)} %merge.2), channel_id=1, source_target_pairs={{0,4},{1,5},{2,6},{3,7},{4,8},{5,9},{6,10},{7,11},{8,12},{9,13},{1... | collective-permute-start | bytes 2752520 | tf_op jit(solution)/shard_map/ppermute | solution.py:322
  184.9 0.1 collective-permute-start.15
  185.0 9.7 %collective-permute-done.15.theirs_ref = bf16[1,40,7168]{2,1,0:T(8,128)(2,1)S(1)} collective-permute-done((bf16[1,40,7168]{2,1,0:T(8,128)(2,1)S(1)}, bf16[1,40,7168]{2,1,0:T(8,128)(2,1)S(1)}, u32[]{:S(2)}, u32[]{:S(2)}) %collective-permute-start.15) | collective-permute-done | bytes 573472 | tf_op jit(solution)/shard_map/ppermute | solution.py:322
  194.7 0.0 collective-permute-done.16.refs_0_
  194.7 6.1 %collective-permute-done.20.refs_2_ = bf16[64,7168]{1,0:T(8,128)(2,1)S(1)} collective-permute-done((bf16[64,7168]{1,0:T(8,128)(2,1)S(1)}, bf16[64,7168]{1,0:T(8,128)(2,1)S(1)}, u32[]{:S(2)}, u32[]{:S(2)}) %collective-permute-start.20) | collective-permute-done | bytes 917536 | tf_op jit(solution)/shard_map/ppermute | solution.py:322
  200.8 0.5 collective-permute-done.18.refs_1_
  201.3 2.4 %combine.7 = bf16[64,7168]{1,0:T(8,128)(2,1)} custom-call(s32[5]{0:T(128)S(1)} %stack.35.at_ref, bf16[64,7296]{1,0:T(8,128)(2,1)S(1)} %get-tuple-element.45.refs_0_.refs_4_.block_ref, bf16[64,7168]{1,0:T(8,128)(2,1)S(1)} %get-tuple-element.42.mine_ref, bf16[1,40,7168]{2,1,0:T(8,128)(2,1)S(1)} %collective-permute-done.15.theirs_ref, ...), custom_call_target="tpu_custom_call" | custom-call | tf_op jit(solution)/shard_map/combine/pallas_call | solution.py:278
Async XLA Ops:
  0.0 37.2 %collective-permute-start.3 = (bf16[1,7168,512]{2,1,0:T(8,128)(2,1)}, bf16[1,7168,512]{2,1,0:T(8,128)(2,1)}, u32[]{:S(2)}, u32[]{:S(2)}) collective-permute-start(bf16[1,7168,512]{2,1,0:T(8,128)(2,1)} %refs_8_.3), channel_id=1, source_target_pairs={{0,1},{1,0},{2,3},{3,2},{4,5},{5,4},{6,7},{7,6},{8,9},{9,8},{10,11... | collective-permute-start | bytes 22020104 | tf_op jit(solution)/shard_map/ppermute | solution.py:322
  0.5 36.7 %collective-permute-start.4 = (bf16[1,7168,512]{2,1,0:T(8,128)(2,1)}, bf16[1,7168,512]{2,1,0:T(8,128)(2,1)}, u32[]{:S(2)}, u32[]{:S(2)}) collective-permute-start(bf16[1,7168,512]{2,1,0:T(8,128)(2,1)} %refs_10_.3), channel_id=1, source_target_pairs={{0,1},{1,0},{2,3},{3,2},{4,5},{5,4},{6,7},{7,6},{8,9},{9,8},{10,11... | collective-permute-start | bytes 22020104 | tf_op jit(solution)/shard_map/ppermute | solution.py:322
  0.6 1.2 copy-start
  1.8 0.7 copy-start.1
  2.5 0.7 copy-start.2
  7.9 25.0 %collective-permute-start = (bf16[64,7296]{1,0:T(8,128)(2,1)S(1)}, bf16[64,7296]{1,0:T(8,128)(2,1)S(1)}, u32[]{:S(2)}, u32[]{:S(2)}) collective-permute-start(bf16[64,7296]{1,0:T(8,128)(2,1)S(1)} %get-tuple-element.45.refs_0_.refs_4_.block_ref), channel_id=1, source_target_pairs={{0,4},{1,5},{2,6},{3,7},{4,8},{5,9},{6,10},{7,11},{8,12},{9,13},{1... | collective-permute-start | bytes 2801672 | tf_op jit(solution)/shard_map/ppermute | solution.py:322
  12.9 24.2 %collective-permute-start.1 = (bf16[64,7296]{1,0:T(8,128)(2,1)S(1)}, bf16[64,7296]{1,0:T(8,128)(2,1)S(1)}, u32[]{:S(2)}, u32[]{:S(2)}) collective-permute-start(bf16[64,7296]{1,0:T(8,128)(2,1)S(1)} %get-tuple-element.45.refs_0_.refs_4_.block_ref), channel_id=1, source_target_pairs={{4,0},{5,1},{6,2},{7,3},{8,4},{9,5},{10,6},{11,7},{12,8},{13,9},{1... | collective-permute-start | bytes 2801672 | tf_op jit(solution)/shard_map/ppermute | solution.py:322
  14.2 14.9 %collective-permute-start.2 = (bf16[1,40,7296]{2,1,0:T(8,128)(2,1)S(1)}, bf16[1,40,7296]{2,1,0:T(8,128)(2,1)S(1)}, u32[]{:S(2)}, u32[]{:S(2)}) collective-permute-start(bf16[1,40,7296]{2,1,0:T(8,128)(2,1)S(1)} %bitcast.10), channel_id=1, source_target_pairs={{0,2},{1,3},{2,0},{3,1},{4,6},{5,7},{6,4},{7,5},{8,10},{9,11},{10,... | collective-permute-start | bytes 1751048 | tf_op jit(solution)/shard_map/ppermute | solution.py:322
  37.2 26.2 %collective-permute-start.6 = (bf16[1,512,7168]{2,1,0:T(8,128)(2,1)}, bf16[1,512,7168]{2,1,0:T(8,128)(2,1)S(1)}, u32[]{:S(2)}, u32[]{:S(2)}) collective-permute-start(bf16[1,512,7168]{2,1,0:T(8,128)(2,1)} %refs_12_.3), channel_id=1, source_target_pairs={{0,1},{1,0},{2,3},{3,2},{4,5},{5,4},{6,7},{7,6},{8,9},{9,8},{10,11... | collective-permute-start | bytes 22020104 | tf_op jit(solution)/shard_map/ppermute | solution.py:322
  37.2 25.0 %collective-permute-start.7 = (bf16[64,7296]{1,0:T(8,128)(2,1)S(1)}, bf16[64,7296]{1,0:T(8,128)(2,1)S(1)}, u32[]{:S(2)}, u32[]{:S(2)}) collective-permute-start(bf16[64,7296]{1,0:T(8,128)(2,1)S(1)} %collective-permute-done.1.first_ref.second_ref), channel_id=1, source_target_pairs={{4,0},{5,1},{6,2},{7,3},{8,4},{9,5},{10,6},{11,7},{12,8},{13,9},{1... | collective-permute-start | bytes 2801672 | tf_op jit(solution)/shard_map/ppermute | solution.py:322
  38.5 24.9 %collective-permute-start.8 = (bf16[64,7296]{1,0:T(8,128)(2,1)S(1)}, bf16[64,7296]{1,0:T(8,128)(2,1)S(1)}, u32[]{:S(2)}, u32[]{:S(2)}) collective-permute-start(bf16[64,7296]{1,0:T(8,128)(2,1)S(1)} %collective-permute-done.second_ref), channel_id=1, source_target_pairs={{0,4},{1,5},{2,6},{3,7},{4,8},{5,9},{6,10},{7,11},{8,12},{9,13},{1... | collective-permute-start | bytes 2801672 | tf_op jit(solution)/shard_map/ppermute | solution.py:322
  44.3 15.1 %collective-permute-start.5 = (bf16[1,40,7296]{2,1,0:T(8,128)(2,1)S(1)}, bf16[1,40,7296]{2,1,0:T(8,128)(2,1)S(1)}, u32[]{:S(2)}, u32[]{:S(2)}) collective-permute-start(bf16[1,40,7296]{2,1,0:T(8,128)(2,1)S(1)} %get-tuple-element.38), channel_id=1, source_target_pairs={{0,2},{1,3},{2,0},{3,1},{4,6},{5,7},{6,4},{7,5},{8,10},{9,11},{10,... | collective-permute-start | bytes 1751048 | tf_op jit(solution)/shard_map/ppermute | solution.py:322
  63.3 9.2 %copy-start.3 = (bf16[1,512,7168]{2,1,0:T(8,128)(2,1)}, bf16[1,512,7168]{2,1,0:T(8,128)(2,1)S(1)}, u32[]{:S(2)}) copy-start(bf16[1,512,7168]{2,1,0:T(8,128)(2,1)S(1)} %collective-permute-done.6.refs_13_) | copy-start | bytes 22020100
  63.3 29.8 %collective-permute-start.9 = (bf16[64,7296]{1,0:T(8,128)(2,1)S(1)}, bf16[64,7296]{1,0:T(8,128)(2,1)S(1)}, u32[]{:S(2)}, u32[]{:S(2)}) collective-permute-start(bf16[64,7296]{1,0:T(8,128)(2,1)S(1)} %get-tuple-element.45.refs_0_.refs_4_.block_ref), channel_id=1, source_target_pairs={{0,12},{1,13},{2,14},{3,15},{12,0},{13,1},{14,2},{15,3},{16,28},{1... | collective-permute-start | bytes 2801672 | tf_op jit(solution)/shard_map/ppermute | solution.py:327
  71.0 22.2 %collective-permute-start.10 = (bf16[1,40,7296]{2,1,0:T(8,128)(2,1)S(1)}, bf16[1,40,7296]{2,1,0:T(8,128)(2,1)S(1)}, u32[]{:S(2)}, u32[]{:S(2)}) collective-permute-start(bf16[1,40,7296]{2,1,0:T(8,128)(2,1)S(1)} %get-tuple-element.47), channel_id=1, source_target_pairs={{0,2},{1,3},{2,0},{3,1},{4,6},{5,7},{6,4},{7,5},{8,10},{9,11},{10,... | collective-permute-start | bytes 1751048 | tf_op jit(solution)/shard_map/ppermute | solution.py:322
  94.4 14.0 %collective-permute-start.11 = (bf16[1,40,7296]{2,1,0:T(8,128)(2,1)S(1)}, bf16[1,40,7296]{2,1,0:T(8,128)(2,1)S(1)}, u32[]{:S(2)}, u32[]{:S(2)}) collective-permute-start(bf16[1,40,7296]{2,1,0:T(8,128)(2,1)S(1)} %get-tuple-element.49), channel_id=1, source_target_pairs={{0,2},{1,3},{2,0},{3,1},{4,6},{5,7},{6,4},{7,5},{8,10},{9,11},{10,... | collective-permute-start | bytes 1751048 | tf_op jit(solution)/shard_map/ppermute | solution.py:322
  108.4 21.1 %collective-permute-start.12 = (bf16[1,40,7168]{2,1,0:T(8,128)(2,1)S(1)}, bf16[1,40,7168]{2,1,0:T(8,128)(2,1)S(1)}, u32[]{:S(2)}, u32[]{:S(2)}) collective-permute-start(bf16[1,40,7168]{2,1,0:T(8,128)(2,1)S(1)} %get-tuple-element.52.refs_0_), channel_id=1, source_target_pairs={{0,2},{1,3},{2,0},{3,1},{4,6},{5,7},{6,4},{7,5},{8,10},{9,11},{10,... | collective-permute-start | bytes 1720328 | tf_op jit(solution)/shard_map/ppermute | solution.py:322
  129.4 12.6 %collective-permute-start.13 = (bf16[1,40,7168]{2,1,0:T(8,128)(2,1)S(1)}, bf16[1,40,7168]{2,1,0:T(8,128)(2,1)S(1)}, u32[]{:S(2)}, u32[]{:S(2)}) collective-permute-start(bf16[1,40,7168]{2,1,0:T(8,128)(2,1)S(1)} %get-tuple-element.53), channel_id=1, source_target_pairs={{0,2},{1,3},{2,0},{3,1},{4,6},{5,7},{6,4},{7,5},{8,10},{9,11},{10,... | collective-permute-start | bytes 1720328 | tf_op jit(solution)/shard_map/ppermute | solution.py:322
  143.1 18.6 %collective-permute-start.19 = (bf16[64,7168]{1,0:T(8,128)(2,1)S(1)}, bf16[64,7168]{1,0:T(8,128)(2,1)S(1)}, u32[]{:S(2)}, u32[]{:S(2)}) collective-permute-start(bf16[64,7168]{1,0:T(8,128)(2,1)S(1)} %combine.4.refs_0_), channel_id=1, source_target_pairs={{8,4},{9,5},{10,6},{11,7},{12,8},{13,9},{14,10},{15,11},{24,20},{2... | collective-permute-start | bytes 2752520 | tf_op jit(solution)/shard_map/ppermute | solution.py:322
  143.9 21.9 %collective-permute-start.17 = (bf16[64,7168]{1,0:T(8,128)(2,1)S(1)}, bf16[64,7168]{1,0:T(8,128)(2,1)S(1)}, u32[]{:S(2)}, u32[]{:S(2)}) collective-permute-start(bf16[64,7168]{1,0:T(8,128)(2,1)S(1)} %combine.4.refs_0_), channel_id=1, source_target_pairs={{0,4},{1,5},{2,6},{3,7},{4,8},{5,9},{6,10},{7,11},{16,20},{17,21},... | collective-permute-start | bytes 2752520 | tf_op jit(solution)/shard_map/ppermute | solution.py:322
  145.2 11.6 %collective-permute-start.14 = (bf16[1,40,7168]{2,1,0:T(8,128)(2,1)S(1)}, bf16[1,40,7168]{2,1,0:T(8,128)(2,1)S(1)}, u32[]{:S(2)}, u32[]{:S(2)}) collective-permute-start(bf16[1,40,7168]{2,1,0:T(8,128)(2,1)S(1)} %get-tuple-element.54), channel_id=1, source_target_pairs={{0,2},{1,3},{2,0},{3,1},{4,6},{5,7},{6,4},{7,5},{8,10},{9,11},{10,... | collective-permute-start | bytes 1720328 | tf_op jit(solution)/shard_map/ppermute | solution.py:322
  158.0 36.7 %collective-permute-start.16 = (bf16[64,7168]{1,0:T(8,128)(2,1)S(1)}, bf16[64,7168]{1,0:T(8,128)(2,1)S(1)}, u32[]{:S(2)}, u32[]{:S(2)}) collective-permute-start(bf16[64,7168]{1,0:T(8,128)(2,1)S(1)} %combine.5.second_ref), channel_id=1, source_target_pairs={{0,12},{1,13},{2,14},{3,15},{12,0},{13,1},{14,2},{15,3},{16,28},{1... | collective-permute-start | bytes 2752520 | tf_op jit(solution)/shard_map/ppermute | solution.py:327
  162.5 38.3 %collective-permute-start.20 = (bf16[64,7168]{1,0:T(8,128)(2,1)S(1)}, bf16[64,7168]{1,0:T(8,128)(2,1)S(1)}, u32[]{:S(2)}, u32[]{:S(2)}) collective-permute-start(bf16[64,7168]{1,0:T(8,128)(2,1)S(1)} %merge.3), channel_id=1, source_target_pairs={{4,0},{5,1},{6,2},{7,3},{8,4},{9,5},{10,6},{11,7},{12,8},{13,9},{1... | collective-permute-start | bytes 2752520 | tf_op jit(solution)/shard_map/ppermute | solution.py:322
  166.6 34.7 %collective-permute-start.18 = (bf16[64,7168]{1,0:T(8,128)(2,1)S(1)}, bf16[64,7168]{1,0:T(8,128)(2,1)S(1)}, u32[]{:S(2)}, u32[]{:S(2)}) collective-permute-start(bf16[64,7168]{1,0:T(8,128)(2,1)S(1)} %merge.2), channel_id=1, source_target_pairs={{0,4},{1,5},{2,6},{3,7},{4,8},{5,9},{6,10},{7,11},{8,12},{9,13},{1... | collective-permute-start | bytes 2752520 | tf_op jit(solution)/shard_map/ppermute | solution.py:322
  184.9 9.8 %collective-permute-start.15 = (bf16[1,40,7168]{2,1,0:T(8,128)(2,1)S(1)}, bf16[1,40,7168]{2,1,0:T(8,128)(2,1)S(1)}, u32[]{:S(2)}, u32[]{:S(2)}) collective-permute-start(bf16[1,40,7168]{2,1,0:T(8,128)(2,1)S(1)} %get-tuple-element.55), channel_id=1, source_target_pairs={{0,2},{1,3},{2,0},{3,1},{4,6},{5,7},{6,4},{7,5},{8,10},{9,11},{10,... | collective-permute-start | bytes 1720328 | tf_op jit(solution)/shard_map/ppermute | solution.py:322

commit v4 on v3

--- a/solution.py
+++ b/solution.py
@@ -250,7 +250,7 @@
             pltpu.VMEM((total, 2 * half), BF16),
             pltpu.VMEM((total, LANES), F32),
         ],
-        compiler_params=params(44, 1),
+        compiler_params=params(34, 1),
         cost_estimate=pl.CostEstimate(flops=COST, bytes_accessed=COST, transcendentals=0),
         name="expert",
     )(at, *inputs, *inputs, own[0], other[0], own[1], other[1], own[2], other[2], *behind)
@@ -341,33 +341,33 @@
     end = (place == 0) | (place == DEPTH - 1)
     at = jnp.stack([chip, chip ^ 1, place == 0, place < DEPTH // 2, end]).astype(jnp.int32)
     block, picked = prepare(at, tokens, routes, gates, experts, capacity)
-    other_gate, other_up = send(w_gate, dc=1), send(w_up, dc=1)
+    other = tuple(send(w, dc=1) for w in (w_gate, w_up, w_down))
     from_left = send(block, dz=1)
     from_right = send(block, dz=-1)
-    picked = send(picked[None], dy=1)
-
-    first = (from_left, from_right, picked, other_gate, other_up)
-    from_left, from_right, picked, other_gate, other_up = lax.optimization_barrier(first)
-    other_down = send(after(w_down, *first), dc=1)
+
+    first = (from_left, from_right, picked) + other
+    from_left, from_right, picked, *other = lax.optimization_barrier(first)
+    weights = ((w_gate, w_up, w_down), other)
     mid_left = send(from_left, dz=1)
     mid_right = send(from_right, dz=-1)
     near_picked, near = compact(at, FIRST, from_right, from_left, experts, capacity)
     near_picked = send(near_picked, dy=1)
-
-    far = send_far(after(block, mid_left, mid_right, near_picked, other_down))
-    mid_picked, mid = compact(at, LOWER, mid_right, mid_left, experts, capacity)
+    picked = send(picked[None], dy=1)
+    block_out, near_out = run_expert(at, (block, near), (), weights, experts)
+
+    far = send_far(after(block, mid_left, mid_right, block_out, near_picked))
+    mid_picked, mid = compact(
+        at, LOWER, mid_right, mid_left, experts, capacity, behind=(picked,)
+    )
     mid_picked = send(mid_picked, dy=1)
-    weights = ((w_gate, w_up, w_down), (other_gate, other_up, other_down))
-    block_out, near_out, back, near_back = run_expert(
-        at, (block, near), (picked, near_picked), weights, experts
-    )
+    mid_out, back, near_back = run_expert(at, (mid,), (picked, near_picked), weights, experts)
 
     last_picked, last = compact(
         at, END, far, from_right, experts, capacity, behind=(near_back, mid_picked)
     )
     last_picked = send(last_picked, dy=1)
-    mid_out, last_out, mid_back, last_back = run_expert(
-        at, (mid, last), (mid_picked, last_picked), weights, experts
+    last_out, mid_back, last_back = run_expert(
+        at, (last,), (mid_picked, last_picked), weights, experts
     )
     near_back = send(after(near_back, last_picked), dy=1)
     mid_back = send(after(mid_back, near_back), dy=1)

time: 204 us -> 200 us (0.980)
  waiting for transfers between devices: 90.4 us -> 69 us
  Pallas kernels: 56.8 us -> 69.1 us
  local copies, waits for them, and re-layouts: 2.63 us -> 5.73 us
    ppermute x19, waiting for transfers between devices: 90.4 us -> 68.9 us  [send(): return lax.ppermute(array, 'ep', pairs)]
    pallas_call x2 -> x3, Pallas kernels: 41.1 us -> 51.7 us  [run_expert(): pl.pallas_call(functools.partial(expert_kernel, experts, tuple((a.shape[0...]
    ppermute x19, starting transfers between devices: 43.5 us -> 47.7 us  [send(): return lax.ppermute(array, 'ep', pairs)]
    unnamed x8 -> x18, local copies, waits for them, and re-layouts: 2.54 us -> 5.65 us
    ppermute x2, starting transfers between devices: 10.1 us -> 7.12 us  [send_far(): return lax.ppermute(array, 'ep', pairs)]
  transfers between devices with their start and end apart: 21 -> 21, of which waited for: 13 -> 11; matrix products, arithmetic and copies ran while one was open for 0% -> 0% of each run, Pallas kernels for 26% -> 32%
where the time goes in v4:
time: 200 us; the launch traced here: 199 us
  Pallas kernels  69.1 us (35%)
  waiting for transfers between devices  69 us (34%)
  starting transfers between devices  54.8 us (27%)
  local copies, waits for them, and re-layouts  5.73 us (3%)
    ppermute x19, waiting for transfers between devices, send(): return lax.ppermute(array, 'ep', pairs)  68.9 us
    pallas_call x3, Pallas kernels, run_expert(): pl.pallas_call(functools.partial(expert_kernel, experts, tuple((a.shape[0...  51.7 us
    ppermute x19, starting transfers between devices, send(): return lax.ppermute(array, 'ep', pairs)  47.7 us
    ppermute x2, starting transfers between devices, send_far(): return lax.ppermute(array, 'ep', pairs)  7.12 us
    pallas_call x4, Pallas kernels, combine(): pl.pallas_call(functools.partial(combine_kernel, experts, capacity, index...  5.81 us
    unnamed x18, local copies, waits for them, and re-layouts  5.65 us
    pallas_call x1, Pallas kernels, prepare(): pl.pallas_call(functools.partial(prepare_kernel, experts, capacity), out_...  5.63 us
    pallas_call x3, Pallas kernels, compact(): pl.pallas_call(functools.partial(compact_kernel, experts, capacity, choic...  4.45 us
  transfers between devices with their start and end apart: 21, of which 11 were waited for; matrix products, arithmetic and copies ran while one was open for 0% of the time, Pallas kernels for 32%

profile of v4, /device:TPU:0, one launch (start us, length us, event | category | flops | bytes accessed | tf_op | source)
XLA Modules:
  0.0 198.8 jit_solution(10354789186039461398)
XLA Ops:
  0.0 0.5 collective-permute-start.2
  0.5 0.1 collective-permute-start.3
  0.5 0.5 collective-permute-start.4
  1.0 0.1 stack.35.at_ref
  1.1 1.2 copy-done.4
  2.2 0.7 copy-done.7
  2.9 0.7 copy-done.8
  3.6 5.6 %prepare.1 = (bf16[64,7296]{1,0:T(8,128)(2,1)S(1)}, bf16[40,7296]{1,0:T(8,128)(2,1)}) custom-call(s32[5]{0:T(128)S(1)} %stack.35.at_ref, bf16[64,7168]{1,0:T(8,128)(2,1)S(1)} %copy-done.4, s32[4,64]{1,0:T(4,128)S(1)} %bitcast.8, f32[4,64]{1,0:T(4,128)S(1)} %bitcast.9), custom_call_target="tpu_custom_call" | custom-call | tf_op jit(solution)/shard_map/prepare/pallas_call | solution.py:106
  9.2 4.5 %collective-permute-start = (bf16[64,7296]{1,0:T(8,128)(2,1)S(1)}, bf16[64,7296]{1,0:T(8,128)(2,1)S(1)}, u32[]{:S(2)}, u32[]{:S(2)}) collective-permute-start(bf16[64,7296]{1,0:T(8,128)(2,1)S(1)} %get-tuple-element.45.refs_0_.refs_2_.block_ref), channel_id=1, source_target_pairs={{0,4},{1,5},{2,6},{3,7},{4,8},{5,9},{6,10},{7,11},{8,12},{9,13},{1... | collective-permute-start | bytes 2801672 | tf_op jit(solution)/shard_map/ppermute | solution.py:322
  13.8 1.3 collective-permute-start.1
  15.1 19.3 %collective-permute-done.second_ref = bf16[64,7296]{1,0:T(8,128)(2,1)S(1)} collective-permute-done((bf16[64,7296]{1,0:T(8,128)(2,1)S(1)}, bf16[64,7296]{1,0:T(8,128)(2,1)S(1)}, u32[]{:S(2)}, u32[]{:S(2)}) %collective-permute-start) | collective-permute-done | bytes 933920 | tf_op jit(solution)/shard_map/ppermute | solution.py:322
  34.3 4.2 %collective-permute-done.1.first_ref.second_ref = bf16[64,7296]{1,0:T(8,128)(2,1)S(1)} collective-permute-done((bf16[64,7296]{1,0:T(8,128)(2,1)S(1)}, bf16[64,7296]{1,0:T(8,128)(2,1)S(1)}, u32[]{:S(2)}, u32[]{:S(2)}) %collective-permute-start.1) | collective-permute-done | bytes 933920 | tf_op jit(solution)/shard_map/ppermute | solution.py:322
  38.5 0.0 collective-permute-done.2.refs_5_.refs_7_
  38.5 0.0 collective-permute-done.3.refs_7_.refs_9_
  38.5 0.0 collective-permute-done.4.refs_9_.refs_11_
  38.5 1.3 collective-permute-start.5
  39.8 4.6 %collective-permute-start.6 = (bf16[64,7296]{1,0:T(8,128)(2,1)S(1)}, bf16[64,7296]{1,0:T(8,128)(2,1)S(1)}, u32[]{:S(2)}, u32[]{:S(2)}) collective-permute-start(bf16[64,7296]{1,0:T(8,128)(2,1)S(1)} %collective-permute-done.second_ref), channel_id=1, source_target_pairs={{0,4},{1,5},{2,6},{3,7},{4,8},{5,9},{6,10},{7,11},{8,12},{9,13},{1... | collective-permute-start | bytes 2801672 | tf_op jit(solution)/shard_map/ppermute | solution.py:322
  44.4 2.0 %compact.3 = (bf16[1,40,7296]{2,1,0:T(8,128)(2,1)}, bf16[64,7296]{1,0:T(8,128)(2,1)S(1)}) custom-call(s32[5]{0:T(128)S(1)} %stack.35.at_ref, bf16[64,7296]{1,0:T(8,128)(2,1)S(1)} %collective-permute-done.1.first_ref.second_ref, bf16[64,7296]{1,0:T(8,128)(2,1)S(1)} %collective-permute-done.second_ref), custom_call_target="tpu_custom_call" | custom-call | tf_op jit(solution)/shard_map/compact/pallas_call | solution.py:143
  46.4 1.5 collective-permute-start.8
  48.0 0.5 collective-permute-start.7
  48.5 3.1 %copy-done = bf16[1,7168,512]{2,1,0:T(8,128)(2,1)S(1)} copy-done((bf16[1,7168,512]{2,1,0:T(8,128)(2,1)S(1)}, bf16[1,7168,512]{2,1,0:T(8,128)(2,1)}, u32[]{:S(2)}) %copy-start) | copy-done | bytes 7340056
  51.6 17.1 %expert.3 = (bf16[64,7168]{1,0:T(8,128)(2,1)S(1)}, bf16[64,7168]{1,0:T(8,128)(2,1)S(1)}) custom-call(s32[5]{0:T(128)S(1)} %stack.35.at_ref, bf16[64,7296]{1,0:T(8,128)(2,1)S(1)} %get-tuple-element.45.refs_0_.refs_2_.block_ref, bf16[64,7296]{1,0:T(8,128)(2,1)S(1)} %get-tuple-element.36.refs_1_.refs_3_.block_ref, ...), custom_call_target="tpu_custom_call" | custom-call | flops 1024 | bytes 1024 | tf_op jit(solution)/shard_map/expert/pallas_call | solution.py:235
  68.6 0.0 copy-start.2
  68.7 0.0 copy-start.5
  68.7 0.0 collective-permute-done.8.refs_2_.refs_5_
  68.7 0.0 collective-permute-done.5.first_ref
  68.7 0.0 collective-permute-done.6.second_ref
  68.7 3.3 %collective-permute-start.9 = (bf16[64,7296]{1,0:T(8,128)(2,1)S(1)}, bf16[64,7296]{1,0:T(8,128)(2,1)S(1)}, u32[]{:S(2)}, u32[]{:S(2)}) collective-permute-start(bf16[64,7296]{1,0:T(8,128)(2,1)S(1)} %get-tuple-element.45.refs_0_.refs_2_.block_ref), channel_id=1, source_target_pairs={{0,12},{1,13},{2,14},{3,15},{12,0},{13,1},{14,2},{15,3},{16,28},{1... | collective-permute-start | bytes 2801672 | tf_op jit(solution)/shard_map/ppermute | solution.py:327
  72.0 1.1 collective-permute-done.7.refs_0_.refs_1_.refs_4_
  73.1 1.2 compact.4
  74.3 1.6 collective-permute-start.10
  75.9 0.0 copy-done.1
  75.9 17.3 %expert.4 = (bf16[64,7168]{1,0:T(8,128)(2,1)S(1)}, bf16[1,40,7168]{2,1,0:T(8,128)(2,1)S(1)}, bf16[1,40,7168]{2,1,0:T(8,128)(2,1)S(1)}) custom-call(s32[5]{0:T(128)S(1)} %stack.35.at_ref, bf16[64,7296]{1,0:T(8,128)(2,1)S(1)} %get-tuple-element.42.refs_0_.refs_3_.block_ref, bf16[1,40,7296]{2,1,0:T(8,128)(2,1)S(1)} %collective-permute-done.7.refs_0_.refs_1_.refs_4_, ...), custom_call_target="tpu_custom_call" | custom-call | flops 1024 | bytes 1024 | tf_op jit(solution)/shard_map/expert/pallas_call | solution.py:235
  93.2 0.0 collective-permute-done.10.refs_1_.refs_4_
  93.2 0.1 collective-permute-done.9.first_ref
  93.3 1.2 compact.5
  94.5 1.6 collective-permute-start.11
  96.1 11.8 %collective-permute-done.11.refs_2_.refs_5_ = bf16[1,40,7296]{2,1,0:T(8,128)(2,1)S(1)} collective-permute-done((bf16[1,40,7296]{2,1,0:T(8,128)(2,1)S(1)}, bf16[1,40,7296]{2,1,0:T(8,128)(2,1)S(1)}, u32[]{:S(2)}, u32[]{:S(2)}) %collective-permute-start.11) | collective-permute-done | bytes 583712 | tf_op jit(solution)/shard_map/ppermute | solution.py:322
  107.9 1.5 collective-permute-start.12
  109.5 17.4 %expert.5 = (bf16[64,7168]{1,0:T(8,128)(2,1)S(1)}, bf16[1,40,7168]{2,1,0:T(8,128)(2,1)S(1)}, bf16[1,40,7168]{2,1,0:T(8,128)(2,1)S(1)}) custom-call(s32[5]{0:T(128)S(1)} %stack.35.at_ref, bf16[64,7296]{1,0:T(8,128)(2,1)S(1)} %get-tuple-element.48.refs_0_.refs_3_.block_ref, bf16[1,40,7296]{2,1,0:T(8,128)(2,1)S(1)} %collective-permute-done.10.refs_1_.refs_4_, ...), custom_call_target="tpu_custom_call" | custom-call | flops 1024 | bytes 1024 | tf_op jit(solution)/shard_map/expert/pallas_call | solution.py:235
  126.8 0.0 collective-permute-done.12.theirs_ref
  126.8 0.6 collective-permute-start.13
  127.4 9.7 %collective-permute-done.13.theirs_ref = bf16[1,40,7168]{2,1,0:T(8,128)(2,1)S(1)} collective-permute-done((bf16[1,40,7168]{2,1,0:T(8,128)(2,1)S(1)}, bf16[1,40,7168]{2,1,0:T(8,128)(2,1)S(1)}, u32[]{:S(2)}, u32[]{:S(2)}) %collective-permute-start.13) | collective-permute-done | bytes 573472 | tf_op jit(solution)/shard_map/ppermute | solution.py:322
  137.1 1.1 combine.4.refs_0_
  138.2 0.7 collective-permute-start.19
  138.9 3.5 %collective-permute-start.17 = (bf16[64,7168]{1,0:T(8,128)(2,1)S(1)}, bf16[64,7168]{1,0:T(8,128)(2,1)S(1)}, u32[]{:S(2)}, u32[]{:S(2)}) collective-permute-start(bf16[64,7168]{1,0:T(8,128)(2,1)S(1)} %combine.4.refs_0_), channel_id=1, source_target_pairs={{0,4},{1,5},{2,6},{3,7},{4,8},{5,9},{6,10},{7,11},{16,20},{17,21},... | collective-permute-start | bytes 2752520 | tf_op jit(solution)/shard_map/ppermute | solution.py:322
  142.4 1.5 collective-permute-start.14
  143.9 0.0 copy-done.6
  143.9 1.1 combine.6.first_ref.second_ref
  145.0 7.1 %collective-permute-done.14.theirs_ref = bf16[1,40,7168]{2,1,0:T(8,128)(2,1)S(1)} collective-permute-done((bf16[1,40,7168]{2,1,0:T(8,128)(2,1)S(1)}, bf16[1,40,7168]{2,1,0:T(8,128)(2,1)S(1)}, u32[]{:S(2)}, u32[]{:S(2)}) %collective-permute-start.14) | collective-permute-done | bytes 573472 | tf_op jit(solution)/shard_map/ppermute | solution.py:322
  152.2 1.1 combine.5.second_ref
  153.3 3.8 %collective-permute-start.16 = (bf16[64,7168]{1,0:T(8,128)(2,1)S(1)}, bf16[64,7168]{1,0:T(8,128)(2,1)S(1)}, u32[]{:S(2)}, u32[]{:S(2)}) collective-permute-start(bf16[64,7168]{1,0:T(8,128)(2,1)S(1)} %combine.5.second_ref), channel_id=1, source_target_pairs={{0,12},{1,13},{2,14},{3,15},{12,0},{13,1},{14,2},{15,3},{16,28},{1... | collective-permute-start | bytes 2752520 | tf_op jit(solution)/shard_map/ppermute | solution.py:327
  157.2 0.0 collective-permute-done.19.more_ref
  157.2 0.8 merge.3
  157.9 1.3 collective-permute-start.20
  159.2 3.9 %collective-permute-done.17.more_ref = bf16[64,7168]{1,0:T(8,128)(2,1)S(1)} collective-permute-done((bf16[64,7168]{1,0:T(8,128)(2,1)S(1)}, bf16[64,7168]{1,0:T(8,128)(2,1)S(1)}, u32[]{:S(2)}, u32[]{:S(2)}) %collective-permute-start.17) | collective-permute-done | bytes 917536 | tf_op jit(solution)/shard_map/ppermute | solution.py:322
  163.1 0.8 merge.2
  163.9 19.0 %collective-permute-start.18 = (bf16[64,7168]{1,0:T(8,128)(2,1)S(1)}, bf16[64,7168]{1,0:T(8,128)(2,1)S(1)}, u32[]{:S(2)}, u32[]{:S(2)}) collective-permute-start(bf16[64,7168]{1,0:T(8,128)(2,1)S(1)} %merge.2), channel_id=1, source_target_pairs={{0,4},{1,5},{2,6},{3,7},{4,8},{5,9},{6,10},{7,11},{8,12},{9,13},{1... | collective-permute-start | bytes 2752520 | tf_op jit(solution)/shard_map/ppermute | solution.py:322
  182.9 1.8 collective-permute-start.15
  184.6 8.0 %collective-permute-done.15.theirs_ref = bf16[1,40,7168]{2,1,0:T(8,128)(2,1)S(1)} collective-permute-done((bf16[1,40,7168]{2,1,0:T(8,128)(2,1)S(1)}, bf16[1,40,7168]{2,1,0:T(8,128)(2,1)S(1)}, u32[]{:S(2)}, u32[]{:S(2)}) %collective-permute-start.15) | collective-permute-done | bytes 573472 | tf_op jit(solution)/shard_map/ppermute | solution.py:322
  192.7 0.0 collective-permute-done.16.refs_0_
  192.7 1.1 collective-permute-done.20.refs_2_
  193.8 2.6 %collective-permute-done.18.refs_1_ = bf16[64,7168]{1,0:T(8,128)(2,1)S(1)} collective-permute-done((bf16[64,7168]{1,0:T(8,128)(2,1)S(1)}, bf16[64,7168]{1,0:T(8,128)(2,1)S(1)}, u32[]{:S(2)}, u32[]{:S(2)}) %collective-permute-start.18) | collective-permute-done | bytes 917536 | tf_op jit(solution)/shard_map/ppermute | solution.py:322
  196.4 2.4 %combine.7 = bf16[64,7168]{1,0:T(8,128)(2,1)} custom-call(s32[5]{0:T(128)S(1)} %stack.35.at_ref, bf16[64,7296]{1,0:T(8,128)(2,1)S(1)} %get-tuple-element.45.refs_0_.refs_2_.block_ref, bf16[64,7168]{1,0:T(8,128)(2,1)S(1)} %copy-done.3, bf16[1,40,7168]{2,1,0:T(8,128)(2,1)S(1)} %collective-permute-done.15.theirs_ref, ...), custom_call_target="tpu_custom_call" | custom-call | tf_op jit(solution)/shard_map/combine/pallas_call | solution.py:278
  (10 shorter events, 0.0 us)
Async XLA Ops:
  0.0 38.5 %collective-permute-start.2 = (bf16[1,7168,512]{2,1,0:T(8,128)(2,1)}, bf16[1,7168,512]{2,1,0:T(8,128)(2,1)}, u32[]{:S(2)}, u32[]{:S(2)}) collective-permute-start(bf16[1,7168,512]{2,1,0:T(8,128)(2,1)} %refs_6_.5), channel_id=1, source_target_pairs={{0,1},{1,0},{2,3},{3,2},{4,5},{5,4},{6,7},{7,6},{8,9},{9,8},{10,11... | collective-permute-start | bytes 22020104 | tf_op jit(solution)/shard_map/ppermute | solution.py:322
  0.5 38.0 %collective-permute-start.3 = (bf16[1,7168,512]{2,1,0:T(8,128)(2,1)}, bf16[1,7168,512]{2,1,0:T(8,128)(2,1)}, u32[]{:S(2)}, u32[]{:S(2)}) collective-permute-start(bf16[1,7168,512]{2,1,0:T(8,128)(2,1)} %refs_8_.5), channel_id=1, source_target_pairs={{0,1},{1,0},{2,3},{3,2},{4,5},{5,4},{6,7},{7,6},{8,9},{9,8},{10,11... | collective-permute-start | bytes 22020104 | tf_op jit(solution)/shard_map/ppermute | solution.py:322
  0.5 38.0 %collective-permute-start.4 = (bf16[1,512,7168]{2,1,0:T(8,128)(2,1)}, bf16[1,512,7168]{2,1,0:T(8,128)(2,1)}, u32[]{:S(2)}, u32[]{:S(2)}) collective-permute-start(bf16[1,512,7168]{2,1,0:T(8,128)(2,1)} %refs_10_.3), channel_id=1, source_target_pairs={{0,1},{1,0},{2,3},{3,2},{4,5},{5,4},{6,7},{7,6},{8,9},{9,8},{10,11... | collective-permute-start | bytes 22020104 | tf_op jit(solution)/shard_map/ppermute | solution.py:322
  1.0 1.2 copy-start.4
  2.2 0.7 copy-start.7
  2.9 0.7 copy-start.8
  9.2 25.1 %collective-permute-start = (bf16[64,7296]{1,0:T(8,128)(2,1)S(1)}, bf16[64,7296]{1,0:T(8,128)(2,1)S(1)}, u32[]{:S(2)}, u32[]{:S(2)}) collective-permute-start(bf16[64,7296]{1,0:T(8,128)(2,1)S(1)} %get-tuple-element.45.refs_0_.refs_2_.block_ref), channel_id=1, source_target_pairs={{0,4},{1,5},{2,6},{3,7},{4,8},{5,9},{6,10},{7,11},{8,12},{9,13},{1... | collective-permute-start | bytes 2801672 | tf_op jit(solution)/shard_map/ppermute | solution.py:322
  13.8 24.7 %collective-permute-start.1 = (bf16[64,7296]{1,0:T(8,128)(2,1)S(1)}, bf16[64,7296]{1,0:T(8,128)(2,1)S(1)}, u32[]{:S(2)}, u32[]{:S(2)}) collective-permute-start(bf16[64,7296]{1,0:T(8,128)(2,1)S(1)} %get-tuple-element.45.refs_0_.refs_2_.block_ref), channel_id=1, source_target_pairs={{4,0},{5,1},{6,2},{7,3},{8,4},{9,5},{10,6},{11,7},{12,8},{13,9},{1... | collective-permute-start | bytes 2801672 | tf_op jit(solution)/shard_map/ppermute | solution.py:322
  38.5 30.2 %collective-permute-start.5 = (bf16[64,7296]{1,0:T(8,128)(2,1)S(1)}, bf16[64,7296]{1,0:T(8,128)(2,1)S(1)}, u32[]{:S(2)}, u32[]{:S(2)}) collective-permute-start(bf16[64,7296]{1,0:T(8,128)(2,1)S(1)} %collective-permute-done.1.first_ref.second_ref), channel_id=1, source_target_pairs={{4,0},{5,1},{6,2},{7,3},{8,4},{9,5},{10,6},{11,7},{12,8},{13,9},{1... | collective-permute-start | bytes 2801672 | tf_op jit(solution)/shard_map/ppermute | solution.py:322
  39.8 28.9 %collective-permute-start.6 = (bf16[64,7296]{1,0:T(8,128)(2,1)S(1)}, bf16[64,7296]{1,0:T(8,128)(2,1)S(1)}, u32[]{:S(2)}, u32[]{:S(2)}) collective-permute-start(bf16[64,7296]{1,0:T(8,128)(2,1)S(1)} %collective-permute-done.second_ref), channel_id=1, source_target_pairs={{0,4},{1,5},{2,6},{3,7},{4,8},{5,9},{6,10},{7,11},{8,12},{9,13},{1... | collective-permute-start | bytes 2801672 | tf_op jit(solution)/shard_map/ppermute | solution.py:322
  46.4 22.2 %collective-permute-start.8 = (bf16[1,40,7296]{2,1,0:T(8,128)(2,1)}, bf16[1,40,7296]{2,1,0:T(8,128)(2,1)S(1)}, u32[]{:S(2)}, u32[]{:S(2)}) collective-permute-start(bf16[1,40,7296]{2,1,0:T(8,128)(2,1)} %get-tuple-element.43), channel_id=1, source_target_pairs={{0,2},{1,3},{2,0},{3,1},{4,6},{5,7},{6,4},{7,5},{8,10},{9,11},{10,... | collective-permute-start | bytes 1751048 | tf_op jit(solution)/shard_map/ppermute | solution.py:322
  48.0 25.1 %collective-permute-start.7 = (bf16[1,40,7296]{2,1,0:T(8,128)(2,1)}, bf16[1,40,7296]{2,1,0:T(8,128)(2,1)S(1)}, u32[]{:S(2)}, u32[]{:S(2)}) collective-permute-start(bf16[1,40,7296]{2,1,0:T(8,128)(2,1)} %bitcast.7), channel_id=1, source_target_pairs={{0,2},{1,3},{2,0},{3,1},{4,6},{5,7},{6,4},{7,5},{8,10},{9,11},{10,... | collective-permute-start | bytes 1751048 | tf_op jit(solution)/shard_map/ppermute | solution.py:322
  48.5 3.1 %copy-start = (bf16[1,7168,512]{2,1,0:T(8,128)(2,1)S(1)}, bf16[1,7168,512]{2,1,0:T(8,128)(2,1)}, u32[]{:S(2)}) copy-start(bf16[1,7168,512]{2,1,0:T(8,128)(2,1)} %refs_6_.5) | copy-start | bytes 22020100
  51.6 24.4 %copy-start.1 = (bf16[1,7168,512]{2,1,0:T(8,128)(2,1)S(1)}, bf16[1,7168,512]{2,1,0:T(8,128)(2,1)}, u32[]{:S(2)}) copy-start(bf16[1,7168,512]{2,1,0:T(8,128)(2,1)} %refs_6_.5) | copy-start | bytes 22020100
  68.6 5.7 %copy-start.2 = (bf16[64,7168]{1,0:T(8,128)(2,1)}, bf16[64,7168]{1,0:T(8,128)(2,1)S(1)}, u32[]{:S(2)}) copy-start(bf16[64,7168]{1,0:T(8,128)(2,1)S(1)} %get-tuple-element.40.mine_ref) | copy-start | bytes 2752516
  68.7 5.7 %copy-start.5 = (bf16[64,7168]{1,0:T(8,128)(2,1)}, bf16[64,7168]{1,0:T(8,128)(2,1)S(1)}, u32[]{:S(2)}) copy-start(bf16[64,7168]{1,0:T(8,128)(2,1)S(1)} %get-tuple-element.58.mine_ref) | copy-start | bytes 2752516
  68.7 24.6 %collective-permute-start.9 = (bf16[64,7296]{1,0:T(8,128)(2,1)S(1)}, bf16[64,7296]{1,0:T(8,128)(2,1)S(1)}, u32[]{:S(2)}, u32[]{:S(2)}) collective-permute-start(bf16[64,7296]{1,0:T(8,128)(2,1)S(1)} %get-tuple-element.45.refs_0_.refs_2_.block_ref), channel_id=1, source_target_pairs={{0,12},{1,13},{2,14},{3,15},{12,0},{13,1},{14,2},{15,3},{16,28},{1... | collective-permute-start | bytes 2801672 | tf_op jit(solution)/shard_map/ppermute | solution.py:327
  74.3 18.9 %collective-permute-start.10 = (bf16[1,40,7296]{2,1,0:T(8,128)(2,1)S(1)}, bf16[1,40,7296]{2,1,0:T(8,128)(2,1)S(1)}, u32[]{:S(2)}, u32[]{:S(2)}) collective-permute-start(bf16[1,40,7296]{2,1,0:T(8,128)(2,1)S(1)} %get-tuple-element.47), channel_id=1, source_target_pairs={{0,2},{1,3},{2,0},{3,1},{4,6},{5,7},{6,4},{7,5},{8,10},{9,11},{10,... | collective-permute-start | bytes 1751048 | tf_op jit(solution)/shard_map/ppermute | solution.py:322
  94.5 13.4 %collective-permute-start.11 = (bf16[1,40,7296]{2,1,0:T(8,128)(2,1)S(1)}, bf16[1,40,7296]{2,1,0:T(8,128)(2,1)S(1)}, u32[]{:S(2)}, u32[]{:S(2)}) collective-permute-start(bf16[1,40,7296]{2,1,0:T(8,128)(2,1)S(1)} %get-tuple-element.49), channel_id=1, source_target_pairs={{0,2},{1,3},{2,0},{3,1},{4,6},{5,7},{6,4},{7,5},{8,10},{9,11},{10,... | collective-permute-start | bytes 1751048 | tf_op jit(solution)/shard_map/ppermute | solution.py:322
  107.9 18.9 %collective-permute-start.12 = (bf16[1,40,7168]{2,1,0:T(8,128)(2,1)S(1)}, bf16[1,40,7168]{2,1,0:T(8,128)(2,1)S(1)}, u32[]{:S(2)}, u32[]{:S(2)}) collective-permute-start(bf16[1,40,7168]{2,1,0:T(8,128)(2,1)S(1)} %get-tuple-element.52.refs_0_), channel_id=1, source_target_pairs={{0,2},{1,3},{2,0},{3,1},{4,6},{5,7},{6,4},{7,5},{8,10},{9,11},{10,... | collective-permute-start | bytes 1720328 | tf_op jit(solution)/shard_map/ppermute | solution.py:322
  109.5 34.4 %copy-start.6 = (bf16[64,7168]{1,0:T(8,128)(2,1)S(1)}, bf16[64,7168]{1,0:T(8,128)(2,1)}, u32[]{:S(2)}) copy-start(bf16[64,7168]{1,0:T(8,128)(2,1)} %copy-done.5) | copy-start | bytes 2752516
  126.8 10.2 %collective-permute-start.13 = (bf16[1,40,7168]{2,1,0:T(8,128)(2,1)S(1)}, bf16[1,40,7168]{2,1,0:T(8,128)(2,1)S(1)}, u32[]{:S(2)}, u32[]{:S(2)}) collective-permute-start(bf16[1,40,7168]{2,1,0:T(8,128)(2,1)S(1)} %get-tuple-element.53), channel_id=1, source_target_pairs={{0,2},{1,3},{2,0},{3,1},{4,6},{5,7},{6,4},{7,5},{8,10},{9,11},{10,... | collective-permute-start | bytes 1720328 | tf_op jit(solution)/shard_map/ppermute | solution.py:322
  138.2 18.9 %collective-permute-start.19 = (bf16[64,7168]{1,0:T(8,128)(2,1)S(1)}, bf16[64,7168]{1,0:T(8,128)(2,1)S(1)}, u32[]{:S(2)}, u32[]{:S(2)}) collective-permute-start(bf16[64,7168]{1,0:T(8,128)(2,1)S(1)} %combine.4.refs_0_), channel_id=1, source_target_pairs={{8,4},{9,5},{10,6},{11,7},{12,8},{13,9},{14,10},{15,11},{24,20},{2... | collective-permute-start | bytes 2752520 | tf_op jit(solution)/shard_map/ppermute | solution.py:322
  138.9 24.2 %collective-permute-start.17 = (bf16[64,7168]{1,0:T(8,128)(2,1)S(1)}, bf16[64,7168]{1,0:T(8,128)(2,1)S(1)}, u32[]{:S(2)}, u32[]{:S(2)}) collective-permute-start(bf16[64,7168]{1,0:T(8,128)(2,1)S(1)} %combine.4.refs_0_), channel_id=1, source_target_pairs={{0,4},{1,5},{2,6},{3,7},{4,8},{5,9},{6,10},{7,11},{16,20},{17,21},... | collective-permute-start | bytes 2752520 | tf_op jit(solution)/shard_map/ppermute | solution.py:322
  142.4 9.8 %collective-permute-start.14 = (bf16[1,40,7168]{2,1,0:T(8,128)(2,1)S(1)}, bf16[1,40,7168]{2,1,0:T(8,128)(2,1)S(1)}, u32[]{:S(2)}, u32[]{:S(2)}) collective-permute-start(bf16[1,40,7168]{2,1,0:T(8,128)(2,1)S(1)} %get-tuple-element.54), channel_id=1, source_target_pairs={{0,2},{1,3},{2,0},{3,1},{4,6},{5,7},{6,4},{7,5},{8,10},{9,11},{10,... | collective-permute-start | bytes 1720328 | tf_op jit(solution)/shard_map/ppermute | solution.py:322
  143.9 52.5 %copy-start.3 = (bf16[64,7168]{1,0:T(8,128)(2,1)S(1)}, bf16[64,7168]{1,0:T(8,128)(2,1)}, u32[]{:S(2)}) copy-start(bf16[64,7168]{1,0:T(8,128)(2,1)} %copy-done.2) | copy-start | bytes 2752516
  153.3 39.3 %collective-permute-start.16 = (bf16[64,7168]{1,0:T(8,128)(2,1)S(1)}, bf16[64,7168]{1,0:T(8,128)(2,1)S(1)}, u32[]{:S(2)}, u32[]{:S(2)}) collective-permute-start(bf16[64,7168]{1,0:T(8,128)(2,1)S(1)} %combine.5.second_ref), channel_id=1, source_target_pairs={{0,12},{1,13},{2,14},{3,15},{12,0},{13,1},{14,2},{15,3},{16,28},{1... | collective-permute-start | bytes 2752520 | tf_op jit(solution)/shard_map/ppermute | solution.py:327
  157.9 35.8 %collective-permute-start.20 = (bf16[64,7168]{1,0:T(8,128)(2,1)S(1)}, bf16[64,7168]{1,0:T(8,128)(2,1)S(1)}, u32[]{:S(2)}, u32[]{:S(2)}) collective-permute-start(bf16[64,7168]{1,0:T(8,128)(2,1)S(1)} %merge.3), channel_id=1, source_target_pairs={{4,0},{5,1},{6,2},{7,3},{8,4},{9,5},{10,6},{11,7},{12,8},{13,9},{1... | collective-permute-start | bytes 2752520 | tf_op jit(solution)/shard_map/ppermute | solution.py:322
  163.9 32.5 %collective-permute-start.18 = (bf16[64,7168]{1,0:T(8,128)(2,1)S(1)}, bf16[64,7168]{1,0:T(8,128)(2,1)S(1)}, u32[]{:S(2)}, u32[]{:S(2)}) collective-permute-start(bf16[64,7168]{1,0:T(8,128)(2,1)S(1)} %merge.2), channel_id=1, source_target_pairs={{0,4},{1,5},{2,6},{3,7},{4,8},{5,9},{6,10},{7,11},{8,12},{9,13},{1... | collective-permute-start | bytes 2752520 | tf_op jit(solution)/shard_map/ppermute | solution.py:322
  182.9 9.8 %collective-permute-start.15 = (bf16[1,40,7168]{2,1,0:T(8,128)(2,1)S(1)}, bf16[1,40,7168]{2,1,0:T(8,128)(2,1)S(1)}, u32[]{:S(2)}, u32[]{:S(2)}) collective-permute-start(bf16[1,40,7168]{2,1,0:T(8,128)(2,1)S(1)} %get-tuple-element.55), channel_id=1, source_target_pairs={{0,2},{1,3},{2,0},{3,1},{4,6},{5,7},{6,4},{7,5},{8,10},{9,11},{10,... | collective-permute-start | bytes 1720328 | tf_op jit(solution)/shard_map/ppermute | solution.py:322

commit v5 on v4

--- a/solution.py
+++ b/solution.py
@@ -64,7 +64,7 @@
     return jnp.dot(onehot, rows, preferred_element_type=F32).astype(BF16)
 
 
-def prepare_kernel(experts, capacity, at_ref, tokens_ref, routes_ref, gates_ref, x_ref, y_ref):
+def prepare_kernel(experts, tokens_ref, routes_ref, gates_ref, x_ref):
     rows, features = tokens_ref.shape
     sub = lax.broadcasted_iota(jnp.int32, (LANES, rows), 0)
     value = jnp.zeros((LANES, rows), F32)
@@ -78,9 +78,7 @@
     middle = (value - high).astype(BF16).astype(F32)
     low = value - high - middle
     ext = jnp.where(lane < experts, high, jnp.where(lane < 2 * experts, middle, low)).astype(BF16)
-    onehot = picker(gate_of(ext, at_ref[1], experts), capacity)
     x_ref[:, features:] = ext
-    y_ref[:, features:] = pick_rows(onehot, ext)
     step = 4 * BLOCK
 
     def body(i, carry):
@@ -92,28 +90,22 @@
             largest = jnp.max(jnp.abs(block), axis=1, keepdims=True)
             scale = ((largest + 1e-06) / 448.0).astype(BF16).astype(F32)
             parts.append((to_grid(block / scale) * scale).astype(BF16))
-        restored = jnp.concatenate(parts, axis=1)
-        x_ref[:, pl.ds(start, step)] = restored
-        y_ref[:, pl.ds(start, step)] = pick_rows(onehot, restored)
+        x_ref[:, pl.ds(start, step)] = jnp.concatenate(parts, axis=1)
         return carry
 
     lax.fori_loop(0, features // step, body, 0, unroll=2)
 
 
-def prepare(at, tokens, routes, gates, experts, capacity):
+def prepare(tokens, routes, gates, experts):
     rows, features = tokens.shape
-    width = features + LANES
-    return pl.pallas_call(
-        functools.partial(prepare_kernel, experts, capacity),
-        out_shape=(
-            jax.ShapeDtypeStruct((rows, width), BF16),
-            jax.ShapeDtypeStruct((capacity, width), BF16),
-        ),
-        in_specs=[SMEM] + [VMEM] * 3,
-        out_specs=(VMEM,) * 2,
+    return pl.pallas_call(
+        functools.partial(prepare_kernel, experts),
+        out_shape=jax.ShapeDtypeStruct((rows, features + LANES), BF16),
+        in_specs=[VMEM] * 3,
+        out_specs=VMEM,
         compiler_params=params(12),
         name="prepare",
-    )(at, tokens, routes.T, gates.T)
+    )(tokens, routes.T, gates.T)
 
 
 def compact_kernel(experts, capacity, choice, at_ref, first_ref, second_ref, *refs):
@@ -250,10 +242,102 @@
             pltpu.VMEM((total, 2 * half), BF16),
             pltpu.VMEM((total, LANES), F32),
         ],
-        compiler_params=params(34, 1),
+        compiler_params=params(46, 1),
         cost_estimate=pl.CostEstimate(flops=COST, bytes_accessed=COST, transcendentals=0),
         name="expert",
     )(at, *inputs, *inputs, own[0], other[0], own[1], other[1], own[2], other[2], *behind)
+
+
+def expert_up_kernel(experts, k_steps, at_ref, whole_ref, some_ref, *refs):
+    whole_ext, some_ext, gate_own, gate_other, up_own, up_other = refs[:6]
+    hidden_ref, weight_ref, acc = refs[-3:]
+    i = pl.program_id(0)
+    half = gate_own.shape[2]
+
+    @pl.when(i == 0)
+    def _():
+        acc[...] = jnp.zeros_like(acc)
+        gates = [gate_of(ext, at_ref[0], experts) for ext in (whole_ext[...], some_ext[0])]
+        weight_ref[...] = jnp.broadcast_to(jnp.concatenate(gates, axis=0), weight_ref.shape)
+
+    x = jnp.concatenate([whole_ref[...].astype(F32), some_ref[0].astype(F32)], axis=0)
+    x = x.astype(BF16)
+    for n, ref in enumerate((gate_own, gate_other, up_own, up_other)):
+        acc[:, n * half : (n + 1) * half] += jnp.dot(x, ref[0], preferred_element_type=F32)
+
+    @pl.when(i == k_steps - 1)
+    def _():
+        hidden_ref[...] = (jax.nn.silu(acc[:, : 2 * half]) * acc[:, 2 * half :]).astype(BF16)
+
+
+def expert_up(at, whole, some, weights, experts, tile=1792):
+    own, other = weights
+    features, half = own[0].shape[1:]
+    rows, capacity = whole.shape[0], some.shape[1]
+    total = rows + capacity
+    last = features // LANES
+    up_spec = pl.BlockSpec((1, tile, half), lambda i: (0, i, 0))
+    return pl.pallas_call(
+        functools.partial(expert_up_kernel, experts, features // tile),
+        out_shape=(
+            jax.ShapeDtypeStruct((total, 2 * half), BF16),
+            jax.ShapeDtypeStruct((total, LANES), F32),
+        ),
+        grid=(features // tile,),
+        in_specs=[
+            SMEM,
+            pl.BlockSpec((rows, tile), lambda i: (0, i)),
+            pl.BlockSpec((1, capacity, tile), lambda i: (0, 0, i)),
+            pl.BlockSpec((rows, LANES), lambda i: (0, last)),
+            pl.BlockSpec((1, capacity, LANES), lambda i: (0, 0, last)),
+        ]
+        + [up_spec] * 4,
+        out_specs=(
+            pl.BlockSpec((total, 2 * half), lambda i: (0, 0)),
+            pl.BlockSpec((total, LANES), lambda i: (0, 0)),
+        ),
+        scratch_shapes=[pltpu.VMEM((total, 4 * half), F32)],
+        compiler_params=params(46, 1),
+        cost_estimate=pl.CostEstimate(flops=COST, bytes_accessed=COST, transcendentals=0),
+        name="expert_up",
+    )(at, whole, some, whole, some, own[0], other[0], own[1], other[1])
+
+
+def expert_down_kernel(hidden_ref, weight_ref, down_own, down_other, *refs):
+    whole_out, some_out = refs[-2:]
+    half = down_own.shape[1]
+    rows = whole_out.shape[0]
+    own = jnp.dot(hidden_ref[:, :half], down_own[0], preferred_element_type=F32)
+    other = jnp.dot(hidden_ref[:, half:], down_other[0], preferred_element_type=F32)
+    total = own.astype(BF16).astype(F32) + other.astype(BF16).astype(F32)
+    scaled = total.astype(BF16).astype(F32) * weight_ref[:, :1]
+    whole_out[...] = scaled[:rows].astype(BF16)
+    some_out[0] = scaled[rows:].astype(BF16)
+
+
+def expert_down(hidden, weight, rows, weights, behind=(), tile=1792):
+    own, other = weights
+    half, features = own[2].shape[1:]
+    capacity = hidden.shape[0] - rows
+    down_spec = pl.BlockSpec((1, half, tile), lambda i: (0, 0, i))
+    return pl.pallas_call(
+        expert_down_kernel,
+        out_shape=(
+            jax.ShapeDtypeStruct((rows, features), BF16),
+            jax.ShapeDtypeStruct((1, capacity, features), BF16),
+        ),
+        grid=(features // tile,),
+        in_specs=[pl.BlockSpec(a.shape, lambda i: (0, 0)) for a in (hidden, weight)]
+        + [down_spec] * 2
+        + [ANY] * len(behind),
+        out_specs=(
+            pl.BlockSpec((rows, tile), lambda i: (0, i)),
+            pl.BlockSpec((1, capacity, tile), lambda i: (0, 0, i)),
+        ),
+        compiler_params=params(46, 1),
+        cost_estimate=pl.CostEstimate(flops=COST, bytes_accessed=COST, transcendentals=0),
+        name="expert_down",
+    )(hidden, weight, own[2], other[2], *behind)
 
 
 def combine_kernel(experts, capacity, index, adds, at_ref, block_ref, mine_ref, theirs_ref, *refs):
@@ -340,11 +424,12 @@
     place = chip // 2
     end = (place == 0) | (place == DEPTH - 1)
     at = jnp.stack([chip, chip ^ 1, place == 0, place < DEPTH // 2, end]).astype(jnp.int32)
-    block, picked = prepare(at, tokens, routes, gates, experts, capacity)
+    block = prepare(tokens, routes, gates, experts)
     other = tuple(send(w, dc=1) for w in (w_gate, w_up, w_down))
     from_left = send(block, dz=1)
     from_right = send(block, dz=-1)
 
+    picked, _ = compact(at, END, block, block, experts, capacity)
     first = (from_left, from_right, picked) + other
     from_left, from_right, picked, *other = lax.optimization_barrier(first)
     weights = ((w_gate, w_up, w_down), other)
@@ -352,7 +437,7 @@
     mid_right = send(from_right, dz=-1)
     near_picked, near = compact(at, FIRST, from_right, from_left, experts, capacity)
     near_picked = send(near_picked, dy=1)
-    picked = send(picked[None], dy=1)
+    picked = send(picked, dy=1)
     block_out, near_out = run_expert(at, (block, near), (), weights, experts)
 
     far = send_far(after(block, mid_left, mid_right, block_out, near_picked))
@@ -365,19 +450,21 @@
     last_picked, last = compact(
         at, END, far, from_right, experts, capacity, behind=(near_back, mid_picked)
     )
+    (mid_back,) = run_expert(at, (), (mid_picked,), weights, experts, behind=(last_picked,))
     last_picked = send(last_picked, dy=1)
-    last_out, mid_back, last_back = run_expert(
-        at, (last,), (mid_picked, last_picked), weights, experts
-    )
-    near_back = send(after(near_back, last_picked), dy=1)
-    mid_back = send(after(mid_back, near_back), dy=1)
-    last_back = send(after(last_back, mid_back), dy=1)
-    back = send(after(back, last_back), dy=1)
-
-    near_sum = combine(at, near, near_out, near_back, 0, (), experts)
-    mid_sum = combine(at, mid, mid_out, mid_back, 0, (), experts)
+    mid_back = send(after(mid_back, last_picked), dy=1)
+    hidden, weight = expert_up(at, last, last_picked, weights, experts)
+    mid_sum = combine(at, mid, mid_out, mid_back, 0, (), experts, behind=(hidden,))
     to_right = send(mid_sum, dz=1, only=(0, 1))
     to_left = send(mid_sum, dz=-1, only=(3, 2))
+    last_out, last_back = expert_down(
+        hidden, weight, last.shape[0], weights, behind=(mid_sum,)
+    )
+    near_back = send(after(near_back, mid_back, hidden), dy=1)
+    last_back = send(after(last_back, near_back), dy=1)
+    back = send(after(back, last_back, to_right, to_left), dy=1)
+
+    near_sum = combine(at, near, near_out, near_back, 0, (), experts)
     last_sum = combine(at, last, last_out, last_back, 0, (), experts, behind=(mid_sum,))
     far_home = send_far(last_sum)
     home_left = send(merge(at, FIRST, near_sum, last_sum, to_right), dz=1)

time: 200 us -> 195 us (0.975)
  Pallas kernels: 69.1 us -> 89.5 us
  starting transfers between devices: 54.8 us -> 42.4 us
  waiting for transfers between devices: 69 us -> 60.1 us
  local copies, waits for them, and re-layouts: 5.73 us -> 2.63 us
    ppermute x19, waiting for transfers between devices: 68.9 us -> 40.9 us  [send(): return lax.ppermute(array, 'ep', pairs)]
    ppermute x2, waiting for transfers between devices: 0.07 us -> 19.2 us  [send_far(): return lax.ppermute(array, 'ep', pairs)]
    ppermute x19, starting transfers between devices: 47.7 us -> 30.9 us  [send(): return lax.ppermute(array, 'ep', pairs)]
    pallas_call x1 -> x3, Pallas kernels: 5.63 us -> 21.4 us  [the longest x1 11.6 us: expert_up(): pl.pallas_call(functools.partial(expert_up_kernel, experts, features // t...]
    ppermute x2, starting transfers between devices: 7.12 us -> 11.5 us  [send_far(): return lax.ppermute(array, 'ep', pairs)]
    pallas_call x3, Pallas kernels: 51.7 us -> 55.7 us  [run_expert(): pl.pallas_call(functools.partial(expert_kernel, experts, tuple((a.shape[0...]
    unnamed x18 -> x6, local copies, waits for them, and re-layouts: 5.65 us -> 2.54 us
    pallas_call x3 -> x4, Pallas kernels: 4.45 us -> 5.19 us  [compact(): pl.pallas_call(functools.partial(compact_kernel, experts, capacity, choic...]
  transfers between devices with their start and end apart: 21 -> 21, of which waited for: 11 -> 10; matrix products, arithmetic and copies ran while one was open for 0% -> 0% of each run, Pallas kernels for 32% -> 44%
where the time goes in v5:
time: 195 us
  Pallas kernels  89.5 us (46%)
  waiting for transfers between devices  60.1 us (31%)
  starting transfers between devices  42.4 us (22%)
  local copies, waits for them, and re-layouts  2.63 us (1%)
    pallas_call x3, Pallas kernels, run_expert(): pl.pallas_call(functools.partial(expert_kernel, experts, tuple((a.shape[0...  55.7 us
    ppermute x19, waiting for transfers between devices, send(): return lax.ppermute(array, 'ep', pairs)  40.9 us
    ppermute x19, starting transfers between devices, send(): return lax.ppermute(array, 'ep', pairs)  30.9 us
    ppermute x2, waiting for transfers between devices, send_far(): return lax.ppermute(array, 'ep', pairs)  19.2 us
    pallas_call x1, Pallas kernels, expert_up(): pl.pallas_call(functools.partial(expert_up_kernel, experts, features // t...  11.6 us
    ppermute x2, starting transfers between devices, send_far(): return lax.ppermute(array, 'ep', pairs)  11.5 us
    pallas_call x1, Pallas kernels, expert_down(): pl.pallas_call(expert_down_kernel, out_shape=(jax.ShapeDtypeStruct((rows,...  6.95 us
    pallas_call x4, Pallas kernels, combine(): pl.pallas_call(functools.partial(combine_kernel, experts, capacity, index...  5.78 us
  transfers between devices with their start and end apart: 21, of which 10 were waited for; matrix products, arithmetic and copies ran while one was open for 0% of the time, Pallas kernels for 44%

profile of v5, /device:TPU:0, one launch (start us, length us, event | category | flops | bytes accessed | tf_op | source)
XLA Modules:
  0.0 194.9 jit_solution(3782621319575309695)
XLA Ops:
  0.0 0.5 collective-permute-start.2
  0.5 0.1 collective-permute-start.3
  0.5 0.5 collective-permute-start.4
  1.0 0.0 copy-start
  1.0 1.2 copy-done
  2.1 0.0 copy-start.1
  2.1 0.7 copy-done.1
  2.8 0.7 copy-done.2
  3.5 2.9 %prepare.1.first_ref.second_ref.refs_0_.refs_2_.block_ref = bf16[64,7296]{1,0:T(8,128)(2,1)S(1)} custom-call(bf16[64,7168]{1,0:T(8,128)(2,1)S(1)} %copy-done, s32[4,64]{1,0:T(4,128)S(1)} %bitcast.7, f32[4,64]{1,0:T(4,128)S(1)} %bitcast.8), custom_call_target="tpu_custom_call" | custom-call | tf_op jit(solution)/shard_map/prepare/pallas_call | solution.py:101
  6.4 1.3 collective-permute-start.1
  7.7 5.2 %collective-permute-start = (bf16[64,7296]{1,0:T(8,128)(2,1)S(1)}, bf16[64,7296]{1,0:T(8,128)(2,1)S(1)}, u32[]{:S(2)}, u32[]{:S(2)}) collective-permute-start(bf16[64,7296]{1,0:T(8,128)(2,1)S(1)} %prepare.1.first_ref.second_ref.refs_0_.refs_2_.block_ref), channel_id=1, source_target_pairs={{0,4},{1,5},{2,6},{3,7},{4,8},{5,9},{6,10},{7,11},{8,12},{9,13},{1... | collective-permute-start | bytes 2801672 | tf_op jit(solution)/shard_map/ppermute | solution.py:406
  12.9 0.1 stack.35.at_ref
  13.0 1.6 compact.4
  14.5 17.7 %collective-permute-done.1.first_ref.second_ref = bf16[64,7296]{1,0:T(8,128)(2,1)S(1)} collective-permute-done((bf16[64,7296]{1,0:T(8,128)(2,1)S(1)}, bf16[64,7296]{1,0:T(8,128)(2,1)S(1)}, u32[]{:S(2)}, u32[]{:S(2)}) %collective-permute-start.1) | collective-permute-done | bytes 933920 | tf_op jit(solution)/shard_map/ppermute | solution.py:406
  32.2 1.2 collective-permute-done.second_ref
  33.4 0.0 collective-permute-done.2.refs_5_.refs_7_.refs_3_
  33.4 0.0 collective-permute-done.3.refs_7_.refs_9_.refs_5_
  33.4 0.0 collective-permute-done.4.refs_9_.refs_11_.refs_7_.down_other
  33.4 4.6 %collective-permute-start.6 = (bf16[64,7296]{1,0:T(8,128)(2,1)S(1)}, bf16[64,7296]{1,0:T(8,128)(2,1)S(1)}, u32[]{:S(2)}, u32[]{:S(2)}) collective-permute-start(bf16[64,7296]{1,0:T(8,128)(2,1)S(1)} %collective-permute-done.second_ref), channel_id=1, source_target_pairs={{0,4},{1,5},{2,6},{3,7},{4,8},{5,9},{6,10},{7,11},{8,12},{9,13},{1... | collective-permute-start | bytes 2801672 | tf_op jit(solution)/shard_map/ppermute | solution.py:406
  38.0 1.3 collective-permute-start.5
  39.3 1.2 compact.5
  40.5 1.6 collective-permute-start.8
  42.1 0.5 collective-permute-start.7
  42.6 18.3 %expert.3 = (bf16[64,7168]{1,0:T(8,128)(2,1)S(1)}, bf16[64,7168]{1,0:T(8,128)(2,1)S(1)}) custom-call(s32[5]{0:T(128)S(1)} %stack.35.at_ref, bf16[64,7296]{1,0:T(8,128)(2,1)S(1)} %prepare.1.first_ref.second_ref.refs_0_.refs_2_.block_ref, bf16[64,7296]{1,0:T(8,128)(2,1)S(1)} %get-tuple-element.35.refs_1_.refs_3_.block_ref, ...), custom_call_target="tpu_custom_call" | custom-call | flops 1024 | bytes 1024 | tf_op jit(solution)/shard_map/expert/pallas_call | solution.py:227
  60.8 0.0 collective-permute-done.8.refs_2_.refs_5_
  60.9 0.0 collective-permute-done.6.second_ref
  60.9 1.5 collective-permute-done.5.first_ref
  62.3 5.2 %collective-permute-start.9 = (bf16[64,7296]{1,0:T(8,128)(2,1)S(1)}, bf16[64,7296]{1,0:T(8,128)(2,1)S(1)}, u32[]{:S(2)}, u32[]{:S(2)}) collective-permute-start(bf16[64,7296]{1,0:T(8,128)(2,1)S(1)} %prepare.1.first_ref.second_ref.refs_0_.refs_2_.block_ref), channel_id=1, source_target_pairs={{0,12},{1,13},{2,14},{3,15},{12,0},{13,1},{14,2},{15,3},{16,28},{1... | collective-permute-start | bytes 2801672 | tf_op jit(solution)/shard_map/ppermute | solution.py:411
  67.6 0.5 collective-permute-done.7.refs_0_.refs_1_.refs_4_
  68.0 1.2 compact.6
  69.2 1.6 collective-permute-start.10
  70.8 18.8 %expert.4 = (bf16[64,7168]{1,0:T(8,128)(2,1)S(1)}, bf16[1,40,7168]{2,1,0:T(8,128)(2,1)S(1)}, bf16[1,40,7168]{2,1,0:T(8,128)(2,1)S(1)}) custom-call(s32[5]{0:T(128)S(1)} %stack.35.at_ref, bf16[64,7296]{1,0:T(8,128)(2,1)S(1)} %get-tuple-element.41.refs_0_.refs_3_.block_ref, bf16[1,40,7296]{2,1,0:T(8,128)(2,1)S(1)} %collective-permute-done.7.refs_0_.refs_1_.refs_4_, ...), custom_call_target="tpu_custom_call" | custom-call | flops 1024 | bytes 1024 | tf_op jit(solution)/shard_map/expert/pallas_call | solution.py:227
  89.6 0.0 collective-permute-done.10.refs_1_.refs_0_
  89.6 0.0 collective-permute-done.9.first_ref
  89.7 1.2 compact.7
  90.9 0.6 collective-permute-start.11
  91.5 18.6 %expert.5 = bf16[1,40,7168]{2,1,0:T(8,128)(2,1)S(1)} custom-call(s32[5]{0:T(128)S(1)} %stack.35.at_ref, bf16[1,40,7296]{2,1,0:T(8,128)(2,1)S(1)} %collective-permute-done.10.refs_1_.refs_0_, bf16[1,40,7296]{2,1,0:T(8,128)(2,1)S(1)} %collective-permute-done.10.refs_1_.refs_0_, bf16[1,7168,512]{2,1,0:T(8,128)(2,1)} %refs_2_.3, ...), custom_call_target="tpu_custom_call" | custom-call | flops 1024 | bytes 1024 | tf_op jit(solution)/shard_map/expert/pallas_call | solution.py:227
  110.1 0.0 collective-permute-done.11.some_ref.refs_1_
  110.1 1.6 collective-permute-start.12
  111.7 11.6 %expert_up.1 = (bf16[104,1024]{1,0:T(8,128)(2,1)S(1)}, f32[104,128]{1,0:T(8,128)S(1)}) custom-call(s32[5]{0:T(128)S(1)} %stack.35.at_ref, bf16[64,7296]{1,0:T(8,128)(2,1)S(1)} %get-tuple-element.47.whole_ref.refs_0_.block_ref, bf16[1,40,7296]{2,1,0:T(8,128)(2,1)S(1)} %collective-permute-done.11.some_ref.refs_1_, ...), custom_call_target="tpu_custom_call" | custom-call | flops 1024 | bytes 1024 | tf_op jit(solution)/shard_map/expert_up/pallas_call | solution.py:280
  123.2 0.2 collective-permute-done.12.theirs_ref
  123.5 1.5 collective-permute-start.13
  125.0 1.1 combine.4.refs_0_
  126.1 0.7 collective-permute-start.16
  126.8 4.9 %collective-permute-start.15 = (bf16[64,7168]{1,0:T(8,128)(2,1)S(1)}, bf16[64,7168]{1,0:T(8,128)(2,1)S(1)}, u32[]{:S(2)}, u32[]{:S(2)}) collective-permute-start(bf16[64,7168]{1,0:T(8,128)(2,1)S(1)} %combine.4.refs_0_), channel_id=1, source_target_pairs={{0,4},{1,5},{2,6},{3,7},{4,8},{5,9},{6,10},{7,11},{16,20},{17,21},... | collective-permute-start | bytes 2752520 | tf_op jit(solution)/shard_map/ppermute | solution.py:406
  131.8 7.0 %expert_down.1 = (bf16[64,7168]{1,0:T(8,128)(2,1)S(1)}, bf16[1,40,7168]{2,1,0:T(8,128)(2,1)S(1)}) custom-call(bf16[104,1024]{1,0:T(8,128)(2,1)S(1)} %get-tuple-element.49.refs_0_.hidden_ref, f32[104,128]{1,0:T(8,128)S(1)} %get-tuple-element.50.weight_ref, bf16[1,512,7168]{2,1,0:T(8,128)(2,1)} %down_own.1, ...), custom_call_target="tpu_custom_call" | custom-call | flops 1024 | bytes 1024 | tf_op jit(solution)/shard_map/expert_down/pallas_call | solution.py:323
  138.7 0.0 collective-permute-done.13.theirs_ref
  138.7 0.6 collective-permute-start.14
  139.3 1.1 combine.6.first_ref.second_ref
  140.4 0.0 collective-permute-done.16.more_ref
  140.5 0.8 merge.3
  141.2 1.3 collective-permute-start.20
  142.5 7.5 %collective-permute-done.14.theirs_ref = bf16[1,40,7168]{2,1,0:T(8,128)(2,1)S(1)} collective-permute-done((bf16[1,40,7168]{2,1,0:T(8,128)(2,1)S(1)}, bf16[1,40,7168]{2,1,0:T(8,128)(2,1)S(1)}, u32[]{:S(2)}, u32[]{:S(2)}) %collective-permute-start.14) | collective-permute-done | bytes 573472 | tf_op jit(solution)/shard_map/ppermute | solution.py:406
  150.0 1.1 combine.5.second_ref
  151.1 6.3 %collective-permute-start.18 = (bf16[64,7168]{1,0:T(8,128)(2,1)S(1)}, bf16[64,7168]{1,0:T(8,128)(2,1)S(1)}, u32[]{:S(2)}, u32[]{:S(2)}) collective-permute-start(bf16[64,7168]{1,0:T(8,128)(2,1)S(1)} %combine.5.second_ref), channel_id=1, source_target_pairs={{0,12},{1,13},{2,14},{3,15},{12,0},{13,1},{14,2},{15,3},{16,28},{1... | collective-permute-start | bytes 2752520 | tf_op jit(solution)/shard_map/ppermute | solution.py:411
  157.4 0.0 collective-permute-done.15.more_ref
  157.4 0.8 merge.2
  158.2 1.3 collective-permute-start.19
  159.6 1.4 collective-permute-start.17
  161.0 9.2 %collective-permute-done.17.theirs_ref = bf16[1,40,7168]{2,1,0:T(8,128)(2,1)S(1)} collective-permute-done((bf16[1,40,7168]{2,1,0:T(8,128)(2,1)S(1)}, bf16[1,40,7168]{2,1,0:T(8,128)(2,1)S(1)}, u32[]{:S(2)}, u32[]{:S(2)}) %collective-permute-start.17) | collective-permute-done | bytes 573472 | tf_op jit(solution)/shard_map/ppermute | solution.py:406
  170.2 0.7 collective-permute-done.20.refs_2_
  170.8 19.2 %collective-permute-done.18.refs_0_ = bf16[64,7168]{1,0:T(8,128)(2,1)S(1)} collective-permute-done((bf16[64,7168]{1,0:T(8,128)(2,1)S(1)}, bf16[64,7168]{1,0:T(8,128)(2,1)S(1)}, u32[]{:S(2)}, u32[]{:S(2)}) %collective-permute-start.18) | collective-permute-done | bytes 917536 | tf_op jit(solution)/shard_map/ppermute | solution.py:411
  190.0 2.5 %collective-permute-done.19.refs_1_ = bf16[64,7168]{1,0:T(8,128)(2,1)S(1)} collective-permute-done((bf16[64,7168]{1,0:T(8,128)(2,1)S(1)}, bf16[64,7168]{1,0:T(8,128)(2,1)S(1)}, u32[]{:S(2)}, u32[]{:S(2)}) %collective-permute-start.19) | collective-permute-done | bytes 917536 | tf_op jit(solution)/shard_map/ppermute | solution.py:406
  192.5 2.4 %combine.7 = bf16[64,7168]{1,0:T(8,128)(2,1)} custom-call(s32[5]{0:T(128)S(1)} %stack.35.at_ref, bf16[64,7296]{1,0:T(8,128)(2,1)S(1)} %prepare.1.first_ref.second_ref.refs_0_.refs_2_.block_ref, bf16[64,7168]{1,0:T(8,128)(2,1)S(1)} %get-tuple-element.39.mine_ref, bf16[1,40,7168]{2,1,0:T(8,128)(2,1)S(1)} %collective-permute-done.17.theirs_ref, ...), custom_call_target="tpu_custom_call" | custom-call | tf_op jit(solution)/shard_map/combine/pallas_call | solution.py:362
  (1 shorter events, 0.0 us)
Async XLA Ops:
  0.0 33.4 %collective-permute-start.2 = (bf16[1,7168,512]{2,1,0:T(8,128)(2,1)}, bf16[1,7168,512]{2,1,0:T(8,128)(2,1)}, u32[]{:S(2)}, u32[]{:S(2)}) collective-permute-start(bf16[1,7168,512]{2,1,0:T(8,128)(2,1)} %refs_2_.3), channel_id=1, source_target_pairs={{0,1},{1,0},{2,3},{3,2},{4,5},{5,4},{6,7},{7,6},{8,9},{9,8},{10,11... | collective-permute-start | bytes 22020104 | tf_op jit(solution)/shard_map/ppermute | solution.py:406
  0.5 32.9 %collective-permute-start.3 = (bf16[1,7168,512]{2,1,0:T(8,128)(2,1)}, bf16[1,7168,512]{2,1,0:T(8,128)(2,1)}, u32[]{:S(2)}, u32[]{:S(2)}) collective-permute-start(bf16[1,7168,512]{2,1,0:T(8,128)(2,1)} %refs_4_.5), channel_id=1, source_target_pairs={{0,1},{1,0},{2,3},{3,2},{4,5},{5,4},{6,7},{7,6},{8,9},{9,8},{10,11... | collective-permute-start | bytes 22020104 | tf_op jit(solution)/shard_map/ppermute | solution.py:406
  0.5 32.9 %collective-permute-start.4 = (bf16[1,512,7168]{2,1,0:T(8,128)(2,1)}, bf16[1,512,7168]{2,1,0:T(8,128)(2,1)}, u32[]{:S(2)}, u32[]{:S(2)}) collective-permute-start(bf16[1,512,7168]{2,1,0:T(8,128)(2,1)} %down_own.1), channel_id=1, source_target_pairs={{0,1},{1,0},{2,3},{3,2},{4,5},{5,4},{6,7},{7,6},{8,9},{9,8},{10,11... | collective-permute-start | bytes 22020104 | tf_op jit(solution)/shard_map/ppermute | solution.py:406
  1.0 1.2 copy-start
  2.1 0.7 copy-start.1
  2.8 0.7 copy-start.2
  6.4 25.8 %collective-permute-start.1 = (bf16[64,7296]{1,0:T(8,128)(2,1)S(1)}, bf16[64,7296]{1,0:T(8,128)(2,1)S(1)}, u32[]{:S(2)}, u32[]{:S(2)}) collective-permute-start(bf16[64,7296]{1,0:T(8,128)(2,1)S(1)} %prepare.1.first_ref.second_ref.refs_0_.refs_2_.block_ref), channel_id=1, source_target_pairs={{4,0},{5,1},{6,2},{7,3},{8,4},{9,5},{10,6},{11,7},{12,8},{13,9},{1... | collective-permute-start | bytes 2801672 | tf_op jit(solution)/shard_map/ppermute | solution.py:406
  7.7 25.7 %collective-permute-start = (bf16[64,7296]{1,0:T(8,128)(2,1)S(1)}, bf16[64,7296]{1,0:T(8,128)(2,1)S(1)}, u32[]{:S(2)}, u32[]{:S(2)}) collective-permute-start(bf16[64,7296]{1,0:T(8,128)(2,1)S(1)} %prepare.1.first_ref.second_ref.refs_0_.refs_2_.block_ref), channel_id=1, source_target_pairs={{0,4},{1,5},{2,6},{3,7},{4,8},{5,9},{6,10},{7,11},{8,12},{9,13},{1... | collective-permute-start | bytes 2801672 | tf_op jit(solution)/shard_map/ppermute | solution.py:406
  33.4 27.5 %collective-permute-start.6 = (bf16[64,7296]{1,0:T(8,128)(2,1)S(1)}, bf16[64,7296]{1,0:T(8,128)(2,1)S(1)}, u32[]{:S(2)}, u32[]{:S(2)}) collective-permute-start(bf16[64,7296]{1,0:T(8,128)(2,1)S(1)} %collective-permute-done.second_ref), channel_id=1, source_target_pairs={{0,4},{1,5},{2,6},{3,7},{4,8},{5,9},{6,10},{7,11},{8,12},{9,13},{1... | collective-permute-start | bytes 2801672 | tf_op jit(solution)/shard_map/ppermute | solution.py:406
  38.0 24.4 %collective-permute-start.5 = (bf16[64,7296]{1,0:T(8,128)(2,1)S(1)}, bf16[64,7296]{1,0:T(8,128)(2,1)S(1)}, u32[]{:S(2)}, u32[]{:S(2)}) collective-permute-start(bf16[64,7296]{1,0:T(8,128)(2,1)S(1)} %collective-permute-done.1.first_ref.second_ref), channel_id=1, source_target_pairs={{4,0},{5,1},{6,2},{7,3},{8,4},{9,5},{10,6},{11,7},{12,8},{13,9},{1... | collective-permute-start | bytes 2801672 | tf_op jit(solution)/shard_map/ppermute | solution.py:406
  40.5 20.4 %collective-permute-start.8 = (bf16[1,40,7296]{2,1,0:T(8,128)(2,1)S(1)}, bf16[1,40,7296]{2,1,0:T(8,128)(2,1)S(1)}, u32[]{:S(2)}, u32[]{:S(2)}) collective-permute-start(bf16[1,40,7296]{2,1,0:T(8,128)(2,1)S(1)} %get-tuple-element.42), channel_id=1, source_target_pairs={{0,2},{1,3},{2,0},{3,1},{4,6},{5,7},{6,4},{7,5},{8,10},{9,11},{10,... | collective-permute-start | bytes 1751048 | tf_op jit(solution)/shard_map/ppermute | solution.py:406
  42.1 25.9 %collective-permute-start.7 = (bf16[1,40,7296]{2,1,0:T(8,128)(2,1)S(1)}, bf16[1,40,7296]{2,1,0:T(8,128)(2,1)S(1)}, u32[]{:S(2)}, u32[]{:S(2)}) collective-permute-start(bf16[1,40,7296]{2,1,0:T(8,128)(2,1)S(1)} %get-tuple-element.40), channel_id=1, source_target_pairs={{0,2},{1,3},{2,0},{3,1},{4,6},{5,7},{6,4},{7,5},{8,10},{9,11},{10,... | collective-permute-start | bytes 1751048 | tf_op jit(solution)/shard_map/ppermute | solution.py:406
  62.3 27.3 %collective-permute-start.9 = (bf16[64,7296]{1,0:T(8,128)(2,1)S(1)}, bf16[64,7296]{1,0:T(8,128)(2,1)S(1)}, u32[]{:S(2)}, u32[]{:S(2)}) collective-permute-start(bf16[64,7296]{1,0:T(8,128)(2,1)S(1)} %prepare.1.first_ref.second_ref.refs_0_.refs_2_.block_ref), channel_id=1, source_target_pairs={{0,12},{1,13},{2,14},{3,15},{12,0},{13,1},{14,2},{15,3},{16,28},{1... | collective-permute-start | bytes 2801672 | tf_op jit(solution)/shard_map/ppermute | solution.py:411
  69.2 20.4 %collective-permute-start.10 = (bf16[1,40,7296]{2,1,0:T(8,128)(2,1)S(1)}, bf16[1,40,7296]{2,1,0:T(8,128)(2,1)S(1)}, u32[]{:S(2)}, u32[]{:S(2)}) collective-permute-start(bf16[1,40,7296]{2,1,0:T(8,128)(2,1)S(1)} %get-tuple-element.46), channel_id=1, source_target_pairs={{0,2},{1,3},{2,0},{3,1},{4,6},{5,7},{6,4},{7,5},{8,10},{9,11},{10,... | collective-permute-start | bytes 1751048 | tf_op jit(solution)/shard_map/ppermute | solution.py:406
  90.9 19.2 %collective-permute-start.11 = (bf16[1,40,7296]{2,1,0:T(8,128)(2,1)S(1)}, bf16[1,40,7296]{2,1,0:T(8,128)(2,1)S(1)}, u32[]{:S(2)}, u32[]{:S(2)}) collective-permute-start(bf16[1,40,7296]{2,1,0:T(8,128)(2,1)S(1)} %get-tuple-element.48.refs_8_), channel_id=1, source_target_pairs={{0,2},{1,3},{2,0},{3,1},{4,6},{5,7},{6,4},{7,5},{8,10},{9,11},{10,... | collective-permute-start | bytes 1751048 | tf_op jit(solution)/shard_map/ppermute | solution.py:406
  110.1 13.4 %collective-permute-start.12 = (bf16[1,40,7168]{2,1,0:T(8,128)(2,1)S(1)}, bf16[1,40,7168]{2,1,0:T(8,128)(2,1)S(1)}, u32[]{:S(2)}, u32[]{:S(2)}) collective-permute-start(bf16[1,40,7168]{2,1,0:T(8,128)(2,1)S(1)} %expert.5), channel_id=1, source_target_pairs={{0,2},{1,3},{2,0},{3,1},{4,6},{5,7},{6,4},{7,5},{8,10},{9,11},{10,... | collective-permute-start | bytes 1720328 | tf_op jit(solution)/shard_map/ppermute | solution.py:406
  123.5 15.3 %collective-permute-start.13 = (bf16[1,40,7168]{2,1,0:T(8,128)(2,1)S(1)}, bf16[1,40,7168]{2,1,0:T(8,128)(2,1)S(1)}, u32[]{:S(2)}, u32[]{:S(2)}) collective-permute-start(bf16[1,40,7168]{2,1,0:T(8,128)(2,1)S(1)} %get-tuple-element.54.refs_0_), channel_id=1, source_target_pairs={{0,2},{1,3},{2,0},{3,1},{4,6},{5,7},{6,4},{7,5},{8,10},{9,11},{10,... | collective-permute-start | bytes 1720328 | tf_op jit(solution)/shard_map/ppermute | solution.py:406
  126.1 14.4 %collective-permute-start.16 = (bf16[64,7168]{1,0:T(8,128)(2,1)S(1)}, bf16[64,7168]{1,0:T(8,128)(2,1)S(1)}, u32[]{:S(2)}, u32[]{:S(2)}) collective-permute-start(bf16[64,7168]{1,0:T(8,128)(2,1)S(1)} %combine.4.refs_0_), channel_id=1, source_target_pairs={{8,4},{9,5},{10,6},{11,7},{12,8},{13,9},{14,10},{15,11},{24,20},{2... | collective-permute-start | bytes 2752520 | tf_op jit(solution)/shard_map/ppermute | solution.py:406
  126.8 30.6 %collective-permute-start.15 = (bf16[64,7168]{1,0:T(8,128)(2,1)S(1)}, bf16[64,7168]{1,0:T(8,128)(2,1)S(1)}, u32[]{:S(2)}, u32[]{:S(2)}) collective-permute-start(bf16[64,7168]{1,0:T(8,128)(2,1)S(1)} %combine.4.refs_0_), channel_id=1, source_target_pairs={{0,4},{1,5},{2,6},{3,7},{4,8},{5,9},{6,10},{7,11},{16,20},{17,21},... | collective-permute-start | bytes 2752520 | tf_op jit(solution)/shard_map/ppermute | solution.py:406
  138.7 11.3 %collective-permute-start.14 = (bf16[1,40,7168]{2,1,0:T(8,128)(2,1)S(1)}, bf16[1,40,7168]{2,1,0:T(8,128)(2,1)S(1)}, u32[]{:S(2)}, u32[]{:S(2)}) collective-permute-start(bf16[1,40,7168]{2,1,0:T(8,128)(2,1)S(1)} %get-tuple-element.55), channel_id=1, source_target_pairs={{0,2},{1,3},{2,0},{3,1},{4,6},{5,7},{6,4},{7,5},{8,10},{9,11},{10,... | collective-permute-start | bytes 1720328 | tf_op jit(solution)/shard_map/ppermute | solution.py:406
  141.2 29.6 %collective-permute-start.20 = (bf16[64,7168]{1,0:T(8,128)(2,1)S(1)}, bf16[64,7168]{1,0:T(8,128)(2,1)S(1)}, u32[]{:S(2)}, u32[]{:S(2)}) collective-permute-start(bf16[64,7168]{1,0:T(8,128)(2,1)S(1)} %merge.3), channel_id=1, source_target_pairs={{4,0},{5,1},{6,2},{7,3},{8,4},{9,5},{10,6},{11,7},{12,8},{13,9},{1... | collective-permute-start | bytes 2752520 | tf_op jit(solution)/shard_map/ppermute | solution.py:406
  151.1 38.9 %collective-permute-start.18 = (bf16[64,7168]{1,0:T(8,128)(2,1)S(1)}, bf16[64,7168]{1,0:T(8,128)(2,1)S(1)}, u32[]{:S(2)}, u32[]{:S(2)}) collective-permute-start(bf16[64,7168]{1,0:T(8,128)(2,1)S(1)} %combine.5.second_ref), channel_id=1, source_target_pairs={{0,12},{1,13},{2,14},{3,15},{12,0},{13,1},{14,2},{15,3},{16,28},{1... | collective-permute-start | bytes 2752520 | tf_op jit(solution)/shard_map/ppermute | solution.py:411
  158.2 34.3 %collective-permute-start.19 = (bf16[64,7168]{1,0:T(8,128)(2,1)S(1)}, bf16[64,7168]{1,0:T(8,128)(2,1)S(1)}, u32[]{:S(2)}, u32[]{:S(2)}) collective-permute-start(bf16[64,7168]{1,0:T(8,128)(2,1)S(1)} %merge.2), channel_id=1, source_target_pairs={{0,4},{1,5},{2,6},{3,7},{4,8},{5,9},{6,10},{7,11},{8,12},{9,13},{1... | collective-permute-start | bytes 2752520 | tf_op jit(solution)/shard_map/ppermute | solution.py:406
  159.6 10.6 %collective-permute-start.17 = (bf16[1,40,7168]{2,1,0:T(8,128)(2,1)S(1)}, bf16[1,40,7168]{2,1,0:T(8,128)(2,1)S(1)}, u32[]{:S(2)}, u32[]{:S(2)}) collective-permute-start(bf16[1,40,7168]{2,1,0:T(8,128)(2,1)S(1)} %get-tuple-element.56), channel_id=1, source_target_pairs={{0,2},{1,3},{2,0},{3,1},{4,6},{5,7},{6,4},{7,5},{8,10},{9,11},{10,... | collective-permute-start | bytes 1720328 | tf_op jit(solution)/shard_map/ppermute | solution.py:406
